TPU v7x, 32 devices: a whole 2x2x4 slice. The times are simulated.
32 devices in a mesh: wide: 8 (over z, y), narrow: 4 (over x, core).
Axes of the slice: x: 2, y: 2, z: 4, core: 2. Of those that a mesh axis runs over, the one named last changes fastest.
Arguments:
- tokens: bfloat16 [16, 512, 768], P('wide', 'narrow'), may hold values from -6 to 6
- query_weight: bfloat16 [2, 768, 768], P(None, ('wide', 'narrow')), may hold values from -0.21875 to 0.21875
- key_weight: bfloat16 [2, 768, 768], P(None, ('wide', 'narrow')), may hold values from -0.21875 to 0.21875
- value_weight: bfloat16 [2, 768, 768], P(None, ('wide', 'narrow')), may hold values from -0.21875 to 0.21875
- out_weight: bfloat16 [2, 768, 768], P(None, ('wide', 'narrow')), may hold values from -0.875 to 0.875
- up_weight: bfloat16 [2, 768, 3072], P(None, ('wide', 'narrow')), may hold values from -0.21875 to 0.21875
- down_weight: bfloat16 [2, 3072, 768], P(None, ('wide', 'narrow')), may hold values from -0.109375 to 0.109375
- query_bias: bfloat16 [2, 768], P(None, ('wide', 'narrow')), may hold values from -1.796875 to 1.796875
- value_bias: bfloat16 [2, 768], P(None, ('wide', 'narrow')), may hold values from -1.796875 to 1.796875
- out_bias: bfloat16 [2, 768], P(None, ('wide', 'narrow')), may hold values from -1.796875 to 1.796875
- up_bias: bfloat16 [2, 3072], P(None, ('wide', 'narrow')), may hold values from -1.796875 to 1.796875
- down_bias: bfloat16 [2, 768], P(None, ('wide', 'narrow')), may hold values from -1.796875 to 1.796875
- first_gain: bfloat16 [2, 768], P(None, ('wide', 'narrow')), may hold values from 0.5 to 1.5
- first_shift: bfloat16 [2, 768], P(None, ('wide', 'narrow')), may hold values from -1.1953125 to 1.1953125
- second_gain: bfloat16 [2, 768], P(None, ('wide', 'narrow')), may hold values from 0.5 to 1.5
- second_shift: bfloat16 [2, 768], P(None, ('wide', 'narrow')), may hold values from -1.1953125 to 1.1953125
- lengths: int32 [16], P('wide'), may hold values from 1 to 512, as said below
- cotangent: bfloat16 [16, 512, 768], P('wide', 'narrow'), may hold values from -6 to 6
Outputs:
- output: bfloat16 [16, 512, 768], P('wide', 'narrow')
- tokens_grad: bfloat16 [16, 512, 768], P('wide', 'narrow')
- query_weight_grad: float32 [2, 768, 768], P(None, ('wide', 'narrow'))
- key_weight_grad: float32 [2, 768, 768], P(None, ('wide', 'narrow'))
- value_weight_grad: float32 [2, 768, 768], P(None, ('wide', 'narrow'))
- out_weight_grad: float32 [2, 768, 768], P(None, ('wide', 'narrow'))
- up_weight_grad: float32 [2, 768, 3072], P(None, ('wide', 'narrow'))
- down_weight_grad: float32 [2, 3072, 768], P(None, ('wide', 'narrow'))
- query_bias_grad: float32 [2, 768], P(None, ('wide', 'narrow'))
- value_bias_grad: float32 [2, 768], P(None, ('wide', 'narrow'))
- out_bias_grad: float32 [2, 768], P(None, ('wide', 'narrow'))
- up_bias_grad: float32 [2, 3072], P(None, ('wide', 'narrow'))
- down_bias_grad: float32 [2, 768], P(None, ('wide', 'narrow'))
- first_gain_grad: float32 [2, 768], P(None, ('wide', 'narrow'))
- first_shift_grad: float32 [2, 768], P(None, ('wide', 'narrow'))
- second_gain_grad: float32 [2, 768], P(None, ('wide', 'narrow'))
- second_shift_grad: float32 [2, 768], P(None, ('wide', 'narrow'))
Inputs may be any that keep to these rules, and one draw needn't show every extreme that they name: `lengths`: in each aligned block of 2 pairs at least one pair has length 512; the others are heavy-tailed.
All inputs are finite; a program needn't handle non-finite values.
Results may differ from a plain program's by a relative error of at most 0.024.
Values may be sent and summed in bfloat16 or wider, within the bound.
No kernel may reach another device: no remote copies, remote signals or barrier semaphores. Data moves between devices by JAX's collectives and lax.ppermute only.
A program may use at most 192 MiB of HBM per device.

v0:
```python
import jax
import jax.numpy as jnp
from jax import lax
from jax.sharding import PartitionSpec as P

D = 768
HEADS = 12
HD = 64
LAYERS = 2
MICRO = 2


def layer_norm(values, gain, offset):
    average = jnp.mean(values, axis=-1, keepdims=True)
    centred = values - average
    variance = jnp.mean(centred * centred, axis=-1, keepdims=True)
    return centred * lax.rsqrt(variance + 1e-05) * gain + offset


def exact_gelu(values):
    return jax.nn.gelu(values, approximate=False)


def matmul(left, right):
    return jnp.dot(left, right, preferred_element_type=jnp.float32)


def matmul_left_t(left, right):
    return jnp.einsum("ra,rb->ab", left, right, preferred_element_type=jnp.float32)


def matmul_right_t(left, right):
    return jnp.einsum("ra,ba->rb", left, right, preferred_element_type=jnp.float32)


def column_sum(values):
    return jnp.sum(values.astype(jnp.float32), axis=0)


def split_features(values):
    count_wide = lax.axis_size("wide")
    count_narrow = lax.axis_size("narrow")
    rows, width = values.shape
    return values.reshape(rows, count_wide, count_narrow, width // (count_wide * count_narrow))


def own_features(vector):
    count_wide = lax.axis_size("wide")
    count_narrow = lax.axis_size("narrow")
    width = vector.shape[-1]
    share = width // (count_wide * count_narrow)
    shaped = vector.reshape(count_wide, count_narrow, share)
    picked = lax.dynamic_slice_in_dim(shaped, lax.axis_index("narrow"), 1, 1)
    return picked.reshape(count_wide * share)


def gather_forward(keys, values):
    return (
        lax.all_gather(keys, "narrow", axis=1, tiled=True),
        lax.all_gather(values, "narrow", axis=1, tiled=True),
    )


def gather_backward(keys, values):
    return (
        lax.all_gather(keys, "narrow", axis=1, tiled=True),
        lax.all_gather(values, "narrow", axis=1, tiled=True),
    )


def attention_inputs(hidden, params, lengths, gather_pair):
    pairs_now, rows_pair, width = hidden.shape
    rows = pairs_now * rows_pair
    flat = hidden.reshape(rows, width)
    inputs = flat.astype(jnp.bfloat16)
    queries = (matmul(inputs, params[0]) + params[6]).astype(jnp.bfloat16)
    keys = matmul(inputs, params[1]).astype(jnp.bfloat16)
    values = (matmul(inputs, params[2]) + params[7]).astype(jnp.bfloat16)
    keys_all, values_all = gather_pair(
        keys.reshape(pairs_now, rows_pair, width), values.reshape(pairs_now, rows_pair, width)
    )
    seq_len = keys_all.shape[1]
    heads_query = queries.reshape(pairs_now, rows_pair, HEADS, HD)
    heads_key = keys_all.reshape(pairs_now, seq_len, HEADS, HD)
    heads_value = values_all.reshape(pairs_now, seq_len, HEADS, HD)
    raw = jnp.einsum(
        "pqhd,pkhd->phqk", heads_query, heads_key, preferred_element_type=jnp.float32
    ) * HD ** (-0.5)
    valid = jnp.arange(seq_len)[None, :] < lengths[:, None]
    scores = jnp.where(valid[:, None, None, :], raw, -1e30)
    return (flat, inputs, heads_query, heads_key, heads_value, scores)


def after_attention(flat, probs_low, heads_value, params):
    rows = flat.shape[0]
    mixed = jnp.einsum(
        "phqk,pkhd->pqhd", probs_low, heads_value, preferred_element_type=jnp.float32
    )
    mixed = mixed.reshape(rows, D).astype(jnp.bfloat16)
    pre_one = flat + (matmul(mixed, params[3]) + params[8])
    normed = layer_norm(pre_one, params[11], params[12])
    normed_low = normed.astype(jnp.bfloat16)
    upward = matmul(normed_low, params[4]) + params[9]
    activated = exact_gelu(upward).astype(jnp.bfloat16)
    pre_two = normed + (matmul(activated, params[5]) + params[10])
    return (mixed, pre_one, normed_low, upward, activated, pre_two)


def forward_layer(hidden, params, lengths):
    flat, inputs, heads_query, heads_key, heads_value, scores = attention_inputs(
        hidden, params, lengths, gather_forward
    )
    row_peak = jnp.max(scores, axis=-1, keepdims=True)
    raised = jnp.exp(scores - row_peak)
    total = jnp.sum(raised, axis=-1, keepdims=True)
    probs = raised / total
    log_total = (row_peak + jnp.log(total))[..., 0]
    outcome = after_attention(flat, probs.astype(jnp.bfloat16), heads_value, params)
    result = layer_norm(outcome[5], params[13], params[14])
    return (result.reshape(hidden.shape), log_total)


def backward_layer(hidden, log_total, upstream, params, lengths, sums):
    pairs_now, rows_pair, width = hidden.shape
    flat, inputs, heads_query, heads_key, heads_value, scores = attention_inputs(
        hidden, params, lengths, gather_backward
    )
    seq_len = heads_key.shape[1]
    probs = jnp.exp(scores - log_total[..., None])
    probs_low = probs.astype(jnp.bfloat16)
    mixed, pre_one, normed_low, upward, activated, pre_two = after_attention(
        flat, probs_low, heads_value, params
    )
    second_back = jax.vjp(
        layer_norm, pre_two, params[13].astype(jnp.float32), params[14].astype(jnp.float32)
    )[1]
    d_two, d_second_gain, d_second_shift = second_back(upstream)
    down_grad = d_two.astype(jnp.bfloat16)
    d_activated = matmul_right_t(down_grad, params[5])
    d_upward = jax.vjp(exact_gelu, upward)[1](d_activated)[0]
    up_grad = d_upward.astype(jnp.bfloat16)
    d_normed = d_two + matmul_right_t(up_grad, params[4])
    first_back = jax.vjp(
        layer_norm, pre_one, params[11].astype(jnp.float32), params[12].astype(jnp.float32)
    )[1]
    d_one, d_first_gain, d_first_shift = first_back(d_normed)
    branch_grad = d_one.astype(jnp.bfloat16)
    mixed_grad = (
        matmul_right_t(branch_grad, params[3])
        .astype(jnp.bfloat16)
        .reshape(pairs_now, rows_pair, HEADS, HD)
    )
    prob_grad = jnp.einsum(
        "pqhd,pkhd->phqk", mixed_grad, heads_value, preferred_element_type=jnp.float32
    )
    value_part = jnp.einsum(
        "phqk,pqhd->pkhd", probs_low, mixed_grad, preferred_element_type=jnp.float32
    )
    weighted = jnp.sum(probs * prob_grad, axis=-1, keepdims=True)
    score_grad = (probs * (prob_grad - weighted)).astype(jnp.bfloat16)
    query_part = jnp.einsum(
        "phqk,pkhd->pqhd", score_grad, heads_key, preferred_element_type=jnp.float32
    ) * HD ** (-0.5)
    key_part = jnp.einsum(
        "phqk,pqhd->pkhd", score_grad, heads_query, preferred_element_type=jnp.float32
    ) * HD ** (-0.5)
    key_sum, value_sum = (
        lax.psum_scatter(
            key_part.reshape(pairs_now, seq_len, width).astype(jnp.bfloat16),
            "narrow",
            scatter_dimension=1,
            tiled=True,
        ).astype(jnp.float32),
        lax.psum_scatter(
            value_part.reshape(pairs_now, seq_len, width).astype(jnp.bfloat16),
            "narrow",
            scatter_dimension=1,
            tiled=True,
        ).astype(jnp.float32),
    )
    rows = pairs_now * rows_pair
    query_grad = query_part.reshape(rows, width).astype(jnp.bfloat16)
    key_grad = key_sum.reshape(rows, width).astype(jnp.bfloat16)
    value_grad = value_sum.reshape(rows, width).astype(jnp.bfloat16)
    d_input = (
        d_one
        + matmul_right_t(query_grad, params[0])
        + matmul_right_t(key_grad, params[1])
        + matmul_right_t(value_grad, params[2])
    )
    moved = (
        lax.all_to_all(split_features(inputs), "narrow", split_axis=2, concat_axis=0, tiled=True),
        lax.all_to_all(split_features(mixed), "narrow", split_axis=2, concat_axis=0, tiled=True),
        lax.all_to_all(
            split_features(normed_low), "narrow", split_axis=2, concat_axis=0, tiled=True
        ),
        lax.all_to_all(
            split_features(activated), "narrow", split_axis=2, concat_axis=0, tiled=True
        ),
    )
    left_all = [piece.reshape(piece.shape[0], piece.shape[1] * piece.shape[3]) for piece in moved]
    right_all = (
        lax.all_gather(query_grad, "narrow", axis=0, tiled=True),
        lax.all_gather(key_grad, "narrow", axis=0, tiled=True),
        lax.all_gather(value_grad, "narrow", axis=0, tiled=True),
        lax.all_gather(branch_grad, "narrow", axis=0, tiled=True),
        lax.all_gather(up_grad, "narrow", axis=0, tiled=True),
        lax.all_gather(down_grad, "narrow", axis=0, tiled=True),
    )
    mixed_all = left_all[1]
    terms = (
        matmul_left_t(left_all[0], right_all[0]),
        matmul_left_t(left_all[0], right_all[1]),
        matmul_left_t(left_all[0], right_all[2]),
        matmul_left_t(mixed_all, right_all[3]),
        matmul_left_t(left_all[2], right_all[4]),
        matmul_left_t(left_all[3], right_all[5]),
        own_features(column_sum(right_all[0])),
        own_features(column_sum(right_all[2])),
        own_features(column_sum(right_all[3])),
        own_features(column_sum(right_all[4])),
        own_features(column_sum(right_all[5])),
        d_first_gain,
        d_first_shift,
        d_second_gain,
        d_second_shift,
    )
    if sums is None:
        sums = terms
    else:
        sums = tuple((total + part for total, part in zip(sums, terms)))
    return (d_input, sums)


def reduce_layer(sums):
    count_wide = lax.axis_size("wide")
    count_narrow = lax.axis_size("narrow")
    share = D // (count_wide * count_narrow)
    norm_stack = jnp.stack([sums[11], sums[12], sums[13], sums[14]], axis=0).reshape(
        4, count_wide, count_narrow, share
    )
    norm_part = lax.psum_scatter(norm_stack, "narrow", scatter_dimension=2, tiled=True).reshape(
        4, count_wide * share
    )
    reduced = (
        lax.psum_scatter(sums[0], "wide", scatter_dimension=0, tiled=True),
        lax.psum_scatter(sums[1], "wide", scatter_dimension=0, tiled=True),
        lax.psum_scatter(sums[2], "wide", scatter_dimension=0, tiled=True),
        lax.psum_scatter(sums[3], "wide", scatter_dimension=0, tiled=True),
        lax.psum_scatter(sums[4], "wide", scatter_dimension=0, tiled=True),
        lax.psum_scatter(sums[5], "wide", scatter_dimension=0, tiled=True),
        lax.psum_scatter(sums[6], "wide", scatter_dimension=0, tiled=True),
        lax.psum_scatter(sums[7], "wide", scatter_dimension=0, tiled=True),
        lax.psum_scatter(sums[8], "wide", scatter_dimension=0, tiled=True),
        lax.psum_scatter(sums[9], "wide", scatter_dimension=0, tiled=True),
        lax.psum_scatter(sums[10], "wide", scatter_dimension=0, tiled=True),
        lax.psum_scatter(norm_part[0], "wide", scatter_dimension=0, tiled=True),
        lax.psum_scatter(norm_part[1], "wide", scatter_dimension=0, tiled=True),
        lax.psum_scatter(norm_part[2], "wide", scatter_dimension=0, tiled=True),
        lax.psum_scatter(norm_part[3], "wide", scatter_dimension=0, tiled=True),
    )
    return reduced


def body(
    tokens,
    query_weight,
    key_weight,
    value_weight,
    out_weight,
    up_weight,
    down_weight,
    query_bias,
    value_bias,
    out_bias,
    up_bias,
    down_bias,
    first_gain,
    first_shift,
    second_gain,
    second_shift,
    lengths,
    cotangent,
):

    def fetch_forward(index):
        return (
            lax.all_gather(query_weight[index], ("wide", "narrow"), axis=0, tiled=True),
            lax.all_gather(key_weight[index], ("wide", "narrow"), axis=0, tiled=True),
            lax.all_gather(value_weight[index], ("wide", "narrow"), axis=0, tiled=True),
            lax.all_gather(out_weight[index], ("wide", "narrow"), axis=0, tiled=True),
            lax.all_gather(up_weight[index], ("wide", "narrow"), axis=0, tiled=True),
            lax.all_gather(down_weight[index], ("wide", "narrow"), axis=0, tiled=True),
            lax.all_gather(query_bias[index], ("wide", "narrow"), axis=0, tiled=True),
            lax.all_gather(value_bias[index], ("wide", "narrow"), axis=0, tiled=True),
            lax.all_gather(out_bias[index], ("wide", "narrow"), axis=0, tiled=True),
            lax.all_gather(up_bias[index], ("wide", "narrow"), axis=0, tiled=True),
            lax.all_gather(down_bias[index], ("wide", "narrow"), axis=0, tiled=True),
            lax.all_gather(first_gain[index], ("wide", "narrow"), axis=0, tiled=True),
            lax.all_gather(first_shift[index], ("wide", "narrow"), axis=0, tiled=True),
            lax.all_gather(second_gain[index], ("wide", "narrow"), axis=0, tiled=True),
            lax.all_gather(second_shift[index], ("wide", "narrow"), axis=0, tiled=True),
        )

    def fetch_backward(index):
        return (
            lax.all_gather(query_weight[index], ("wide", "narrow"), axis=0, tiled=True),
            lax.all_gather(key_weight[index], ("wide", "narrow"), axis=0, tiled=True),
            lax.all_gather(value_weight[index], ("wide", "narrow"), axis=0, tiled=True),
            lax.all_gather(out_weight[index], ("wide", "narrow"), axis=0, tiled=True),
            lax.all_gather(up_weight[index], ("wide", "narrow"), axis=0, tiled=True),
            lax.all_gather(down_weight[index], ("wide", "narrow"), axis=0, tiled=True),
            lax.all_gather(query_bias[index], ("wide", "narrow"), axis=0, tiled=True),
            lax.all_gather(value_bias[index], ("wide", "narrow"), axis=0, tiled=True),
            lax.all_gather(out_bias[index], ("wide", "narrow"), axis=0, tiled=True),
            lax.all_gather(up_bias[index], ("wide", "narrow"), axis=0, tiled=True),
            lax.all_gather(down_bias[index], ("wide", "narrow"), axis=0, tiled=True),
            lax.all_gather(first_gain[index], ("wide", "narrow"), axis=0, tiled=True),
            lax.all_gather(first_shift[index], ("wide", "narrow"), axis=0, tiled=True),
            lax.all_gather(second_gain[index], ("wide", "narrow"), axis=0, tiled=True),
            lax.all_gather(second_shift[index], ("wide", "narrow"), axis=0, tiled=True),
        )

    forward_params = [fetch_forward(index) for index in range(LAYERS)]
    pairs_micro = tokens.shape[0] // MICRO
    rows_pair = tokens.shape[1]
    rows = pairs_micro * rows_pair
    kept_inputs = []
    kept_totals = []
    outputs = []
    for micro in range(MICRO):
        first_pair = micro * pairs_micro
        hidden = tokens[first_pair : first_pair + pairs_micro].astype(jnp.float32)
        micro_lengths = lengths[first_pair : first_pair + pairs_micro]
        inputs_here = []
        totals_here = []
        for index in range(LAYERS):
            inputs_here.append(hidden)
            hidden, log_total = forward_layer(hidden, forward_params[index], micro_lengths)
            totals_here.append(log_total)
        kept_inputs.append(inputs_here)
        kept_totals.append(totals_here)
        outputs.append(hidden.astype(jnp.bfloat16))
    back_params = [fetch_backward(index) for index in range(LAYERS)]
    sums = [None for index in range(LAYERS)]
    reduced = [None for index in range(LAYERS)]
    input_grads = []
    for micro in range(MICRO):
        first_pair = micro * pairs_micro
        micro_lengths = lengths[first_pair : first_pair + pairs_micro]
        upstream = (
            cotangent[first_pair : first_pair + pairs_micro].astype(jnp.float32).reshape(rows, D)
        )
        for index in reversed(range(LAYERS)):
            upstream, sums[index] = backward_layer(
                kept_inputs[micro][index],
                kept_totals[micro][index],
                upstream,
                back_params[index],
                micro_lengths,
                sums[index],
            )
        input_grads.append(upstream.reshape(pairs_micro, rows_pair, D).astype(jnp.bfloat16))
    reduced = [reduce_layer(sums[index]) for index in range(LAYERS)]
    grads = tuple(
        (
            jnp.stack([reduced[index][member] for index in range(LAYERS)], axis=0)
            for member in range(15)
        )
    )
    output = jnp.concatenate(outputs, axis=0)
    tokens_grad = jnp.concatenate(input_grads, axis=0)
    return (
        output,
        tokens_grad,
        grads[0],
        grads[1],
        grads[2],
        grads[3],
        grads[4],
        grads[5],
        grads[6],
        grads[7],
        grads[8],
        grads[9],
        grads[10],
        grads[11],
        grads[12],
        grads[13],
        grads[14],
    )


def solution(mesh):
    return jax.shard_map(
        body,
        mesh=mesh,
        in_specs=(
            P("wide", "narrow", None),
            P(None, ("wide", "narrow"), None),
            P(None, ("wide", "narrow"), None),
            P(None, ("wide", "narrow"), None),
            P(None, ("wide", "narrow"), None),
            P(None, ("wide", "narrow"), None),
            P(None, ("wide", "narrow"), None),
            P(None, ("wide", "narrow")),
            P(None, ("wide", "narrow")),
            P(None, ("wide", "narrow")),
            P(None, ("wide", "narrow")),
            P(None, ("wide", "narrow")),
            P(None, ("wide", "narrow")),
            P(None, ("wide", "narrow")),
            P(None, ("wide", "narrow")),
            P(None, ("wide", "narrow")),
            P("wide"),
            P("wide", "narrow", None),
        ),
        out_specs=(
            P("wide", "narrow", None),
            P("wide", "narrow", None),
            P(None, ("wide", "narrow"), None),
            P(None, ("wide", "narrow"), None),
            P(None, ("wide", "narrow"), None),
            P(None, ("wide", "narrow"), None),
            P(None, ("wide", "narrow"), None),
            P(None, ("wide", "narrow"), None),
            P(None, ("wide", "narrow")),
            P(None, ("wide", "narrow")),
            P(None, ("wide", "narrow")),
            P(None, ("wide", "narrow")),
            P(None, ("wide", "narrow")),
            P(None, ("wide", "narrow")),
            P(None, ("wide", "narrow")),
            P(None, ("wide", "narrow")),
            P(None, ("wide", "narrow")),
        ),
        check_vma=False,
    )
```

profile of v0, /device:TPU:0, one launch (start us, length us, event | category | flops | bytes accessed | tf_op | source)
XLA Modules:
  0.0 2088.4 jit_solution(13037911399118564888)
XLA Ops:
  24.2 43.0 %all-reduce.37 = (bf16[3072]{0:T(1024)(128)(2,1)S(1)}, bf16[3072]{0:T(1024)(128)(2,1)S(1)}, bf16[768]{0:T(1024)(128)(2,1)S(1)}, bf16[768]{0:T(1024)(128)(2,1)S(1...) all-reduce(bf16[3072]{0:T(1024)(128)(2,1)S(1)} %dynamic-update-slic, ...), channel_id=31, replica_groups=mesh['wide'=8,'narrow'=4] {'wide','narrow'}, use_global_device_ids=true, to_apply=%add.14 | all-reduce | flops 18432 | bytes 73728
  80.9 43.5 %all-gather.75.cloned.1.call-done = bf16[1,768,768]{2,1,0:T(8,128)(2,1)} async-done(((bf16[1,24,768]{2,1,0:T(8,128)(2,1)}), bf16[1,768,768]{2,1,0:T(8,128)(2,1)}) %all-gather.75.cloned.1.call-update) | async-done | bytes 1179664 | tf_op jit(solution)/shard_map/all_gather | solution.py:289
  126.0 8.6 all-gather.6
  135.8 45.1 %all-gather.71.cloned.1.call-done = bf16[1,768,768]{2,1,0:T(8,128)(2,1)} async-done(((bf16[1,24,768]{2,1,0:T(8,128)(2,1)}), bf16[1,768,768]{2,1,0:T(8,128)(2,1)}) %all-gather.71.cloned.1.call-update) | async-done | bytes 1179664 | tf_op jit(solution)/shard_map/all_gather | solution.py:290
  182.5 9.2 all-gather.2
  198.3 38.3 %all-gather.77.cloned.1.call-done = bf16[1,768,768]{2,1,0:T(8,128)(2,1)} async-done(((bf16[1,24,768]{2,1,0:T(8,128)(2,1)}), bf16[1,768,768]{2,1,0:T(8,128)(2,1)}) %all-gather.77.cloned.1.call-update) | async-done | bytes 1179664 | tf_op jit(solution)/shard_map/all_gather | solution.py:291
  244.0 10.1 all-gather.35
  258.1 9.2 all-gather.34
  281.6 20.9 %all-gather.79.cloned.1.call-done = bf16[1,768,3072]{2,1,0:T(8,128)(2,1)} async-done(((bf16[1,24,3072]{2,1,0:T(8,128)(2,1)}), bf16[1,768,3072]{2,1,0:T(8,128)(2,1)}) %all-gather.79.cloned.1.call-update) | async-done | bytes 4718608 | tf_op jit(solution)/shard_map/all_gather | solution.py:292
  302.5 65.8 %all-gather.81.cloned.1.call-done = bf16[1,3072,768]{2,1,0:T(8,128)(2,1)} async-done(((bf16[1,96,768]{2,1,0:T(8,128)(2,1)}), bf16[1,3072,768]{2,1,0:T(8,128)(2,1)}) %all-gather.81.cloned.1.call-update) | async-done | bytes 4718608 | tf_op jit(solution)/shard_map/all_gather | solution.py:293
  368.3 8.6 fusion.815
  377.2 8.9 fusion.822
  387.3 36.8 %all-gather.87.cloned.1.call-done = bf16[1,768,768]{2,1,0:T(8,128)(2,1)} async-done(((bf16[1,24,768]{2,1,0:T(8,128)(2,1)}), bf16[1,768,768]{2,1,0:T(8,128)(2,1)}) %all-gather.87.cloned.1.call-update) | async-done | bytes 1179664 | tf_op jit(solution)/shard_map/all_gather | solution.py:289
  425.8 8.6 all-gather.23
  435.6 45.0 %all-gather.85.cloned.1.call-done = bf16[1,768,768]{2,1,0:T(8,128)(2,1)} async-done(((bf16[1,24,768]{2,1,0:T(8,128)(2,1)}), bf16[1,768,768]{2,1,0:T(8,128)(2,1)}) %all-gather.85.cloned.1.call-update) | async-done | bytes 1179664 | tf_op jit(solution)/shard_map/all_gather | solution.py:288
  483.0 54.1 %all-gather.83.cloned.1.call-done = bf16[1,768,768]{2,1,0:T(8,128)(2,1)} async-done(((bf16[1,24,768]{2,1,0:T(8,128)(2,1)}), bf16[1,768,768]{2,1,0:T(8,128)(2,1)}) %all-gather.83.cloned.1.call-update) | async-done | bytes 1179664 | tf_op jit(solution)/shard_map/all_gather | solution.py:290
  538.7 8.6 all-gather.19
  553.7 39.1 %all-gather.89.cloned.1.call-done = bf16[1,768,768]{2,1,0:T(8,128)(2,1)} async-done(((bf16[1,24,768]{2,1,0:T(8,128)(2,1)}), bf16[1,768,768]{2,1,0:T(8,128)(2,1)}) %all-gather.89.cloned.1.call-update) | async-done | bytes 1179664 | tf_op jit(solution)/shard_map/all_gather | solution.py:291
  596.2 62.7 %all-gather.91.cloned.1.call-done = bf16[1,768,3072]{2,1,0:T(8,128)(2,1)} async-done(((bf16[1,24,3072]{2,1,0:T(8,128)(2,1)}), bf16[1,768,3072]{2,1,0:T(8,128)(2,1)}) %all-gather.91.cloned.1.call-update) | async-done | bytes 4718608 | tf_op jit(solution)/shard_map/all_gather | solution.py:292
  658.9 65.8 %all-gather.93.cloned.1.call-done = bf16[1,3072,768]{2,1,0:T(8,128)(2,1)} async-done(((bf16[1,96,768]{2,1,0:T(8,128)(2,1)}), bf16[1,3072,768]{2,1,0:T(8,128)(2,1)}) %all-gather.93.cloned.1.call-update) | async-done | bytes 4718608 | tf_op jit(solution)/shard_map/all_gather | solution.py:293
  724.7 10.0 fusion.840
  738.8 9.1 all-gather.37
  755.8 9.6 all-gather.36
  774.7 10.0 fusion.834
  823.7 5.6 multiply_reduce_fusion.5
  875.7 8.4 multiply_convert_fusion.5
  893.2 8.5 multiply_convert_fusion.9
  913.1 10.5 reduce-scatter.77.cloned.1.call-done
  925.8 23.7 %reduce-scatter.75.cloned.1.call-done = bf16[128,768]{1,0:T(8,128)(2,1)} async-done(((bf16[512,768]{1,0:T(8,128)(2,1)}), bf16[128,768]{1,0:T(8,128)(2,1)}) %reduce-scatter.75.cloned.1.call-update) | async-done | bytes 196624
  1030.9 13.1 all_gather.274
  1048.2 10.3 all_gather.275
  1080.7 13.0 all_gather.272
  1093.7 8.7 all_gather.273
  1108.2 5.7 all-to-all-done.1
  1119.0 14.1 all_gather.262
  1137.5 14.2 all_gather.263
  1155.6 13.3 all_gather.260
  1170.9 8.7 all_gather.261
  1183.3 9.2 all-gather.44
  1193.8 8.7 all-gather.45
  1207.9 9.1 all-gather.42
  1218.3 8.7 all-gather.43
  1237.3 15.7 all-gather.40
  1253.4 8.7 all-gather.41
  1265.7 8.7 all-gather.38
  1276.4 8.7 all-gather.39
  1290.2 16.7 all_gather.282
  1306.8 8.9 all_gather.283
  1328.8 10.2 all-to-all-done.12
  1343.4 10.8 all-to-all-done.13
  1354.7 8.0 all_gather.280
  1362.8 8.7 all_gather.281
  1463.0 11.5 reduce-scatter.39.cloned.1.call-done
  1482.9 20.8 all-gather.63.cloned.1.call-done
  1507.8 25.9 %all-gather.65.cloned.1.call-done = bf16[512,3072]{1,0:T(8,128)(2,1)} async-done(((bf16[128,3072]{1,0:T(8,128)(2,1)}), bf16[512,3072]{1,0:T(8,128)(2,1)}) %all-gather.65.cloned.1.call-update) | async-done | bytes 3145744 | tf_op jit(solution)/shard_map/all_gather | solution.py:207
  1541.1 58.0 %reduce-scatter.49.cloned.1.call-done = f32[24,768]{1,0:T(8,128)} async-done(((f32[192,768]{1,0:T(8,128)}), f32[24,768]{1,0:T(8,128)}) %reduce-scatter.49.cloned.1.call-update) | async-done | bytes 73744 | tf_op jit(solution)/shard_map/reduce_scatter | solution.py:248
  1599.1 64.9 %reduce-scatter.47.cloned.1.call-done = f32[24,768]{1,0:T(8,128)} async-done(((f32[192,768]{1,0:T(8,128)}), f32[24,768]{1,0:T(8,128)}) %reduce-scatter.47.cloned.1.call-update) | async-done | bytes 73744 | tf_op jit(solution)/shard_map/reduce_scatter | solution.py:248
  1665.6 62.6 %reduce-scatter.45.cloned.1.call-done = f32[24,768]{1,0:T(8,128)} async-done(((f32[192,768]{1,0:T(8,128)}), f32[24,768]{1,0:T(8,128)}) %reduce-scatter.45.cloned.1.call-update) | async-done | bytes 73744 | tf_op jit(solution)/shard_map/reduce_scatter | solution.py:247
  1728.2 64.9 %reduce-scatter.43.cloned.1.call-done = f32[24,768]{1,0:T(8,128)} async-done(((f32[192,768]{1,0:T(8,128)}), f32[24,768]{1,0:T(8,128)}) %reduce-scatter.43.cloned.1.call-update) | async-done | bytes 73744 | tf_op jit(solution)/shard_map/reduce_scatter | solution.py:247
  1802.2 35.9 %all-reduce.36 = (f32[192]{0:T(256)S(1)}, f32[192]{0:T(256)S(1)}, f32[192]{0:T(256)S(1)}, f32[192]{0:T(256)S(1)}, f32[192]{0:T(256)S(1)}, /*index=5*/f32[192]{0:...) all-reduce(f32[192]{0:T(256)S(1)} %copy-done.269, ...), channel_id=69, replica_groups=mesh['wide'=8,'narrow'=4] {'wide'}, use_global_device_ids=true, to_apply=%region_85.86.clone | all-reduce | flops 4608 | bytes 36864
  1844.6 20.1 reduce-scatter.61.cloned.1.call-done
  1864.8 71.6 %reduce-scatter.59.cloned.1.call-done = f32[96,768]{1,0:T(8,128)} async-done(((f32[768,768]{1,0:T(8,128)}), f32[96,768]{1,0:T(8,128)}) %reduce-scatter.59.cloned.1.call-update) | async-done | bytes 294928 | tf_op jit(solution)/shard_map/reduce_scatter | solution.py:251
  1938.3 69.7 %reduce-scatter.57.cloned.1.call-done = f32[24,3072]{1,0:T(8,128)} async-done(((f32[192,3072]{1,0:T(8,128)}), f32[24,3072]{1,0:T(8,128)}) %reduce-scatter.57.cloned.1.call-update) | async-done | bytes 294928 | tf_op jit(solution)/shard_map/reduce_scatter | solution.py:250
  2007.9 71.8 %reduce-scatter.55.cloned.1.call-done = f32[24,3072]{1,0:T(8,128)} async-done(((f32[192,3072]{1,0:T(8,128)}), f32[24,3072]{1,0:T(8,128)}) %reduce-scatter.55.cloned.1.call-update) | async-done | bytes 294928 | tf_op jit(solution)/shard_map/reduce_scatter | solution.py:250
  (1284 shorter events, 520.8 us)
Async XLA Ops:
  7.3 71.1 %all-gather.73.cloned.1.call-start = ((), (), s32[]{:S(2)}) async-start(), calls=%async_computation.57 | async-start | bytes 1216512 | tf_op jit(solution)/shard_map/all_gather | solution.py:288
  8.9 115.5 %all-gather.75.cloned.1.call-start = ((), (), s32[]{:S(2)}) async-start(), calls=%async_computation.58 | async-start | bytes 1216512 | tf_op jit(solution)/shard_map/all_gather | solution.py:289
  10.4 170.4 %all-gather.71.cloned.1.call-start = ((), (), s32[]{:S(2)}) async-start(), calls=%async_computation.56 | async-start | bytes 1216512 | tf_op jit(solution)/shard_map/all_gather | solution.py:290
  11.9 224.7 %all-gather.77.cloned.1.call-start = ((), (), s32[]{:S(2)}) async-start(), calls=%async_computation.59 | async-start | bytes 1216512 | tf_op jit(solution)/shard_map/all_gather | solution.py:291
  13.4 289.1 %all-gather.79.cloned.1.call-start = ((), (), s32[]{:S(2)}) async-start(), calls=%async_computation.60 | async-start | bytes 4866048 | tf_op jit(solution)/shard_map/all_gather | solution.py:292
  15.2 353.1 %all-gather.81.cloned.1.call-start = ((), (), s32[]{:S(2)}) async-start(), calls=%async_computation.61 | async-start | bytes 4866048 | tf_op jit(solution)/shard_map/all_gather | solution.py:293
  16.0 408.1 %all-gather.87.cloned.1.call-start = ((), (), s32[]{:S(2)}) async-start(), calls=%async_computation.64 | async-start | bytes 1216512 | tf_op jit(solution)/shard_map/all_gather | solution.py:289
  16.8 463.8 %all-gather.85.cloned.1.call-start = ((), (), s32[]{:S(2)}) async-start(), calls=%async_computation.63 | async-start | bytes 1216512 | tf_op jit(solution)/shard_map/all_gather | solution.py:288
  17.5 519.5 %all-gather.83.cloned.1.call-start = ((), (), s32[]{:S(2)}) async-start(), calls=%async_computation.62 | async-start | bytes 1216512 | tf_op jit(solution)/shard_map/all_gather | solution.py:290
  18.2 574.6 %all-gather.89.cloned.1.call-start = ((), (), s32[]{:S(2)}) async-start(), calls=%async_computation.65 | async-start | bytes 1216512 | tf_op jit(solution)/shard_map/all_gather | solution.py:291
  18.8 640.1 %all-gather.91.cloned.1.call-start = ((), (), s32[]{:S(2)}) async-start(), calls=%async_computation.66 | async-start | bytes 4866048 | tf_op jit(solution)/shard_map/all_gather | solution.py:292
  19.6 705.2 %all-gather.93.cloned.1.call-start = ((), (), s32[]{:S(2)}) async-start(), calls=%async_computation.67 | async-start | bytes 4866048 | tf_op jit(solution)/shard_map/all_gather | solution.py:293
  20.1 889.1 %reduce-scatter.69.cloned.1.call-start = ((), (), s32[]{:S(2)}) async-start(), calls=%async_computation.69 | async-start | bytes 983040
  69.0 111.9 %copy-start.219 = (f32[768]{0:T(1024)}, f32[768]{0:T(1024)S(1)}, u32[]{:S(2)}) copy-start(f32[768]{0:T(1024)S(1)} %convert_element_type.998) | copy-start | bytes 9220
  278.2 90.1 %copy-start.168 = (f32[128,768]{1,0:T(8,128)S(1)}, f32[128,768]{1,0:T(8,128)}, u32[]{:S(2)}) copy-start(f32[128,768]{1,0:T(8,128)} %get-tuple-element.175) | copy-start | bytes 1179652
  278.2 90.1 %copy-start.213 = (f32[768]{0:T(1024)S(1)}, f32[768]{0:T(1024)}, u32[]{:S(2)}) copy-start(f32[768]{0:T(1024)} %convert_element_type.1004) | copy-start | bytes 9220
  278.3 90.1 %copy-start.246 = (f32[3072]{0:T(1024)S(1)}, f32[3072]{0:T(1024)}, u32[]{:S(2)}) copy-start(f32[3072]{0:T(1024)} %convert_element_type.1003) | copy-start | bytes 36868
  278.3 90.1 %copy-start.317 = (f32[128]{0:T(128)S(1)}, f32[128]{0:T(128)}, u32[]{:S(2)}) copy-start(f32[128]{0:T(128)} %broadcast_multiply_fusion.15) | copy-start | bytes 1540
  278.8 98.2 %copy-start.225 = (f32[128]{0:T(128)}, f32[128]{0:T(128)S(1)}, u32[]{:S(2)}) copy-start(f32[128]{0:T(128)S(1)} %get-tuple-element.229) | copy-start | bytes 1540
  281.6 95.6 %copy-start.170 = (f32[128,768]{1,0:T(8,128)S(1)}, f32[128,768]{1,0:T(8,128)}, u32[]{:S(2)}) copy-start(f32[128,768]{1,0:T(8,128)} %copy-done.169) | copy-start | bytes 1179652
  281.6 95.6 %copy-start.319 = (f32[128]{0:T(128)S(1)}, f32[128]{0:T(128)}, u32[]{:S(2)}) copy-start(f32[128]{0:T(128)} %copy-done.318) | copy-start | bytes 1540
  387.3 149.8 %copy-start.88 = (bf16[128,768]{1,0:T(8,128)(2,1)}, bf16[128,768]{1,0:T(8,128)(2,1)S(1)}, u32[]{:S(2)}) copy-start(bf16[128,768]{1,0:T(8,128)(2,1)S(1)} %get-tuple-element.133) | copy-start | bytes 589828
  434.4 102.7 %copy-start.217 = (f32[768]{0:T(1024)S(1)}, f32[768]{0:T(1024)}, u32[]{:S(2)}) copy-start(f32[768]{0:T(1024)} %convert_element_type.1007) | copy-start | bytes 9220
  848.4 63.1 %reduce-scatter.67.cloned.1.call-start = ((), (), s32[]{:S(2)}) async-start(), calls=%async_computation.68 | async-start | bytes 983040
  875.6 48.0 %reduce-scatter.77.cloned.1.call-start = ((), (), s32[]{:S(2)}) async-start(), calls=%async_computation.73 | async-start | bytes 983040
  893.1 56.3 %reduce-scatter.75.cloned.1.call-start = ((), (), s32[]{:S(2)}) async-start(), calls=%async_computation.72 | async-start | bytes 983040
  902.8 302.0 %reduce-scatter.73.cloned.1.call-start = ((), (), s32[]{:S(2)}) async-start(), calls=%async_computation.71 | async-start | bytes 983040
  988.6 217.3 %reduce-scatter.81.cloned.1.call-start = ((), (), s32[]{:S(2)}) async-start(), calls=%async_computation.75 | async-start | bytes 983040
  1005.9 257.5 %reduce-scatter.71.cloned.1.call-start = ((), (), s32[]{:S(2)}) async-start(), calls=%async_computation.70 | async-start | bytes 983040
  1016.3 258.5 %reduce-scatter.79.cloned.1.call-start = ((), (), s32[]{:S(2)}) async-start(), calls=%async_computation.74 | async-start | bytes 983040
  1023.7 398.1 %all-gather.67.cloned.1.call-start = ((), (), s32[]{:S(2)}) async-start(), calls=%async_computation.49 | async-start | bytes 3932160 | tf_op jit(solution)/shard_map/all_gather | solution.py:207
  1024.4 400.2 %all-gather.69.cloned.1.call-start = ((), (), s32[]{:S(2)}) async-start(), calls=%async_computation.50 | async-start | bytes 3932160 | tf_op jit(solution)/shard_map/all_gather | solution.py:207
  1027.5 17.3 all-to-all-start.6
  1044.8 15.0 all-to-all-start.7
  1048.2 390.5 %reduce-scatter.65.cloned.1.call-start = ((), (), s32[]{:S(2)}) async-start(), calls=%async_computation.55 | async-start | bytes 81920 | tf_op jit(solution)/shard_map/reduce_scatter | solution.py:242
  1059.8 8.7 all-to-all-start.4
  1063.2 394.8 %reduce-scatter.63.cloned.1.call-start = ((), (), s32[]{:S(2)}) async-start(), calls=%async_computation.54 | async-start | bytes 81920 | tf_op jit(solution)/shard_map/reduce_scatter | solution.py:242
  1066.3 395.1 %reduce-scatter.53.cloned.1.call-start = ((), (), s32[]{:S(2)}) async-start(), calls=%async_computation.45 | async-start | bytes 663552 | tf_op jit(solution)/shard_map/reduce_scatter | solution.py:249
  1068.5 8.7 all-to-all-start.5
  1077.2 25.6 %all-to-all-start = ((bf16[128,8,4,24]{0,3,1,2:T(8,128)(2,1)}), bf16[128,8,4,24]{0,3,1,2:T(8,128)(2,1)S(1)}, u32[]{:S(2)}, u32[]{:S(2)}) async-start(bf16[128,8,4,24]{0,3,1,2:T(8,128)(2,1)} %copy.192), calls=%async_computation | async-start | bytes 393216 | tf_op jit(solution)/shard_map/all_to_all | solution.py:192
  1102.8 11.1 all-to-all-start.1
  1106.2 355.2 %reduce-scatter.51.cloned.1.call-start = ((), (), s32[]{:S(2)}) async-start(), calls=%async_computation.44 | async-start | bytes 663552 | tf_op jit(solution)/shard_map/reduce_scatter | solution.py:249
  1115.6 18.4 all-to-all-start.2
  1134.1 17.8 all-to-all-start.3
  1137.4 325.6 %reduce-scatter.41.cloned.1.call-start = ((), (), s32[]{:S(2)}) async-start(), calls=%async_computation.39 | async-start | bytes 663552 | tf_op jit(solution)/shard_map/reduce_scatter | solution.py:246
  1154.4 320.1 %reduce-scatter.39.cloned.1.call-start = ((), (), s32[]{:S(2)}) async-start(), calls=%async_computation.38 | async-start | bytes 663552 | tf_op jit(solution)/shard_map/reduce_scatter | solution.py:246
  1181.9 321.8 %all-gather.63.cloned.1.call-start = ((), (), s32[]{:S(2)}) async-start(), calls=%async_computation.46 | async-start | bytes 3932160 | tf_op jit(solution)/shard_map/all_gather | solution.py:207
  1182.6 351.1 %all-gather.65.cloned.1.call-start = ((), (), s32[]{:S(2)}) async-start(), calls=%async_computation.47 | async-start | bytes 3932160 | tf_op jit(solution)/shard_map/all_gather | solution.py:207
  1183.2 415.9 %reduce-scatter.49.cloned.1.call-start = ((), (), s32[]{:S(2)}) async-start(), calls=%async_computation.43 | async-start | bytes 663552 | tf_op jit(solution)/shard_map/reduce_scatter | solution.py:248
  1204.7 459.3 %reduce-scatter.47.cloned.1.call-start = ((), (), s32[]{:S(2)}) async-start(), calls=%async_computation.42 | async-start | bytes 663552 | tf_op jit(solution)/shard_map/reduce_scatter | solution.py:248
  1232.6 53.8 %all-to-all-start.14 = ((bf16[128,8,4,96]{0,3,1,2:T(8,128)(2,1)}), bf16[128,8,4,96]{0,3,1,2:T(8,128)(2,1)S(1)}, u32[]{:S(2)}, u32[]{:S(2)}) async-start(bf16[128,8,4,96]{0,3,1,2:T(8,128)(2,1)} %copy.230), calls=%async_computation.25 | async-start | bytes 1572864 | tf_op jit(solution)/shard_map/all_to_all | solution.py:197
  1236.2 492.0 %reduce-scatter.45.cloned.1.call-start = ((), (), s32[]{:S(2)}) async-start(), calls=%async_computation.41 | async-start | bytes 663552 | tf_op jit(solution)/shard_map/reduce_scatter | solution.py:247
  1263.4 529.7 %reduce-scatter.43.cloned.1.call-start = ((), (), s32[]{:S(2)}) async-start(), calls=%async_computation.40 | async-start | bytes 663552 | tf_op jit(solution)/shard_map/reduce_scatter | solution.py:247
  1286.4 30.8 %all-to-all-start.15 = ((bf16[128,8,4,96]{0,3,1,2:T(8,128)(2,1)}), bf16[128,8,4,96]{0,3,1,2:T(8,128)(2,1)S(1)}, u32[]{:S(2)}, u32[]{:S(2)}) async-start(bf16[128,8,4,96]{0,3,1,2:T(8,128)(2,1)} %copy.233), calls=%async_computation.26 | async-start | bytes 1572864 | tf_op jit(solution)/shard_map/all_to_all | solution.py:197
  1290.1 574.6 %reduce-scatter.61.cloned.1.call-start = ((), (), s32[]{:S(2)}) async-start(), calls=%async_computation.53 | async-start | bytes 2654208 | tf_op jit(solution)/shard_map/reduce_scatter | solution.py:251
  1323.9 15.1 all-to-all-start.12
  1339.0 15.1 all-to-all-start.13
  1342.5 593.9 %reduce-scatter.59.cloned.1.call-start = ((), (), s32[]{:S(2)}) async-start(), calls=%async_computation.52 | async-start | bytes 2654208 | tf_op jit(solution)/shard_map/reduce_scatter | solution.py:251
  1376.2 8.8 all-to-all-start.8
  1385.1 8.7 all-to-all-start.9
  1403.6 8.7 all-to-all-start.10
  1412.3 8.7 all-to-all-start.11
  1415.6 592.3 %reduce-scatter.57.cloned.1.call-start = ((), (), s32[]{:S(2)}) async-start(), calls=%async_computation.51 | async-start | bytes 2654208 | tf_op jit(solution)/shard_map/reduce_scatter | solution.py:250
  1428.9 650.8 %reduce-scatter.55.cloned.1.call-start = ((), (), s32[]{:S(2)}) async-start(), calls=%async_computation.48 | async-start | bytes 2654208 | tf_op jit(solution)/shard_map/reduce_scatter | solution.py:250
  (329 other events, 2474.2 us)
Sparse Core Ops, SparseCore 0:
  11.6 56.8 all-gather.72
  71.4 52.9 all-gather.74
  127.9 52.9 all-gather.70
  183.6 52.9 all-gather.76
  239.9 62.5 all-gather.78
  305.8 62.4 all-gather.80
  371.2 52.8 all-gather.86
  427.6 52.9 all-gather.84
  484.1 52.9 all-gather.82
  539.8 52.9 all-gather.88
  596.3 62.5 all-gather.90
  662.2 62.4 all-gather.92
  848.6 22.0 reduce-scatter.68
  875.8 22.1 reduce-scatter.66
  900.4 23.2 reduce-scatter.76
  926.2 23.2 reduce-scatter.74
  988.7 23.2 reduce-scatter.72
  1014.5 26.1 reduce-scatter.80
  1043.2 23.7 reduce-scatter.70
  1069.5 25.6 reduce-scatter.78
  1096.8 34.4 all-gather.66
  1132.8 36.3 all-gather.68
  1172.3 19.4 reduce-scatter.64
  1194.7 19.4 reduce-scatter.62
  1217.5 62.0 reduce-scatter.52
  1283.1 61.1 reduce-scatter.50
  1348.0 61.0 reduce-scatter.40
  1413.4 61.1 reduce-scatter.38
  1476.1 27.5 all-gather.62
  1505.1 28.5 all-gather.64
  1537.0 62.0 reduce-scatter.48
  1602.8 61.1 reduce-scatter.46
  1667.1 61.0 reduce-scatter.44
  1731.9 61.1 reduce-scatter.42
  1796.6 68.1 reduce-scatter.60
  1868.1 68.2 reduce-scatter.58
  1939.7 68.1 reduce-scatter.56
  2011.4 68.2 reduce-scatter.54
where the time goes:
time: 2100 us; the launch traced here: 2090 us
  waiting for transfers between devices  1150 us (55%)
  blocking collectives  367 us (17%)
  matrix products  233 us (11%)
  local copies, waits for them, and re-layouts  186 us (9%)
  other arithmetic  79.2 us (4%)
  starting transfers between devices  57 us (3%)
    reduce_scatter x2, waiting for transfers between devices, reduce_layer(): lax.psum_scatter(sums[4], 'wide', scatter_dimension=0, tiled=True)  141 us
    all_gather x2, waiting for transfers between devices, fetch_forward(): lax.all_gather(down_weight[index], ('wide', 'narrow'), axis=0, tiled=True)  132 us
    reduce_scatter x2, waiting for transfers between devices, reduce_layer(): lax.psum_scatter(sums[1], 'wide', scatter_dimension=0, tiled=True)  128 us
    reduce_scatter x2, waiting for transfers between devices, reduce_layer(): lax.psum_scatter(sums[2], 'wide', scatter_dimension=0, tiled=True)  123 us
    all_gather x2, waiting for transfers between devices, fetch_forward(): lax.all_gather(value_weight[index], ('wide', 'narrow'), axis=0, tiled=True)  99.1 us
    unnamed x756, local copies, waits for them, and re-layouts  97.1 us
    dot_general x32, matrix products, matmul(): return jnp.dot(left, right, preferred_element_type=jnp.float32)  97 us
    reduce_scatter x2, waiting for transfers between devices, reduce_layer(): lax.psum_scatter(sums[5], 'wide', scatter_dimension=0, tiled=True)  91.7 us
  transfers between devices with their start and end apart: 54, of which 33 were waited for; matrix products, arithmetic and copies ran while one was open for 16% of the time, Pallas kernels for 0%

commit v1 on v0

v1 whole, which is shorter than its diff:
```python
import functools

import jax
import jax.numpy as jnp
from jax import lax
from jax.experimental import pallas as pl
from jax.experimental.pallas import tpu as pltpu
from jax.sharding import PartitionSpec as P

D = 768
HEADS = 12
HD = 64
FF = 3072
LAYERS = 2
PAD = 128
LOW = jnp.bfloat16
FULL = jnp.float32


def bits_of(name):
    return lax.axis_size(name).bit_length() - 1


def swap(value, name, bit):
    pairs = [(i, i ^ (1 << bit)) for i in range(lax.axis_size(name))]
    return lax.ppermute(value, name, pairs)


def own_bit(name, bit):
    return (lax.axis_index(name) >> bit) & 1


def axis_of(name, bit):
    if name == "wide":
        return bits_of("wide") - 1 - bit
    return bits_of("wide") + bits_of("narrow") - 1 - bit


def order(first):
    far = [("wide", bit) for bit in range(bits_of("wide") - 1, 0, -1)]
    middle = [("wide", 0), ("narrow", 1)]
    if first == "narrow":
        middle.reverse()
    return far + middle + [("narrow", 0)]


def gather(shard, first):
    lead = bits_of("wide") + bits_of("narrow")
    held = shard.reshape((1,) * lead + shard.shape)
    for name, bit in order(first):
        other = swap(held, name, bit)
        mine_low = own_bit(name, bit) == 0
        held = jnp.concatenate(
            [jnp.where(mine_low, held, other), jnp.where(mine_low, other, held)],
            axis=axis_of(name, bit),
        )
    return held.reshape(-1, shard.shape[-1])


def scatter(whole, first):
    lead = bits_of("wide") + bits_of("narrow")
    count = lax.axis_size("wide") * lax.axis_size("narrow")
    held = whole.reshape((2,) * lead + (whole.shape[0] // count, whole.shape[1]))
    for name, bit in reversed(order(first)):
        axis = axis_of(name, bit)
        mine = own_bit(name, bit)
        kept = lax.dynamic_index_in_dim(held, mine, axis)
        other = swap(lax.dynamic_index_in_dim(held, 1 - mine, axis), name, bit)
        total = kept.astype(FULL) + other.astype(FULL)
        held = total.astype(LOW)
    return total.reshape(total.shape[-2:])


def stack_heads(pair):
    lane = lax.broadcasted_iota(jnp.int32, pair.shape, 1)
    zero = jnp.zeros_like(pair)
    return jnp.concatenate(
        [jnp.where(lane < HD, pair, zero), jnp.where(lane < HD, zero, pair)], axis=0
    )


def pick_heads(stacked):
    rows = stacked.shape[0] // 2
    lane = lax.broadcasted_iota(jnp.int32, (rows, stacked.shape[1]), 1)
    return jnp.where(lane < HD, stacked[:rows], stacked[rows:])


def dot_t(left, right):
    return lax.dot_general(left, right, (((1,), (1,)), ((), ())), preferred_element_type=FULL)


def dot_l(left, right):
    return lax.dot_general(left, right, (((0,), (0,)), ((), ())), preferred_element_type=FULL)


def attend_kernel(meta, query, *rest):
    count = (len(rest) - 2) // 2
    keys, values, mixed, probs = rest[:count], rest[count : 2 * count], rest[-2], rest[-1]
    length = meta[pl.program_id(0)]
    pairs = pl.num_programs(0)
    stacked = stack_heads(query[0])
    parts = []
    for j in range(count):
        part = dot_t(stacked, keys[j][0]) * HD**-0.5
        place = meta[pairs + j] + lax.broadcasted_iota(jnp.int32, part.shape, 1)
        parts.append(jnp.where(place < length, part, -1e30))
    scores = jnp.concatenate(parts, axis=1)
    raised = jnp.exp(scores - jnp.max(scores, axis=1, keepdims=True))
    low = (raised / jnp.sum(raised, axis=1, keepdims=True)).astype(LOW)
    probs[0, 0] = low
    value = jnp.concatenate([block[0] for block in values], axis=0)
    mixed[0] = pick_heads(jnp.dot(low, value, preferred_element_type=FULL)).astype(LOW)


def attend(queries, blocks, meta):
    pairs, rows, width = queries.shape
    steps = width // 128
    count = len(blocks)
    spec_key = pl.BlockSpec((1, rows, 128), lambda p, h, meta: (p, 0, h))
    spec_value = pl.BlockSpec((1, rows, 128), lambda p, h, meta: (p, 0, steps + h))
    return pl.pallas_call(
        attend_kernel,
        grid_spec=pltpu.PrefetchScalarGridSpec(
            num_scalar_prefetch=1,
            grid=(pairs, steps),
            in_specs=[spec_key] + [spec_key] * count + [spec_value] * count,
            out_specs=[
                spec_key,
                pl.BlockSpec((1, 1, 2 * rows, count * rows), lambda p, h, meta: (p, h, 0, 0)),
            ],
        ),
        out_shape=[
            jax.ShapeDtypeStruct(queries.shape, LOW),
            jax.ShapeDtypeStruct((pairs, steps, 2 * rows, count * rows), LOW),
        ],
    )(meta, queries, *blocks, *blocks)


def attend_back_kernel(count, query, mixed_grad, probs, *rest):
    keys, values = rest[:count], rest[count : 2 * count]
    query_grad, key_grad, value_grad = rest[2 * count :]
    rows = query.shape[1]
    queries = stack_heads(query[0])
    grads = stack_heads(mixed_grad[0])
    low = probs[0, 0]
    key = jnp.concatenate([block[0] for block in keys], axis=0)
    value = jnp.concatenate([block[0] for block in values], axis=0)
    prob_grad = dot_t(grads, value)
    wide = low.astype(FULL)
    weighted = jnp.sum(wide * prob_grad, axis=1, keepdims=True)
    score_grad = (wide * (prob_grad - weighted)).astype(LOW)
    query_grad[0] = (
        pick_heads(jnp.dot(score_grad, key, preferred_element_type=FULL)) * HD**-0.5
    ).astype(LOW)
    key_all = (dot_l(score_grad, queries) * HD**-0.5).astype(LOW)
    value_all = dot_l(low, grads).astype(LOW)
    for j in range(count):
        key_grad[j, 0] = key_all[j * rows : (j + 1) * rows]
        value_grad[j, 0] = value_all[j * rows : (j + 1) * rows]


def attend_back(queries, mixed_grad, probs, blocks):
    pairs, rows, width = queries.shape
    steps = width // 128
    count = len(blocks)
    spec_key = pl.BlockSpec((1, rows, 128), lambda p, h: (p, 0, h))
    spec_value = pl.BlockSpec((1, rows, 128), lambda p, h: (p, 0, steps + h))
    spec_probs = pl.BlockSpec((1, 1, 2 * rows, count * rows), lambda p, h: (p, h, 0, 0))
    spec_all = pl.BlockSpec((count, 1, rows, 128), lambda p, h: (0, p, 0, h))
    shape_all = jax.ShapeDtypeStruct((count, pairs, rows, width), LOW)
    return pl.pallas_call(
        functools.partial(attend_back_kernel, count),
        grid=(pairs, steps),
        in_specs=[spec_key, spec_key, spec_probs] + [spec_key] * count + [spec_value] * count,
        out_specs=[spec_key, spec_all, spec_all],
        out_shape=[jax.ShapeDtypeStruct(queries.shape, LOW), shape_all, shape_all],
    )(queries, mixed_grad, probs, *blocks, *blocks)


def matmul(left, right):
    return jnp.dot(left, right, preferred_element_type=FULL)


def normalise(values):
    average = jnp.mean(values, axis=-1, keepdims=True)
    centred = values - average
    variance = jnp.mean(centred * centred, axis=-1, keepdims=True)
    scale = lax.rsqrt(variance + 1e-05)
    return centred * scale, scale


def normalise_back(grad, gain, unit, scale):
    scaled = grad * gain
    first = jnp.mean(scaled, axis=-1, keepdims=True)
    second = jnp.mean(scaled * unit, axis=-1, keepdims=True)
    return scale * (scaled - first - unit * second)


def share_pair(block):
    held = [block]
    for bit in range(bits_of("narrow") - 1, -1, -1):
        stride = 1 << bit
        others = [swap(piece, "narrow", bit) for piece in held]
        held = [
            piece for both in zip(held, others) for piece in both
        ]
        del stride
    return held


def forward_layer(hidden, weights, vectors, meta, shape):
    pairs, rows_pair = shape
    attention, up, down = weights
    inputs = hidden.astype(LOW)
    both = matmul(inputs, attention[:, D : 3 * D])
    offset = jnp.concatenate([jnp.zeros((D,), LOW), vectors["value_bias"]])
    both = (both + offset).astype(LOW).reshape(pairs, rows_pair, 2 * D)
    blocks = share_pair(both)
    queries = (matmul(inputs, attention[:, :D]) + vectors["query_bias"]).astype(LOW)
    queries = queries.reshape(pairs, rows_pair, D)
    mixed, probs = attend(queries, blocks, meta)
    mixed = mixed.reshape(-1, D)
    pre_one = hidden + (matmul(mixed, attention[:, 3 * D : 4 * D]) + vectors["out_bias"])
    unit_one, scale_one = normalise(pre_one)
    normed = unit_one * vectors["first_gain"] + vectors["first_shift"]
    normed_low = normed.astype(LOW)
    upward = matmul(normed_low, up) + vectors["up_bias"]
    share = 0.5 * (1.0 + lax.erf(upward * (0.5**0.5)))
    density = jnp.exp(-0.5 * upward * upward) * 0.3989422804014327
    activated = (upward * share).astype(LOW)
    slope = (share + upward * density).astype(LOW)
    pre_two = normed + (matmul(activated, down) + vectors["down_bias"])
    unit_two, scale_two = normalise(pre_two)
    result = unit_two * vectors["second_gain"] + vectors["second_shift"]
    kept = (inputs, queries, blocks, probs, mixed, unit_one, scale_one, normed_low)
    kept += (activated, slope, unit_two, scale_two)
    return result, kept


def column_sum(values):
    return jnp.sum(values.astype(FULL), axis=0)


def left_t(left, right):
    return jnp.einsum("ra,rb->ab", left, right, preferred_element_type=FULL).astype(LOW)


def right_t(left, right):
    return jnp.einsum("ra,ba->rb", left, right, preferred_element_type=FULL)


def gather_sum(parts):
    held = list(parts)
    for bit in range(bits_of("narrow")):
        kept, sent = held[0::2], held[1::2]
        others = [swap(piece, "narrow", bit) for piece in sent]
        held = [
            (mine.astype(FULL) + other.astype(FULL)).astype(LOW)
            for mine, other in zip(kept, others)
        ]
    return held[0]


def backward_layer(upstream, kept, weights, vectors, shape):
    pairs, rows_pair = shape
    attention, up, down = weights
    (inputs, queries, blocks, probs, mixed, unit_one, scale_one, normed_low) = kept[:8]
    activated, slope, unit_two, scale_two = kept[8:]
    grads = {}
    grads["second_gain"] = column_sum(upstream * unit_two)
    grads["second_shift"] = column_sum(upstream)
    d_two = normalise_back(upstream, vectors["second_gain"], unit_two, scale_two)
    down_grad = d_two.astype(LOW)
    up_grad = (right_t(down_grad, down) * slope).astype(LOW)
    grads["down_bias"] = column_sum(down_grad)
    grads["up_bias"] = column_sum(up_grad)
    d_down = left_t(activated, down_grad)
    d_up = left_t(normed_low, up_grad)
    d_normed = d_two + right_t(up_grad, up)
    grads["first_gain"] = column_sum(d_normed * unit_one)
    grads["first_shift"] = column_sum(d_normed)
    d_one = normalise_back(d_normed, vectors["first_gain"], unit_one, scale_one)
    branch_grad = d_one.astype(LOW)
    grads["out_bias"] = column_sum(branch_grad)
    mixed_grad = right_t(branch_grad, attention[:, 3 * D : 4 * D]).astype(LOW)
    query_grad, key_parts, value_parts = attend_back(
        queries, mixed_grad.reshape(queries.shape), probs, blocks
    )
    count = len(blocks)
    both_parts = [
        jnp.stack([key_parts[j], value_parts[j]], axis=0) for j in range(count)
    ]
    both = gather_sum(both_parts)
    query_grad = query_grad.reshape(-1, D)
    key_grad, value_grad = both[0].reshape(-1, D), both[1].reshape(-1, D)
    grads["query_bias"] = column_sum(query_grad)
    grads["value_bias"] = column_sum(value_grad)
    three = jnp.concatenate([query_grad, key_grad, value_grad], axis=1)
    d_input = d_one + right_t(three, attention[:, : 3 * D])
    d_attention = jnp.concatenate([left_t(inputs, three), left_t(mixed, branch_grad)], axis=1)
    return d_input, (d_attention, d_up, d_down), grads


NAMES = (
    "query_bias",
    "value_bias",
    "out_bias",
    "down_bias",
    "first_gain",
    "first_shift",
    "second_gain",
    "second_shift",
    "up_bias",
)
COLUMNS = 8 + FF // D


def pack_shards(shards):
    rows = []
    for layer in shards:
        for name in NAMES:
            piece = layer[name]
            rows.append(piece.reshape(-1, layer[NAMES[0]].shape[0]))
    stacked = jnp.concatenate(rows, axis=0)
    stacked = jnp.pad(stacked, ((0, PAD - stacked.shape[0]), (0, 0)))
    return stacked.T


def unpack_whole(columns):
    count = lax.axis_size("wide") * lax.axis_size("narrow")
    rows = columns.T
    out = []
    for index in range(LAYERS):
        base = index * COLUMNS
        vectors = {name: rows[base + i] for i, name in enumerate(NAMES[:-1])}
        up = rows[base + 8 : base + COLUMNS].reshape(FF // D, count, D // count)
        vectors["up_bias"] = up.transpose(1, 0, 2).reshape(FF)
        out.append(vectors)
    return out


def pack_whole(grads):
    count = lax.axis_size("wide") * lax.axis_size("narrow")
    rows = []
    for layer in grads:
        rows += [layer[name].reshape(1, D) for name in NAMES[:-1]]
        up = layer["up_bias"].reshape(count, FF // D, D // count)
        rows.append(up.transpose(1, 0, 2).reshape(FF // D, D))
    stacked = jnp.concatenate(rows, axis=0)
    stacked = jnp.pad(stacked, ((0, PAD - stacked.shape[0]), (0, 0)))
    return stacked.T.astype(LOW)


def unpack_shards(columns):
    rows = columns.T
    out = []
    for index in range(LAYERS):
        base = index * COLUMNS
        layer = {name: rows[base + i] for i, name in enumerate(NAMES[:-1])}
        layer["up_bias"] = rows[base + 8 : base + COLUMNS].reshape(-1)
        out.append(layer)
    return out


def body(
    tokens,
    query_weight,
    key_weight,
    value_weight,
    out_weight,
    up_weight,
    down_weight,
    query_bias,
    value_bias,
    out_bias,
    up_bias,
    down_bias,
    first_gain,
    first_shift,
    second_gain,
    second_shift,
    lengths,
    cotangent,
):
    pairs, rows_pair, width = tokens.shape
    shape = (pairs, rows_pair)
    given = dict(
        query_bias=query_bias,
        value_bias=value_bias,
        out_bias=out_bias,
        up_bias=up_bias,
        down_bias=down_bias,
        first_gain=first_gain,
        first_shift=first_shift,
        second_gain=second_gain,
        second_shift=second_shift,
    )
    shards = [{name: given[name][index] for name in NAMES} for index in range(LAYERS)]
    weights = []
    vectors = None
    for index in range(LAYERS):
        attention = [query_weight[index], key_weight[index], value_weight[index], out_weight[index]]
        if index == 0:
            attention.append(pack_shards(shards))
        attention = gather(jnp.concatenate(attention, axis=1), "wide")
        if index == 0:
            vectors = unpack_whole(attention[:, 4 * D :])
        up = gather(up_weight[index], "narrow")
        down = gather(down_weight[index], "wide")
        weights.append((attention, up, down))
    narrow = lax.axis_index("narrow")
    places = [(narrow ^ j) * rows_pair for j in range(lax.axis_size("narrow"))]
    meta = jnp.concatenate([lengths, jnp.stack(places).astype(jnp.int32)])
    hidden = tokens.astype(FULL).reshape(-1, width)
    kept = []
    for index in range(LAYERS):
        hidden, saved = forward_layer(hidden, weights[index], vectors[index], meta, shape)
        kept.append(saved)
    output = hidden.astype(LOW).reshape(tokens.shape)
    upstream = cotangent.astype(FULL).reshape(-1, width)
    small = [None] * LAYERS
    large = [None] * LAYERS
    for index in reversed(range(LAYERS)):
        upstream, large[index], small[index] = backward_layer(
            upstream, kept[index], weights[index], vectors[index], shape
        )
    tokens_grad = upstream.astype(LOW).reshape(tokens.shape)
    shares = [None] * LAYERS
    for index in reversed(range(LAYERS)):
        d_attention, d_up, d_down = large[index]
        if index == 0:
            d_attention = jnp.concatenate([d_attention, pack_whole(small)], axis=1)
        shares[index] = (
            scatter(d_attention, "wide"),
            scatter(d_up, "narrow"),
            scatter(d_down, "wide"),
        )
    vector_shares = unpack_shards(shares[0][0][:, 4 * D :])

    def stacked(select):
        return jnp.stack([select(index) for index in range(LAYERS)], axis=0)

    weight_grads = [
        stacked(lambda index, i=i: shares[index][0][:, i * D : (i + 1) * D]) for i in range(4)
    ]
    weight_grads.append(stacked(lambda index: shares[index][1]))
    weight_grads.append(stacked(lambda index: shares[index][2]))
    names = (
        "query_bias",
        "value_bias",
        "out_bias",
        "up_bias",
        "down_bias",
        "first_gain",
        "first_shift",
        "second_gain",
        "second_shift",
    )
    vector_grads = [stacked(lambda index, n=name: vector_shares[index][n]) for name in names]
    return (output, tokens_grad, *weight_grads, *vector_grads)


def solution(mesh):
    rows = P("wide", "narrow", None)
    weight = P(None, ("wide", "narrow"), None)
    vector = P(None, ("wide", "narrow"))
    return jax.shard_map(
        body,
        mesh=mesh,
        in_specs=(rows,) + (weight,) * 6 + (vector,) * 9 + (P("wide"), rows),
        out_specs=(rows, rows) + (weight,) * 6 + (vector,) * 9,
        check_vma=False,
    )
```

time: 2100 us -> 675 us (0.32)
  waiting for transfers between devices: 1150 us -> 300 us
  blocking collectives: 367 us -> 0 us
  matrix products: 233 us -> 68.6 us
  local copies, waits for them, and re-layouts: 186 us -> 80.1 us
  Pallas kernels: 0 us -> 48.1 us
    all_gather x16 -> x0, waiting for transfers between devices: 564 us -> none  [the longest x2 132 us: fetch_forward(): lax.all_gather(down_weight[index], ('wide', 'narrow'), axis=0, tiled=True)]
    reduce_scatter x14 -> x0, waiting for transfers between devices: 495 us -> none  [the longest x2 141 us: reduce_layer(): lax.psum_scatter(sums[4], 'wide', scatter_dimension=0, tiled=True)]
    ppermute x0 -> x72, waiting for transfers between devices: none -> 300 us  [swap(): return lax.ppermute(value, name, pairs)]
    all_gather x28 -> x0, blocking collectives: 288 us -> none  [the longest x4 50.3 us: backward_layer(): lax.all_gather(query_grad, 'narrow', axis=0, tiled=True)]
    dot_general x108 -> x26, matrix products: 233 us -> 68.6 us  [the longest x10 28.2 us: matmul(): return jnp.dot(left, right, preferred_element_type=FULL)]
    unnamed x756 -> x241, local copies, waits for them, and re-layouts: 97.1 us -> 11.7 us
    unnamed x2 -> x0, blocking collectives: 78.9 us -> none
    ppermute x0 -> x72, starting transfers between devices: none -> 72.2 us  [swap(): return lax.ppermute(value, name, pairs)]
  transfers between devices with their start and end apart: 54 -> 72, of which waited for: 33 -> 39; matrix products, arithmetic and copies ran while one was open for 16% -> 29% of each run, Pallas kernels for 0% -> 4%
where the time goes in v1:
time: 675 us; the launch traced here: 662 us
  waiting for transfers between devices  300 us (44%)
  other arithmetic  89.6 us (13%)
  local copies, waits for them, and re-layouts  80.1 us (12%)
  starting transfers between devices  72.2 us (11%)
  matrix products  68.6 us (10%)
  Pallas kernels  48.1 us (7%)
    ppermute x72, waiting for transfers between devices, swap(): return lax.ppermute(value, name, pairs)  300 us
    ppermute x72, starting transfers between devices, swap(): return lax.ppermute(value, name, pairs)  72.2 us
    dot_general x10, matrix products, matmul(): return jnp.dot(left, right, preferred_element_type=FULL)  28.2 us
    pallas_call x2, Pallas kernels, attend_back(): pl.pallas_call(functools.partial(attend_back_kernel, count), grid=(pairs,...  25.2 us
    pallas_call x2, Pallas kernels, attend(): pl.pallas_call(attend_kernel, grid_spec=pltpu.PrefetchScalarGridSpec(num_...  22.9 us
    dot_general x8, matrix products, right_t(): return jnp.einsum('ra,ba->rb', left, right, preferred_element_type=FULL)  22.2 us
    convert_element_type x24, other arithmetic, scatter(): held = total.astype(LOW)  19.4 us
    concatenate x30, other arithmetic, gather(): jnp.concatenate([jnp.where(mine_low, held, other), jnp.where(mine_low, ot...  19 us
  transfers between devices with their start and end apart: 72, of which 39 were waited for; matrix products, arithmetic and copies ran while one was open for 29% of the time, Pallas kernels for 4%

profile of v1, /device:TPU:0, one launch (start us, length us, event | category | flops | bytes accessed | tf_op | source)
XLA Modules:
  0.0 661.5 jit_solution(9742941215547584216)
XLA Ops:
  1.8 4.1 collective-permute-start.13
  9.0 2.9 collective-permute-start.18
  13.1 2.8 collective-permute-start.8
  26.3 3.2 collective-permute-done.31
  29.6 3.3 collective-permute-start.14
  33.0 3.1 collective-permute-done.18
  36.1 3.1 collective-permute-done.26
  39.2 3.2 collective-permute-done.8
  45.6 5.5 collective-permute-done.14
  51.1 6.3 collective-permute-done.32
  59.2 4.5 collective-permute-done.19
  63.8 6.3 collective-permute-done.27
  72.5 3.9 collective-permute-done.9
  78.2 4.7 collective-permute-done.1
  88.2 10.9 %collective-permute-done.15 = bf16[2,2,1,1,1,96,768]{6,5,4,3,2,1,0:T(8,128)(2,1)S(1)} collective-permute-done((bf16[2,2,1,1,1,96,768]{6,5,4,3,2,1,0:T(8,128)(2,1)S(1)}, bf16[2,2,1,1,1,96,768]{6,5,4,3,2,1,0:T(8,128)(2,1)S(1)}, u32[]{:S(2)}, u32[]{:S(2)}) %collective-permute-start.15) | collective-permute-done | bytes 589856 | tf_op jit(solution)/shard_map/ppermute | solution.py:26
  101.7 3.8 collective-permute-done.28
  107.2 5.1 collective-permute-done.2
  114.2 16.5 %collective-permute-done.34 = bf16[2,2,2,1,1,96,768]{6,5,4,3,2,1,0:T(8,128)(2,1)S(1)} collective-permute-done((bf16[2,2,2,1,1,96,768]{6,5,4,3,2,1,0:T(8,128)(2,1)S(1)}, bf16[2,2,2,1,1,96,768]{6,5,4,3,2,1,0:T(8,128)(2,1)S(1)}, u32[]{:S(2)}, u32[]{:S(2)}) %collective-permute-start.34) | collective-permute-done | bytes 1179680 | tf_op jit(solution)/shard_map/ppermute | solution.py:26
  134.6 21.4 %collective-permute-done.21 = bf16[2,2,2,1,1,24,3072]{6,5,4,3,2,1,0:T(8,128)(2,1)S(1)} collective-permute-done((bf16[2,2,2,1,1,24,3072]{6,5,4,3,2,1,0:T(8,128)(2,1)S(1)}, bf16[2,2,2,1,1,24,3072]{6,5,4,3,2,1,0:T(8,128)(2,1)S(1)}, u32[]{:S(2)}, u32[]{:S(2)}) %collective-permute-start.21) | collective-permute-done | bytes 1179680 | tf_op jit(solution)/shard_map/ppermute | solution.py:26
  156.4 24.9 %collective-permute-done.16 = bf16[2,2,2,1,1,96,768]{6,5,4,3,2,1,0:T(8,128)(2,1)S(1)} collective-permute-done((bf16[2,2,2,1,1,96,768]{6,5,4,3,2,1,0:T(8,128)(2,1)S(1)}, bf16[2,2,2,1,1,96,768]{6,5,4,3,2,1,0:T(8,128)(2,1)S(1)}, u32[]{:S(2)}, u32[]{:S(2)}) %collective-permute-start.16) | collective-permute-done | bytes 1179680 | tf_op jit(solution)/shard_map/ppermute | solution.py:26
  184.6 22.0 %collective-permute-done.3 = bf16[2,2,2,1,1,24,3200]{6,5,4,3,2,1,0:T(8,128)(2,1)S(1)} collective-permute-done((bf16[2,2,2,1,1,24,3200]{6,5,4,3,2,1,0:T(8,128)(2,1)S(1)}, bf16[2,2,2,1,1,24,3200]{6,5,4,3,2,1,0:T(8,128)(2,1)S(1)}, u32[]{:S(2)}, u32[]{:S(2)}) %collective-permute-start.3) | collective-permute-done | bytes 1228832 | tf_op jit(solution)/shard_map/ppermute | solution.py:26
  208.0 2.6 pad_maximum_fusion.4
  226.0 4.4 broadcast_select_fusion.7
  230.4 13.5 %collective-permute-done.6.rest_2_.rest_6_ = bf16[2,128,1536]{2,1,0:T(8,128)(2,1)S(1)} collective-permute-done((bf16[2,128,1536]{2,1,0:T(8,128)(2,1)S(1)}, bf16[2,128,1536]{2,1,0:T(8,128)(2,1)S(1)}, u32[]{:S(2)}, u32[]{:S(2)}) %collective-permute-start.6) | collective-permute-done | bytes 786464 | tf_op jit(solution)/shard_map/ppermute | solution.py:26
  243.9 2.6 pad_maximum_fusion.3
  249.9 2.6 fusion.35
  253.7 11.5 %shard_map.305 = (bf16[2,128,768]{2,1,0:T(8,128)(2,1)}, bf16[2,6,256,512]{3,2,1,0:T(8,128)(2,1)}) custom-call(s32[6]{0:T(128)} %concatenate.124.meta, bf16[2,128,768]{2,1,0:T(8,128)(2,1)} %bitcast.240, bf16[2,128,1536]{2,1,0:T(8,128)(2,1)} %bitcast.197, bf16[2,128,1536]{2,1,0:T(8,128)(2,1)} %copy-done.6, bf16[2,128,1536]{2,1,0:T(8,128)(2,1)} %copy-done.5, ...), custom_call_target="tpu_custom_call" | custom-call | tf_op jit(solution)/shard_map/pallas_call | solution.py:121
  267.4 5.9 multiply_convert_fusion.1
  273.4 4.4 fusion.98
  285.9 13.3 %collective-permute-done.24.rest_2_.rest_6_ = bf16[2,128,1536]{2,1,0:T(8,128)(2,1)S(1)} collective-permute-done((bf16[2,128,1536]{2,1,0:T(8,128)(2,1)S(1)}, bf16[2,128,1536]{2,1,0:T(8,128)(2,1)S(1)}, u32[]{:S(2)}, u32[]{:S(2)}) %collective-permute-start.24) | collective-permute-done | bytes 786464 | tf_op jit(solution)/shard_map/ppermute | solution.py:26
  307.8 2.6 fusion.34
  311.5 11.5 %shard_map.306 = (bf16[2,128,768]{2,1,0:T(8,128)(2,1)}, bf16[2,6,256,512]{3,2,1,0:T(8,128)(2,1)}) custom-call(s32[6]{0:T(128)} %concatenate.124.meta, bf16[2,128,768]{2,1,0:T(8,128)(2,1)} %bitcast.242, bf16[2,128,1536]{2,1,0:T(8,128)(2,1)} %bitcast.203, bf16[2,128,1536]{2,1,0:T(8,128)(2,1)} %copy-done.10, bf16[2,128,1536]{2,1,0:T(8,128)(2,1)} %copy-done.9, ...), custom_call_target="tpu_custom_call" | custom-call | tf_op jit(solution)/shard_map/pallas_call | solution.py:121
  325.3 3.8 multiply_convert_fusion
  333.6 3.5 fusion.102
  342.7 12.6 %shard_map.307 = (bf16[2,128,768]{2,1,0:T(8,128)(2,1)}, bf16[4,2,128,768]{3,2,1,0:T(8,128)(2,1)}, bf16[4,2,128,768]{3,2,1,0:T(8,128)(2,1)}) custom-call(bf16[2,128,768]{2,1,0:T(8,128)(2,1)} %bitcast.243, bf16[2,128,768]{2,1,0:T(8,128)(2,1)} %bitcast.239, bf16[2,6,256,512]{3,2,1,0:T(8,128)(2,1)} %get-tuple-element.29.probs, bf16[2,128,1536]{2,1,0:T(8,128)(2,1)} %bitcast.205, ...), custom_call_target="tpu_custom_call" | custom-call | tf_op jit(solution)/shard_map/pallas_call | solution.py:171
  374.5 3.0 convolution_convert_fusion
  388.0 13.1 %collective-permute-done.38 = bf16[2,2,128,768]{3,2,1,0:T(8,128)(2,1)S(1)} collective-permute-done((bf16[2,2,128,768]{3,2,1,0:T(8,128)(2,1)S(1)}, bf16[2,2,128,768]{3,2,1,0:T(8,128)(2,1)S(1)}, u32[]{:S(2)}, u32[]{:S(2)}) %collective-permute-start.38) | collective-permute-done | bytes 786464 | tf_op jit(solution)/shard_map/ppermute | solution.py:26
  406.7 3.2 fusion.101
  413.0 2.6 convolution_convert_fusion.8
  417.2 2.9 convolution_convert_fusion.4
  420.1 12.6 %shard_map.308 = (bf16[2,128,768]{2,1,0:T(8,128)(2,1)}, bf16[4,2,128,768]{3,2,1,0:T(8,128)(2,1)}, bf16[4,2,128,768]{3,2,1,0:T(8,128)(2,1)}) custom-call(bf16[2,128,768]{2,1,0:T(8,128)(2,1)} %bitcast.241, bf16[2,128,768]{2,1,0:T(8,128)(2,1)} %bitcast.238, bf16[2,6,256,512]{3,2,1,0:T(8,128)(2,1)} %get-tuple-element.33.probs, bf16[2,128,1536]{2,1,0:T(8,128)(2,1)} %bitcast.199, ...), custom_call_target="tpu_custom_call" | custom-call | tf_op jit(solution)/shard_map/pallas_call | solution.py:171
  440.0 3.7 convolution_convert_fusion.3
  450.5 3.4 constant_dynamic-slice_fusion.19
  458.6 2.6 add_convert_fusion.3
  469.6 13.7 %collective-permute-done.41 = bf16[2,2,128,768]{3,2,1,0:T(8,128)(2,1)S(1)} collective-permute-done((bf16[2,2,128,768]{3,2,1,0:T(8,128)(2,1)S(1)}, bf16[2,2,128,768]{3,2,1,0:T(8,128)(2,1)S(1)}, u32[]{:S(2)}, u32[]{:S(2)}) %collective-permute-start.41) | collective-permute-done | bytes 786464 | tf_op jit(solution)/shard_map/ppermute | solution.py:26
  487.7 4.0 concatenate.162
  495.0 2.8 pad_maximum_fusion.1
  497.9 7.7 %copy.87 = bf16[768,3200]{1,0:T(8,128)(2,1)} copy(bf16[768,3200]{0,1:T(8,128)(2,1)} %pad_maximum_fusion.1) | data formatting | bytes 9830400 | tf_op jit(solution)/shard_map/concatenate | solution.py:432
  507.6 4.1 fusion.31
  520.7 3.0 add_convert_fusion.4
  532.1 7.4 %collective-permute-done.70 = bf16[2,1,1,1,1,96,768]{6,5,4,3,2,1,0:T(8,128)(2,1)S(1)} collective-permute-done((bf16[2,1,1,1,1,96,768]{6,5,4,3,2,1,0:T(8,128)(2,1)S(1)}, bf16[2,1,1,1,1,96,768]{6,5,4,3,2,1,0:T(8,128)(2,1)S(1)}, u32[]{:S(2)}, u32[]{:S(2)}) %collective-permute-start.70) | collective-permute-done | bytes 294944 | tf_op jit(solution)/shard_map/ppermute | solution.py:26
  539.9 6.3 collective-permute-done.60
  546.3 3.2 collective-permute-start.71
  549.6 7.0 %collective-permute-done.71 = bf16[1,1,1,1,1,96,768]{6,5,4,3,2,1,0:T(8,128)(2,1)S(1)} collective-permute-done((bf16[1,1,1,1,1,96,768]{6,5,4,3,2,1,0:T(8,128)(2,1)S(1)}, bf16[1,1,1,1,1,96,768]{6,5,4,3,2,1,0:T(8,128)(2,1)S(1)}, u32[]{:S(2)}, u32[]{:S(2)}) %collective-permute-start.71) | collective-permute-done | bytes 147488 | tf_op jit(solution)/shard_map/ppermute | solution.py:26
  556.8 7.4 %collective-permute-done.61 = bf16[1,1,1,1,1,24,3072]{6,5,4,3,2,1,0:T(8,128)(2,1)S(1)} collective-permute-done((bf16[1,1,1,1,1,24,3072]{6,5,4,3,2,1,0:T(8,128)(2,1)S(1)}, bf16[1,1,1,1,1,24,3072]{6,5,4,3,2,1,0:T(8,128)(2,1)S(1)}, u32[]{:S(2)}, u32[]{:S(2)}) %collective-permute-start.61) | collective-permute-done | bytes 147488 | tf_op jit(solution)/shard_map/ppermute | solution.py:26
  568.3 14.2 %collective-permute-done.48 = bf16[2,2,2,1,1,24,3072]{6,5,4,3,2,1,0:T(8,128)(2,1)S(1)} collective-permute-done((bf16[2,2,2,1,1,24,3072]{6,5,4,3,2,1,0:T(8,128)(2,1)S(1)}, bf16[2,2,2,1,1,24,3072]{6,5,4,3,2,1,0:T(8,128)(2,1)S(1)}, u32[]{:S(2)}, u32[]{:S(2)}) %collective-permute-start.48) | collective-permute-done | bytes 1179680 | tf_op jit(solution)/shard_map/ppermute | solution.py:26
  587.1 8.0 %collective-permute-done.54 = bf16[2,2,1,1,1,24,3072]{6,5,4,3,2,1,0:T(8,128)(2,1)S(1)} collective-permute-done((bf16[2,2,1,1,1,24,3072]{6,5,4,3,2,1,0:T(8,128)(2,1)S(1)}, bf16[2,2,1,1,1,24,3072]{6,5,4,3,2,1,0:T(8,128)(2,1)S(1)}, u32[]{:S(2)}, u32[]{:S(2)}) %collective-permute-start.54) | collective-permute-done | bytes 589856 | tf_op jit(solution)/shard_map/ppermute | solution.py:26
  597.8 3.7 collective-permute-start.66
  601.5 8.6 %collective-permute-done.55 = bf16[2,1,1,1,1,24,3072]{6,5,4,3,2,1,0:T(8,128)(2,1)S(1)} collective-permute-done((bf16[2,1,1,1,1,24,3072]{6,5,4,3,2,1,0:T(8,128)(2,1)S(1)}, bf16[2,1,1,1,1,24,3072]{6,5,4,3,2,1,0:T(8,128)(2,1)S(1)}, u32[]{:S(2)}, u32[]{:S(2)}) %collective-permute-start.55) | collective-permute-done | bytes 294944 | tf_op jit(solution)/shard_map/ppermute | solution.py:26
  615.9 7.8 %collective-permute-done.56 = bf16[1,1,1,1,1,24,3072]{6,5,4,3,2,1,0:T(8,128)(2,1)S(1)} collective-permute-done((bf16[1,1,1,1,1,24,3072]{6,5,4,3,2,1,0:T(8,128)(2,1)S(1)}, bf16[1,1,1,1,1,24,3072]{6,5,4,3,2,1,0:T(8,128)(2,1)S(1)}, u32[]{:S(2)}, u32[]{:S(2)}) %collective-permute-start.56) | collective-permute-done | bytes 147488 | tf_op jit(solution)/shard_map/ppermute | solution.py:26
  625.7 10.7 %collective-permute-done.44 = bf16[2,2,1,1,1,24,3200]{6,5,4,3,2,1,0:T(8,128)(2,1)S(1)} collective-permute-done((bf16[2,2,1,1,1,24,3200]{6,5,4,3,2,1,0:T(8,128)(2,1)S(1)}, bf16[2,2,1,1,1,24,3200]{6,5,4,3,2,1,0:T(8,128)(2,1)S(1)}, u32[]{:S(2)}, u32[]{:S(2)}) %collective-permute-start.44) | collective-permute-done | bytes 614432 | tf_op jit(solution)/shard_map/ppermute | solution.py:26
  637.5 6.0 collective-permute-done.45
  643.6 3.0 collective-permute-start.46
  647.5 4.0 collective-permute-done.46
  (621 shorter events, 222.3 us)
Async XLA Ops:
  1.8 24.6 %collective-permute-start.13 = (bf16[1,1,1,1,1,96,768]{6,5,4,3,2,1,0:T(8,128)(2,1)S(1)}, bf16[1,1,1,1,1,96,768]{6,5,4,3,2,1,0:T(8,128)(2,1)S(1)}, u32[]{:S(2)}, u32[]{:S(2)}) collective-permute-start(bf16[1,1,1,1,1,96,768]{6,5,4,3,2,1,0:T(8,128)(2,1)S(1)} %get-tuple-element.220), channel_id=1, source_target_pairs={{0,16},{4,20},{8,24},{12,28},{16,0},{20,4},{24,8},{28,12},{1,17},{... | collective-permute-start | bytes 442376 | tf_op jit(solution)/shard_map/ppermute | solution.py:26
  5.9 23.6 %collective-permute-start.31 = (bf16[1,1,1,1,1,96,768]{6,5,4,3,2,1,0:T(8,128)(2,1)S(1)}, bf16[1,1,1,1,1,96,768]{6,5,4,3,2,1,0:T(8,128)(2,1)S(1)}, u32[]{:S(2)}, u32[]{:S(2)}) collective-permute-start(bf16[1,1,1,1,1,96,768]{6,5,4,3,2,1,0:T(8,128)(2,1)S(1)} %get-tuple-element.219), channel_id=1, source_target_pairs={{0,16},{4,20},{8,24},{12,28},{16,0},{20,4},{24,8},{28,12},{1,17},{... | collective-permute-start | bytes 442376 | tf_op jit(solution)/shard_map/ppermute | solution.py:26
  9.0 27.0 %collective-permute-start.18 = (bf16[1,1,1,1,1,24,3072]{6,5,4,3,2,1,0:T(8,128)(2,1)S(1)}, bf16[1,1,1,1,1,24,3072]{6,5,4,3,2,1,0:T(8,128)(2,1)S(1)}, u32[]{:S(2)}, u32[]{:S(2)}) collective-permute-start(bf16[1,1,1,1,1,24,3072]{6,5,4,3,2,1,0:T(8,128)(2,1)S(1)} %maximum_bitcast_fusion), channel_id=1, source_target_pairs={{0,16},{4,20},{8,24},{12,28},{16,0},{20,4},{24,8},{28,12},{1,17},{... | collective-permute-start | bytes 442376 | tf_op jit(solution)/shard_map/ppermute | solution.py:26
  13.0 26.2 %collective-permute-start.26 = (bf16[1,1,1,1,1,24,3072]{6,5,4,3,2,1,0:T(8,128)(2,1)S(1)}, bf16[1,1,1,1,1,24,3072]{6,5,4,3,2,1,0:T(8,128)(2,1)S(1)}, u32[]{:S(2)}, u32[]{:S(2)}) collective-permute-start(bf16[1,1,1,1,1,24,3072]{6,5,4,3,2,1,0:T(8,128)(2,1)S(1)} %get-tuple-element.226), channel_id=1, source_target_pairs={{0,16},{4,20},{8,24},{12,28},{16,0},{20,4},{24,8},{28,12},{1,17},{... | collective-permute-start | bytes 442376 | tf_op jit(solution)/shard_map/ppermute | solution.py:26
  13.1 29.3 %collective-permute-start.8 = (bf16[1,1,1,1,1,24,3072]{6,5,4,3,2,1,0:T(8,128)(2,1)S(1)}, bf16[1,1,1,1,1,24,3072]{6,5,4,3,2,1,0:T(8,128)(2,1)S(1)}, u32[]{:S(2)}, u32[]{:S(2)}) collective-permute-start(bf16[1,1,1,1,1,24,3072]{6,5,4,3,2,1,0:T(8,128)(2,1)S(1)} %get-tuple-element.225), channel_id=1, source_target_pairs={{0,16},{4,20},{8,24},{12,28},{16,0},{20,4},{24,8},{28,12},{1,17},{... | collective-permute-start | bytes 442376 | tf_op jit(solution)/shard_map/ppermute | solution.py:26
  26.3 18.5 %collective-permute-start = (bf16[1,1,1,1,1,24,3200]{6,5,4,3,2,1,0:T(8,128)(2,1)S(1)}, bf16[1,1,1,1,1,24,3200]{6,5,4,3,2,1,0:T(8,128)(2,1)S(1)}, u32[]{:S(2)}, u32[]{:S(2)}) collective-permute-start(bf16[1,1,1,1,1,24,3200]{6,5,4,3,2,1,0:T(8,128)(2,1)S(1)} %bitcast.266), channel_id=1, source_target_pairs={{0,16},{4,20},{8,24},{12,28},{16,0},{20,4},{24,8},{28,12},{1,17},{... | collective-permute-start | bytes 460808 | tf_op jit(solution)/shard_map/ppermute | solution.py:26
  29.6 21.5 %collective-permute-start.14 = (bf16[2,1,1,1,1,96,768]{6,5,4,3,2,1,0:T(8,128)(2,1)S(1)}, bf16[2,1,1,1,1,96,768]{6,5,4,3,2,1,0:T(8,128)(2,1)S(1)}, u32[]{:S(2)}, u32[]{:S(2)}) collective-permute-start(bf16[2,1,1,1,1,96,768]{6,5,4,3,2,1,0:T(8,128)(2,1)S(1)} %pad_maximum_fusion.40), channel_id=1, source_target_pairs={{0,8},{4,12},{8,0},{12,4},{16,24},{20,28},{24,16},{28,20},{1,9},{5... | collective-permute-start | bytes 884744 | tf_op jit(solution)/shard_map/ppermute | solution.py:26
  36.0 21.4 %collective-permute-start.32 = (bf16[2,1,1,1,1,96,768]{6,5,4,3,2,1,0:T(8,128)(2,1)S(1)}, bf16[2,1,1,1,1,96,768]{6,5,4,3,2,1,0:T(8,128)(2,1)S(1)}, u32[]{:S(2)}, u32[]{:S(2)}) collective-permute-start(bf16[2,1,1,1,1,96,768]{6,5,4,3,2,1,0:T(8,128)(2,1)S(1)} %pad_maximum_fusion.43), channel_id=1, source_target_pairs={{0,8},{4,12},{8,0},{12,4},{16,24},{20,28},{24,16},{28,20},{1,9},{5... | collective-permute-start | bytes 884744 | tf_op jit(solution)/shard_map/ppermute | solution.py:26
  39.2 24.5 %collective-permute-start.19 = (bf16[2,1,1,1,1,24,3072]{6,5,4,3,2,1,0:T(8,128)(2,1)S(1)}, bf16[2,1,1,1,1,24,3072]{6,5,4,3,2,1,0:T(8,128)(2,1)S(1)}, u32[]{:S(2)}, u32[]{:S(2)}) collective-permute-start(bf16[2,1,1,1,1,24,3072]{6,5,4,3,2,1,0:T(8,128)(2,1)S(1)} %pad_maximum_fusion.41), channel_id=1, source_target_pairs={{0,8},{4,12},{8,0},{12,4},{16,24},{20,28},{24,16},{28,20},{1,9},{5... | collective-permute-start | bytes 884744 | tf_op jit(solution)/shard_map/ppermute | solution.py:26
  42.5 27.6 %collective-permute-start.27 = (bf16[2,1,1,1,1,24,3072]{6,5,4,3,2,1,0:T(8,128)(2,1)S(1)}, bf16[2,1,1,1,1,24,3072]{6,5,4,3,2,1,0:T(8,128)(2,1)S(1)}, u32[]{:S(2)}, u32[]{:S(2)}) collective-permute-start(bf16[2,1,1,1,1,24,3072]{6,5,4,3,2,1,0:T(8,128)(2,1)S(1)} %pad_maximum_fusion.42), channel_id=1, source_target_pairs={{0,8},{4,12},{8,0},{12,4},{16,24},{20,28},{24,16},{28,20},{1,9},{5... | collective-permute-start | bytes 884744 | tf_op jit(solution)/shard_map/ppermute | solution.py:26
  44.8 31.6 %collective-permute-start.9 = (bf16[2,1,1,1,1,24,3072]{6,5,4,3,2,1,0:T(8,128)(2,1)S(1)}, bf16[2,1,1,1,1,24,3072]{6,5,4,3,2,1,0:T(8,128)(2,1)S(1)}, u32[]{:S(2)}, u32[]{:S(2)}) collective-permute-start(bf16[2,1,1,1,1,24,3072]{6,5,4,3,2,1,0:T(8,128)(2,1)S(1)} %pad_maximum_fusion.39), channel_id=1, source_target_pairs={{0,8},{4,12},{8,0},{12,4},{16,24},{20,28},{24,16},{28,20},{1,9},{5... | collective-permute-start | bytes 884744 | tf_op jit(solution)/shard_map/ppermute | solution.py:26
  51.1 31.8 %collective-permute-start.1 = (bf16[2,1,1,1,1,24,3200]{6,5,4,3,2,1,0:T(8,128)(2,1)S(1)}, bf16[2,1,1,1,1,24,3200]{6,5,4,3,2,1,0:T(8,128)(2,1)S(1)}, u32[]{:S(2)}, u32[]{:S(2)}) collective-permute-start(bf16[2,1,1,1,1,24,3200]{6,5,4,3,2,1,0:T(8,128)(2,1)S(1)} %pad_maximum_fusion.38), channel_id=1, source_target_pairs={{0,8},{4,12},{8,0},{12,4},{16,24},{20,28},{24,16},{28,20},{1,9},{5... | collective-permute-start | bytes 921608 | tf_op jit(solution)/shard_map/ppermute | solution.py:26
  57.6 27.0 %collective-permute-start.33 = (bf16[2,2,1,1,1,96,768]{6,5,4,3,2,1,0:T(8,128)(2,1)S(1)}, bf16[2,2,1,1,1,96,768]{6,5,4,3,2,1,0:T(8,128)(2,1)S(1)}, u32[]{:S(2)}, u32[]{:S(2)}) collective-permute-start(bf16[2,2,1,1,1,96,768]{6,5,4,3,2,1,0:T(8,128)(2,1)S(1)} %pad_maximum_fusion.31), channel_id=1, source_target_pairs={{0,4},{4,0},{8,12},{12,8},{16,20},{20,16},{24,28},{28,24},{1,5},{5... | collective-permute-start | bytes 1769480 | tf_op jit(solution)/shard_map/ppermute | solution.py:26
  70.2 16.3 %collective-permute-start.20 = (bf16[2,2,1,1,1,24,3072]{6,5,4,3,2,1,0:T(8,128)(2,1)S(1)}, bf16[2,2,1,1,1,24,3072]{6,5,4,3,2,1,0:T(8,128)(2,1)S(1)}, u32[]{:S(2)}, u32[]{:S(2)}) collective-permute-start(bf16[2,2,1,1,1,24,3072]{6,5,4,3,2,1,0:T(8,128)(2,1)S(1)} %pad_maximum_fusion.29), channel_id=1, source_target_pairs={{0,4},{4,0},{8,12},{12,8},{16,20},{20,16},{24,28},{28,24},{1,5},{5... | collective-permute-start | bytes 1769480 | tf_op jit(solution)/shard_map/ppermute | solution.py:26
  71.9 27.2 %collective-permute-start.15 = (bf16[2,2,1,1,1,96,768]{6,5,4,3,2,1,0:T(8,128)(2,1)S(1)}, bf16[2,2,1,1,1,96,768]{6,5,4,3,2,1,0:T(8,128)(2,1)S(1)}, u32[]{:S(2)}, u32[]{:S(2)}) collective-permute-start(bf16[2,2,1,1,1,96,768]{6,5,4,3,2,1,0:T(8,128)(2,1)S(1)} %pad_maximum_fusion.28), channel_id=1, source_target_pairs={{0,4},{4,0},{8,12},{12,8},{16,20},{20,16},{24,28},{28,24},{1,5},{5... | collective-permute-start | bytes 1769480 | tf_op jit(solution)/shard_map/ppermute | solution.py:26
  76.5 24.4 %collective-permute-start.10 = (bf16[2,2,1,1,1,24,3072]{6,5,4,3,2,1,0:T(8,128)(2,1)S(1)}, bf16[2,2,1,1,1,24,3072]{6,5,4,3,2,1,0:T(8,128)(2,1)S(1)}, u32[]{:S(2)}, u32[]{:S(2)}) collective-permute-start(bf16[2,2,1,1,1,24,3072]{6,5,4,3,2,1,0:T(8,128)(2,1)S(1)} %pad_maximum_fusion.27), channel_id=1, source_target_pairs={{0,2},{1,3},{2,0},{3,1},{4,6},{5,7},{6,4},{7,5},{8,10},{9,11},{10,... | collective-permute-start | bytes 1769480 | tf_op jit(solution)/shard_map/ppermute | solution.py:26
  82.9 22.5 %collective-permute-start.28 = (bf16[2,2,1,1,1,24,3072]{6,5,4,3,2,1,0:T(8,128)(2,1)S(1)}, bf16[2,2,1,1,1,24,3072]{6,5,4,3,2,1,0:T(8,128)(2,1)S(1)}, u32[]{:S(2)}, u32[]{:S(2)}) collective-permute-start(bf16[2,2,1,1,1,24,3072]{6,5,4,3,2,1,0:T(8,128)(2,1)S(1)} %pad_maximum_fusion.30), channel_id=1, source_target_pairs={{0,2},{1,3},{2,0},{3,1},{4,6},{5,7},{6,4},{7,5},{8,10},{9,11},{10,... | collective-permute-start | bytes 1769480 | tf_op jit(solution)/shard_map/ppermute | solution.py:26
  84.6 27.7 %collective-permute-start.2 = (bf16[2,2,1,1,1,24,3200]{6,5,4,3,2,1,0:T(8,128)(2,1)S(1)}, bf16[2,2,1,1,1,24,3200]{6,5,4,3,2,1,0:T(8,128)(2,1)S(1)}, u32[]{:S(2)}, u32[]{:S(2)}) collective-permute-start(bf16[2,2,1,1,1,24,3200]{6,5,4,3,2,1,0:T(8,128)(2,1)S(1)} %pad_maximum_fusion.26), channel_id=1, source_target_pairs={{0,4},{4,0},{8,12},{12,8},{16,20},{20,16},{24,28},{28,24},{1,5},{5... | collective-permute-start | bytes 1843208 | tf_op jit(solution)/shard_map/ppermute | solution.py:26
  86.5 44.2 %collective-permute-start.34 = (bf16[2,2,2,1,1,96,768]{6,5,4,3,2,1,0:T(8,128)(2,1)S(1)}, bf16[2,2,2,1,1,96,768]{6,5,4,3,2,1,0:T(8,128)(2,1)S(1)}, u32[]{:S(2)}, u32[]{:S(2)}) collective-permute-start(bf16[2,2,2,1,1,96,768]{6,5,4,3,2,1,0:T(8,128)(2,1)S(1)} %pad_maximum_fusion.19), channel_id=1, source_target_pairs={{0,2},{1,3},{2,0},{3,1},{4,6},{5,7},{6,4},{7,5},{8,10},{9,11},{10,... | collective-permute-start | bytes 3538952 | tf_op jit(solution)/shard_map/ppermute | solution.py:26
  99.1 56.8 %collective-permute-start.21 = (bf16[2,2,2,1,1,24,3072]{6,5,4,3,2,1,0:T(8,128)(2,1)S(1)}, bf16[2,2,2,1,1,24,3072]{6,5,4,3,2,1,0:T(8,128)(2,1)S(1)}, u32[]{:S(2)}, u32[]{:S(2)}) collective-permute-start(bf16[2,2,2,1,1,24,3072]{6,5,4,3,2,1,0:T(8,128)(2,1)S(1)} %pad_maximum_fusion.17), channel_id=1, source_target_pairs={{0,2},{1,3},{2,0},{3,1},{4,6},{5,7},{6,4},{7,5},{8,10},{9,11},{10,... | collective-permute-start | bytes 3538952 | tf_op jit(solution)/shard_map/ppermute | solution.py:26
  100.9 80.3 %collective-permute-start.16 = (bf16[2,2,2,1,1,96,768]{6,5,4,3,2,1,0:T(8,128)(2,1)S(1)}, bf16[2,2,2,1,1,96,768]{6,5,4,3,2,1,0:T(8,128)(2,1)S(1)}, u32[]{:S(2)}, u32[]{:S(2)}) collective-permute-start(bf16[2,2,2,1,1,96,768]{6,5,4,3,2,1,0:T(8,128)(2,1)S(1)} %pad_maximum_fusion.16), channel_id=1, source_target_pairs={{0,2},{1,3},{2,0},{3,1},{4,6},{5,7},{6,4},{7,5},{8,10},{9,11},{10,... | collective-permute-start | bytes 3538952 | tf_op jit(solution)/shard_map/ppermute | solution.py:26
  105.4 76.2 %collective-permute-start.11 = (bf16[2,2,1,2,1,24,3072]{6,5,4,3,2,1,0:T(8,128)(2,1)S(1)}, bf16[2,2,1,2,1,24,3072]{6,5,4,3,2,1,0:T(8,128)(2,1)S(1)}, u32[]{:S(2)}, u32[]{:S(2)}) collective-permute-start(bf16[2,2,1,2,1,24,3072]{6,5,4,3,2,1,0:T(8,128)(2,1)S(1)} %pad_maximum_fusion.15), channel_id=1, source_target_pairs={{0,4},{4,0},{8,12},{12,8},{16,20},{20,16},{24,28},{28,24},{1,5},{5... | collective-permute-start | bytes 3538952 | tf_op jit(solution)/shard_map/ppermute | solution.py:26
  112.3 70.3 %collective-permute-start.29 = (bf16[2,2,1,2,1,24,3072]{6,5,4,3,2,1,0:T(8,128)(2,1)S(1)}, bf16[2,2,1,2,1,24,3072]{6,5,4,3,2,1,0:T(8,128)(2,1)S(1)}, u32[]{:S(2)}, u32[]{:S(2)}) collective-permute-start(bf16[2,2,1,2,1,24,3072]{6,5,4,3,2,1,0:T(8,128)(2,1)S(1)} %pad_maximum_fusion.18), channel_id=1, source_target_pairs={{0,4},{4,0},{8,12},{12,8},{16,20},{20,16},{24,28},{28,24},{1,5},{5... | collective-permute-start | bytes 3538952 | tf_op jit(solution)/shard_map/ppermute | solution.py:26
  130.7 75.9 %collective-permute-start.3 = (bf16[2,2,2,1,1,24,3200]{6,5,4,3,2,1,0:T(8,128)(2,1)S(1)}, bf16[2,2,2,1,1,24,3200]{6,5,4,3,2,1,0:T(8,128)(2,1)S(1)}, u32[]{:S(2)}, u32[]{:S(2)}) collective-permute-start(bf16[2,2,2,1,1,24,3200]{6,5,4,3,2,1,0:T(8,128)(2,1)S(1)} %pad_maximum_fusion.14), channel_id=1, source_target_pairs={{0,2},{1,3},{2,0},{3,1},{4,6},{5,7},{6,4},{7,5},{8,10},{9,11},{10,... | collective-permute-start | bytes 3686408 | tf_op jit(solution)/shard_map/ppermute | solution.py:26
  156.0 124.9 %collective-permute-start.35 = (bf16[2,2,2,2,1,96,768]{6,5,4,3,2,1,0:T(8,128)(2,1)}, bf16[2,2,2,2,1,96,768]{6,5,4,3,2,1,0:T(8,128)(2,1)}, u32[]{:S(2)}, u32[]{:S(2)}) collective-permute-start(bf16[2,2,2,2,1,96,768]{6,5,4,3,2,1,0:T(8,128)(2,1)} %pad_maximum_fusion.13), channel_id=1, source_target_pairs={{0,1},{1,0},{2,3},{3,2},{4,5},{5,4},{6,7},{7,6},{8,9},{9,8},{10,11... | collective-permute-start | bytes 7077896 | tf_op jit(solution)/shard_map/ppermute | solution.py:26
  181.2 25.9 %collective-permute-start.22 = (bf16[2,2,2,2,1,24,3072]{6,5,4,3,2,1,0:T(8,128)(2,1)S(1)}, bf16[2,2,2,2,1,24,3072]{6,5,4,3,2,1,0:T(8,128)(2,1)S(1)}, u32[]{:S(2)}, u32[]{:S(2)}) collective-permute-start(bf16[2,2,2,2,1,24,3072]{6,5,4,3,2,1,0:T(8,128)(2,1)S(1)} %pad_maximum_fusion.11), channel_id=1, source_target_pairs={{0,1},{1,0},{2,3},{3,2},{4,5},{5,4},{6,7},{7,6},{8,9},{9,8},{10,11... | collective-permute-start | bytes 7077896 | tf_op jit(solution)/shard_map/ppermute | solution.py:26
  181.6 33.5 %collective-permute-start.17 = (bf16[2,2,2,2,1,96,768]{6,5,4,3,2,1,0:T(8,128)(2,1)S(1)}, bf16[2,2,2,2,1,96,768]{6,5,4,3,2,1,0:T(8,128)(2,1)S(1)}, u32[]{:S(2)}, u32[]{:S(2)}) collective-permute-start(bf16[2,2,2,2,1,96,768]{6,5,4,3,2,1,0:T(8,128)(2,1)S(1)} %pad_maximum_fusion.10), channel_id=1, source_target_pairs={{0,1},{1,0},{2,3},{3,2},{4,5},{5,4},{6,7},{7,6},{8,9},{9,8},{10,11... | collective-permute-start | bytes 7077896 | tf_op jit(solution)/shard_map/ppermute | solution.py:26
  182.6 28.0 %collective-permute-start.12 = (bf16[2,2,2,2,1,24,3072]{6,5,4,3,2,1,0:T(8,128)(2,1)S(1)}, bf16[2,2,2,2,1,24,3072]{6,5,4,3,2,1,0:T(8,128)(2,1)}, u32[]{:S(2)}, u32[]{:S(2)}) collective-permute-start(bf16[2,2,2,2,1,24,3072]{6,5,4,3,2,1,0:T(8,128)(2,1)S(1)} %pad_maximum_fusion.9), channel_id=1, source_target_pairs={{0,1},{1,0},{2,3},{3,2},{4,5},{5,4},{6,7},{7,6},{8,9},{9,8},{10,11... | collective-permute-start | bytes 7077896 | tf_op jit(solution)/shard_map/ppermute | solution.py:26
  206.6 19.4 %collective-permute-start.30 = (bf16[2,2,2,2,1,24,3072]{6,5,4,3,2,1,0:T(8,128)(2,1)}, bf16[2,2,2,2,1,24,3072]{6,5,4,3,2,1,0:T(8,128)(2,1)}, u32[]{:S(2)}, u32[]{:S(2)}) collective-permute-start(bf16[2,2,2,2,1,24,3072]{6,5,4,3,2,1,0:T(8,128)(2,1)} %pad_maximum_fusion.12), channel_id=1, source_target_pairs={{0,1},{1,0},{2,3},{3,2},{4,5},{5,4},{6,7},{7,6},{8,9},{9,8},{10,11... | collective-permute-start | bytes 7077896 | tf_op jit(solution)/shard_map/ppermute | solution.py:26
  224.3 19.5 %collective-permute-start.6 = (bf16[2,128,1536]{2,1,0:T(8,128)(2,1)S(1)}, bf16[2,128,1536]{2,1,0:T(8,128)(2,1)S(1)}, u32[]{:S(2)}, u32[]{:S(2)}) collective-permute-start(bf16[2,128,1536]{2,1,0:T(8,128)(2,1)S(1)} %bitcast.195), channel_id=1, source_target_pairs={{0,2},{1,3},{2,0},{3,1},{4,6},{5,7},{6,4},{7,5},{8,10},{9,11},{10,... | collective-permute-start | bytes 2359304 | tf_op jit(solution)/shard_map/ppermute | solution.py:26
  230.4 22.1 %collective-permute-start.5 = (bf16[2,128,1536]{2,1,0:T(8,128)(2,1)S(1)}, bf16[2,128,1536]{2,1,0:T(8,128)(2,1)S(1)}, u32[]{:S(2)}, u32[]{:S(2)}) collective-permute-start(bf16[2,128,1536]{2,1,0:T(8,128)(2,1)S(1)} %bitcast.196), channel_id=1, source_target_pairs={{0,1},{1,0},{2,3},{3,2},{4,5},{5,4},{6,7},{7,6},{8,9},{9,8},{10,11... | collective-permute-start | bytes 2359304 | tf_op jit(solution)/shard_map/ppermute | solution.py:26
  279.3 20.0 %collective-permute-start.24 = (bf16[2,128,1536]{2,1,0:T(8,128)(2,1)S(1)}, bf16[2,128,1536]{2,1,0:T(8,128)(2,1)S(1)}, u32[]{:S(2)}, u32[]{:S(2)}) collective-permute-start(bf16[2,128,1536]{2,1,0:T(8,128)(2,1)S(1)} %bitcast.201), channel_id=1, source_target_pairs={{0,2},{1,3},{2,0},{3,1},{4,6},{5,7},{6,4},{7,5},{8,10},{9,11},{10,... | collective-permute-start | bytes 2359304 | tf_op jit(solution)/shard_map/ppermute | solution.py:26
  285.5 24.9 %collective-permute-start.23 = (bf16[2,128,1536]{2,1,0:T(8,128)(2,1)S(1)}, bf16[2,128,1536]{2,1,0:T(8,128)(2,1)S(1)}, u32[]{:S(2)}, u32[]{:S(2)}) collective-permute-start(bf16[2,128,1536]{2,1,0:T(8,128)(2,1)S(1)} %bitcast.202), channel_id=1, source_target_pairs={{0,1},{1,0},{2,3},{3,2},{4,5},{5,4},{6,7},{7,6},{8,9},{9,8},{10,11... | collective-permute-start | bytes 2359304 | tf_op jit(solution)/shard_map/ppermute | solution.py:26
  299.3 11.1 %collective-permute-start.25 = (bf16[2,128,1536]{2,1,0:T(8,128)(2,1)S(1)}, bf16[2,128,1536]{2,1,0:T(8,128)(2,1)S(1)}, u32[]{:S(2)}, u32[]{:S(2)}) collective-permute-start(bf16[2,128,1536]{2,1,0:T(8,128)(2,1)S(1)} %collective-permute-done.24.rest_2_.rest_6_), channel_id=1, source_target_pairs={{0,1},{1,0},{2,3},{3,2},{4,5},{5,4},{6,7},{7,6},{8,9},{9,8},{10,11... | collective-permute-start | bytes 2359304 | tf_op jit(solution)/shard_map/ppermute | solution.py:26
  359.6 28.5 %collective-permute-start.36 = (bf16[2,2,128,768]{3,2,1,0:T(8,128)(2,1)}, bf16[2,2,128,768]{3,2,1,0:T(8,128)(2,1)}, u32[]{:S(2)}, u32[]{:S(2)}) collective-permute-start(bf16[2,2,128,768]{3,2,1,0:T(8,128)(2,1)} %pad_maximum_fusion.22), channel_id=1, source_target_pairs={{0,1},{1,0},{2,3},{3,2},{4,5},{5,4},{6,7},{7,6},{8,9},{9,8},{10,11... | collective-permute-start | bytes 2359304 | tf_op jit(solution)/shard_map/ppermute | solution.py:26
  361.0 18.1 %collective-permute-start.37 = (bf16[2,2,128,768]{3,2,1,0:T(8,128)(2,1)}, bf16[2,2,128,768]{3,2,1,0:T(8,128)(2,1)}, u32[]{:S(2)}, u32[]{:S(2)}) collective-permute-start(bf16[2,2,128,768]{3,2,1,0:T(8,128)(2,1)} %pad_maximum_fusion.23), channel_id=1, source_target_pairs={{0,1},{1,0},{2,3},{3,2},{4,5},{5,4},{6,7},{7,6},{8,9},{9,8},{10,11... | collective-permute-start | bytes 2359304 | tf_op jit(solution)/shard_map/ppermute | solution.py:26
  381.1 20.0 %collective-permute-start.38 = (bf16[2,2,128,768]{3,2,1,0:T(8,128)(2,1)S(1)}, bf16[2,2,128,768]{3,2,1,0:T(8,128)(2,1)S(1)}, u32[]{:S(2)}, u32[]{:S(2)}) collective-permute-start(bf16[2,2,128,768]{3,2,1,0:T(8,128)(2,1)S(1)} %add_convert_fusion.16), channel_id=1, source_target_pairs={{0,2},{1,3},{2,0},{3,1},{4,6},{5,7},{6,4},{7,5},{8,10},{9,11},{10,... | collective-permute-start | bytes 2359304 | tf_op jit(solution)/shard_map/ppermute | solution.py:26
  384.3 78.5 %collective-permute-start.67 = (bf16[2,2,2,2,1,96,768]{6,5,4,3,2,1,0:T(8,128)(2,1)}, bf16[2,2,2,2,1,96,768]{6,5,4,3,2,1,0:T(8,128)(2,1)}, u32[]{:S(2)}, u32[]{:S(2)}) collective-permute-start(bf16[2,2,2,2,1,96,768]{6,5,4,3,2,1,0:T(8,128)(2,1)} %constant_dynamic-slice_fusion.4), channel_id=1, source_target_pairs={{0,1},{1,0},{2,3},{3,2},{4,5},{5,4},{6,7},{7,6},{8,9},{9,8},{10,11... | collective-permute-start | bytes 7077896 | tf_op jit(solution)/shard_map/ppermute | solution.py:26
  386.2 71.9 %collective-permute-start.57 = (bf16[2,2,2,2,1,24,3072]{6,5,4,3,2,1,0:T(8,128)(2,1)}, bf16[2,2,2,2,1,24,3072]{6,5,4,3,2,1,0:T(8,128)(2,1)}, u32[]{:S(2)}, u32[]{:S(2)}) collective-permute-start(bf16[2,2,2,2,1,24,3072]{6,5,4,3,2,1,0:T(8,128)(2,1)} %constant_dynamic-slice_fusion.14), channel_id=1, source_target_pairs={{0,1},{1,0},{2,3},{3,2},{4,5},{5,4},{6,7},{7,6},{8,9},{9,8},{10,11... | collective-permute-start | bytes 7077896 | tf_op jit(solution)/shard_map/ppermute | solution.py:26
  437.0 32.1 %collective-permute-start.39 = (bf16[2,2,128,768]{3,2,1,0:T(8,128)(2,1)}, bf16[2,2,128,768]{3,2,1,0:T(8,128)(2,1)}, u32[]{:S(2)}, u32[]{:S(2)}) collective-permute-start(bf16[2,2,128,768]{3,2,1,0:T(8,128)(2,1)} %pad_maximum_fusion.24), channel_id=1, source_target_pairs={{0,1},{1,0},{2,3},{3,2},{4,5},{5,4},{6,7},{7,6},{8,9},{9,8},{10,11... | collective-permute-start | bytes 2359304 | tf_op jit(solution)/shard_map/ppermute | solution.py:26
  438.0 23.2 %collective-permute-start.40 = (bf16[2,2,128,768]{3,2,1,0:T(8,128)(2,1)}, bf16[2,2,128,768]{3,2,1,0:T(8,128)(2,1)}, u32[]{:S(2)}, u32[]{:S(2)}) collective-permute-start(bf16[2,2,128,768]{3,2,1,0:T(8,128)(2,1)} %pad_maximum_fusion.25), channel_id=1, source_target_pairs={{0,1},{1,0},{2,3},{3,2},{4,5},{5,4},{6,7},{7,6},{8,9},{9,8},{10,11... | collective-permute-start | bytes 2359304 | tf_op jit(solution)/shard_map/ppermute | solution.py:26
  450.5 65.2 %collective-permute-start.62 = (bf16[2,2,2,2,1,96,768]{6,5,4,3,2,1,0:T(8,128)(2,1)}, bf16[2,2,2,2,1,96,768]{6,5,4,3,2,1,0:T(8,128)(2,1)}, u32[]{:S(2)}, u32[]{:S(2)}) collective-permute-start(bf16[2,2,2,2,1,96,768]{6,5,4,3,2,1,0:T(8,128)(2,1)} %constant_dynamic-slice_fusion.9), channel_id=1, source_target_pairs={{0,1},{1,0},{2,3},{3,2},{4,5},{5,4},{6,7},{7,6},{8,9},{9,8},{10,11... | collective-permute-start | bytes 7077896 | tf_op jit(solution)/shard_map/ppermute | solution.py:26
  458.1 61.7 %collective-permute-start.52 = (bf16[2,2,2,2,1,24,3072]{6,5,4,3,2,1,0:T(8,128)(2,1)}, bf16[2,2,2,2,1,24,3072]{6,5,4,3,2,1,0:T(8,128)(2,1)}, u32[]{:S(2)}, u32[]{:S(2)}) collective-permute-start(bf16[2,2,2,2,1,24,3072]{6,5,4,3,2,1,0:T(8,128)(2,1)} %constant_dynamic-slice_fusion.19), channel_id=1, source_target_pairs={{0,1},{1,0},{2,3},{3,2},{4,5},{5,4},{6,7},{7,6},{8,9},{9,8},{10,11... | collective-permute-start | bytes 7077896 | tf_op jit(solution)/shard_map/ppermute | solution.py:26
  461.2 62.5 %collective-permute-start.47 = (bf16[2,2,2,2,1,24,3072]{6,5,4,3,2,1,0:T(8,128)(2,1)}, bf16[2,2,2,2,1,24,3072]{6,5,4,3,2,1,0:T(8,128)(2,1)}, u32[]{:S(2)}, u32[]{:S(2)}) collective-permute-start(bf16[2,2,2,2,1,24,3072]{6,5,4,3,2,1,0:T(8,128)(2,1)} %constant_dynamic-slice_fusion.24), channel_id=1, source_target_pairs={{0,1},{1,0},{2,3},{3,2},{4,5},{5,4},{6,7},{7,6},{8,9},{9,8},{10,11... | collective-permute-start | bytes 7077896 | tf_op jit(solution)/shard_map/ppermute | solution.py:26
  462.9 20.4 %collective-permute-start.41 = (bf16[2,2,128,768]{3,2,1,0:T(8,128)(2,1)S(1)}, bf16[2,2,128,768]{3,2,1,0:T(8,128)(2,1)S(1)}, u32[]{:S(2)}, u32[]{:S(2)}) collective-permute-start(bf16[2,2,128,768]{3,2,1,0:T(8,128)(2,1)S(1)} %add_convert_fusion.13), channel_id=1, source_target_pairs={{0,2},{1,3},{2,0},{3,1},{4,6},{5,7},{6,4},{7,5},{8,10},{9,11},{10,... | collective-permute-start | bytes 2359304 | tf_op jit(solution)/shard_map/ppermute | solution.py:26
  469.1 42.7 %collective-permute-start.68 = (bf16[2,2,2,1,1,96,768]{6,5,4,3,2,1,0:T(8,128)(2,1)}, bf16[2,2,2,1,1,96,768]{6,5,4,3,2,1,0:T(8,128)(2,1)}, u32[]{:S(2)}, u32[]{:S(2)}) collective-permute-start(bf16[2,2,2,1,1,96,768]{6,5,4,3,2,1,0:T(8,128)(2,1)} %constant_dynamic-slice_fusion.3), channel_id=1, source_target_pairs={{0,2},{1,3},{2,0},{3,1},{4,6},{5,7},{6,4},{7,5},{8,10},{9,11},{10,... | collective-permute-start | bytes 3538952 | tf_op jit(solution)/shard_map/ppermute | solution.py:26
  483.3 30.1 %collective-permute-start.58 = (bf16[2,2,1,2,1,24,3072]{6,5,4,3,2,1,0:T(8,128)(2,1)}, bf16[2,2,1,2,1,24,3072]{6,5,4,3,2,1,0:T(8,128)(2,1)}, u32[]{:S(2)}, u32[]{:S(2)}) collective-permute-start(bf16[2,2,1,2,1,24,3072]{6,5,4,3,2,1,0:T(8,128)(2,1)} %constant_dynamic-slice_fusion.13), channel_id=1, source_target_pairs={{0,4},{4,0},{8,12},{12,8},{16,20},{20,16},{24,28},{28,24},{1,5},{5... | collective-permute-start | bytes 3538952 | tf_op jit(solution)/shard_map/ppermute | solution.py:26
  511.8 72.8 %collective-permute-start.42 = (bf16[2,2,2,2,1,24,3200]{6,5,4,3,2,1,0:T(8,128)(2,1)S(1)}, bf16[2,2,2,2,1,24,3200]{6,5,4,3,2,1,0:T(8,128)(2,1)S(1)}, u32[]{:S(2)}, u32[]{:S(2)}) collective-permute-start(bf16[2,2,2,2,1,24,3200]{6,5,4,3,2,1,0:T(8,128)(2,1)S(1)} %constant_dynamic-slice_fusion.29), channel_id=1, source_target_pairs={{0,1},{1,0},{2,3},{3,2},{4,5},{5,4},{6,7},{7,6},{8,9},{9,8},{10,11... | collective-permute-start | bytes 7372808 | tf_op jit(solution)/shard_map/ppermute | solution.py:26
  513.4 16.2 %collective-permute-start.69 = (bf16[2,2,1,1,1,96,768]{6,5,4,3,2,1,0:T(8,128)(2,1)S(1)}, bf16[2,2,1,1,1,96,768]{6,5,4,3,2,1,0:T(8,128)(2,1)S(1)}, u32[]{:S(2)}, u32[]{:S(2)}) collective-permute-start(bf16[2,2,1,1,1,96,768]{6,5,4,3,2,1,0:T(8,128)(2,1)S(1)} %constant_dynamic-slice_fusion.2), channel_id=1, source_target_pairs={{0,4},{4,0},{8,12},{12,8},{16,20},{20,16},{24,28},{28,24},{1,5},{5... | collective-permute-start | bytes 1769480 | tf_op jit(solution)/shard_map/ppermute | solution.py:26
  515.7 16.2 %collective-permute-start.59 = (bf16[2,2,1,1,1,24,3072]{6,5,4,3,2,1,0:T(8,128)(2,1)S(1)}, bf16[2,2,1,1,1,24,3072]{6,5,4,3,2,1,0:T(8,128)(2,1)S(1)}, u32[]{:S(2)}, u32[]{:S(2)}) collective-permute-start(bf16[2,2,1,1,1,24,3072]{6,5,4,3,2,1,0:T(8,128)(2,1)S(1)} %constant_dynamic-slice_fusion.12), channel_id=1, source_target_pairs={{0,2},{1,3},{2,0},{3,1},{4,6},{5,7},{6,4},{7,5},{8,10},{9,11},{10,... | collective-permute-start | bytes 1769480 | tf_op jit(solution)/shard_map/ppermute | solution.py:26
  519.8 44.5 %collective-permute-start.63 = (bf16[2,2,2,1,1,96,768]{6,5,4,3,2,1,0:T(8,128)(2,1)S(1)}, bf16[2,2,2,1,1,96,768]{6,5,4,3,2,1,0:T(8,128)(2,1)S(1)}, u32[]{:S(2)}, u32[]{:S(2)}) collective-permute-start(bf16[2,2,2,1,1,96,768]{6,5,4,3,2,1,0:T(8,128)(2,1)S(1)} %constant_dynamic-slice_fusion.8), channel_id=1, source_target_pairs={{0,2},{1,3},{2,0},{3,1},{4,6},{5,7},{6,4},{7,5},{8,10},{9,11},{10,... | collective-permute-start | bytes 3538952 | tf_op jit(solution)/shard_map/ppermute | solution.py:26
  523.8 42.5 %collective-permute-start.53 = (bf16[2,2,1,2,1,24,3072]{6,5,4,3,2,1,0:T(8,128)(2,1)S(1)}, bf16[2,2,1,2,1,24,3072]{6,5,4,3,2,1,0:T(8,128)(2,1)S(1)}, u32[]{:S(2)}, u32[]{:S(2)}) collective-permute-start(bf16[2,2,1,2,1,24,3072]{6,5,4,3,2,1,0:T(8,128)(2,1)S(1)} %constant_dynamic-slice_fusion.18), channel_id=1, source_target_pairs={{0,4},{4,0},{8,12},{12,8},{16,20},{20,16},{24,28},{28,24},{1,5},{5... | collective-permute-start | bytes 3538952 | tf_op jit(solution)/shard_map/ppermute | solution.py:26
  529.6 52.9 %collective-permute-start.48 = (bf16[2,2,2,1,1,24,3072]{6,5,4,3,2,1,0:T(8,128)(2,1)S(1)}, bf16[2,2,2,1,1,24,3072]{6,5,4,3,2,1,0:T(8,128)(2,1)S(1)}, u32[]{:S(2)}, u32[]{:S(2)}) collective-permute-start(bf16[2,2,2,1,1,24,3072]{6,5,4,3,2,1,0:T(8,128)(2,1)S(1)} %constant_dynamic-slice_fusion.23), channel_id=1, source_target_pairs={{0,2},{1,3},{2,0},{3,1},{4,6},{5,7},{6,4},{7,5},{8,10},{9,11},{10,... | collective-permute-start | bytes 3538952 | tf_op jit(solution)/shard_map/ppermute | solution.py:26
  564.7 22.2 %collective-permute-start.64 = (bf16[2,2,1,1,1,96,768]{6,5,4,3,2,1,0:T(8,128)(2,1)S(1)}, bf16[2,2,1,1,1,96,768]{6,5,4,3,2,1,0:T(8,128)(2,1)S(1)}, u32[]{:S(2)}, u32[]{:S(2)}) collective-permute-start(bf16[2,2,1,1,1,96,768]{6,5,4,3,2,1,0:T(8,128)(2,1)S(1)} %constant_dynamic-slice_fusion.7), channel_id=1, source_target_pairs={{0,4},{4,0},{8,12},{12,8},{16,20},{20,16},{24,28},{28,24},{1,5},{5... | collective-permute-start | bytes 1769480 | tf_op jit(solution)/shard_map/ppermute | solution.py:26
  566.7 28.4 %collective-permute-start.54 = (bf16[2,2,1,1,1,24,3072]{6,5,4,3,2,1,0:T(8,128)(2,1)S(1)}, bf16[2,2,1,1,1,24,3072]{6,5,4,3,2,1,0:T(8,128)(2,1)S(1)}, u32[]{:S(2)}, u32[]{:S(2)}) collective-permute-start(bf16[2,2,1,1,1,24,3072]{6,5,4,3,2,1,0:T(8,128)(2,1)S(1)} %constant_dynamic-slice_fusion.17), channel_id=1, source_target_pairs={{0,2},{1,3},{2,0},{3,1},{4,6},{5,7},{6,4},{7,5},{8,10},{9,11},{10,... | collective-permute-start | bytes 1769480 | tf_op jit(solution)/shard_map/ppermute | solution.py:26
  583.0 14.0 %collective-permute-start.49 = (bf16[2,2,1,1,1,24,3072]{6,5,4,3,2,1,0:T(8,128)(2,1)S(1)}, bf16[2,2,1,1,1,24,3072]{6,5,4,3,2,1,0:T(8,128)(2,1)S(1)}, u32[]{:S(2)}, u32[]{:S(2)}) collective-permute-start(bf16[2,2,1,1,1,24,3072]{6,5,4,3,2,1,0:T(8,128)(2,1)S(1)} %constant_dynamic-slice_fusion.22), channel_id=1, source_target_pairs={{0,4},{4,0},{8,12},{12,8},{16,20},{20,16},{24,28},{28,24},{1,5},{5... | collective-permute-start | bytes 1769480 | tf_op jit(solution)/shard_map/ppermute | solution.py:26
  585.3 38.4 %collective-permute-start.43 = (bf16[2,2,2,1,1,24,3200]{6,5,4,3,2,1,0:T(8,128)(2,1)S(1)}, bf16[2,2,2,1,1,24,3200]{6,5,4,3,2,1,0:T(8,128)(2,1)S(1)}, u32[]{:S(2)}, u32[]{:S(2)}) collective-permute-start(bf16[2,2,2,1,1,24,3200]{6,5,4,3,2,1,0:T(8,128)(2,1)S(1)} %constant_dynamic-slice_fusion.28), channel_id=1, source_target_pairs={{0,2},{1,3},{2,0},{3,1},{4,6},{5,7},{6,4},{7,5},{8,10},{9,11},{10,... | collective-permute-start | bytes 3686408 | tf_op jit(solution)/shard_map/ppermute | solution.py:26
  587.0 10.6 %collective-permute-start.65 = (bf16[2,1,1,1,1,96,768]{6,5,4,3,2,1,0:T(8,128)(2,1)S(1)}, bf16[2,1,1,1,1,96,768]{6,5,4,3,2,1,0:T(8,128)(2,1)S(1)}, u32[]{:S(2)}, u32[]{:S(2)}) collective-permute-start(bf16[2,1,1,1,1,96,768]{6,5,4,3,2,1,0:T(8,128)(2,1)S(1)} %constant_dynamic-slice_fusion.6), channel_id=1, source_target_pairs={{0,8},{4,12},{8,0},{12,4},{16,24},{20,28},{24,16},{28,20},{1,9},{5... | collective-permute-start | bytes 884744 | tf_op jit(solution)/shard_map/ppermute | solution.py:26
  595.3 14.8 %collective-permute-start.55 = (bf16[2,1,1,1,1,24,3072]{6,5,4,3,2,1,0:T(8,128)(2,1)S(1)}, bf16[2,1,1,1,1,24,3072]{6,5,4,3,2,1,0:T(8,128)(2,1)S(1)}, u32[]{:S(2)}, u32[]{:S(2)}) collective-permute-start(bf16[2,1,1,1,1,24,3072]{6,5,4,3,2,1,0:T(8,128)(2,1)S(1)} %constant_dynamic-slice_fusion.16), channel_id=1, source_target_pairs={{0,8},{4,12},{8,0},{12,4},{16,24},{20,28},{24,16},{28,20},{1,9},{5... | collective-permute-start | bytes 884744 | tf_op jit(solution)/shard_map/ppermute | solution.py:26
  597.1 16.9 %collective-permute-start.50 = (bf16[2,1,1,1,1,24,3072]{6,5,4,3,2,1,0:T(8,128)(2,1)S(1)}, bf16[2,1,1,1,1,24,3072]{6,5,4,3,2,1,0:T(8,128)(2,1)S(1)}, u32[]{:S(2)}, u32[]{:S(2)}) collective-permute-start(bf16[2,1,1,1,1,24,3072]{6,5,4,3,2,1,0:T(8,128)(2,1)S(1)} %constant_dynamic-slice_fusion.21), channel_id=1, source_target_pairs={{0,8},{4,12},{8,0},{12,4},{16,24},{20,28},{24,16},{28,20},{1,9},{5... | collective-permute-start | bytes 884744 | tf_op jit(solution)/shard_map/ppermute | solution.py:26
  597.8 18.0 %collective-permute-start.66 = (bf16[1,1,1,1,1,96,768]{6,5,4,3,2,1,0:T(8,128)(2,1)S(1)}, bf16[1,1,1,1,1,96,768]{6,5,4,3,2,1,0:T(8,128)(2,1)S(1)}, u32[]{:S(2)}, u32[]{:S(2)}) collective-permute-start(bf16[1,1,1,1,1,96,768]{6,5,4,3,2,1,0:T(8,128)(2,1)S(1)} %constant_dynamic-slice_fusion.5), channel_id=1, source_target_pairs={{0,16},{4,20},{8,24},{12,28},{16,0},{20,4},{24,8},{28,12},{1,17},{... | collective-permute-start | bytes 442376 | tf_op jit(solution)/shard_map/ppermute | solution.py:26
  610.2 13.5 %collective-permute-start.56 = (bf16[1,1,1,1,1,24,3072]{6,5,4,3,2,1,0:T(8,128)(2,1)S(1)}, bf16[1,1,1,1,1,24,3072]{6,5,4,3,2,1,0:T(8,128)(2,1)S(1)}, u32[]{:S(2)}, u32[]{:S(2)}) collective-permute-start(bf16[1,1,1,1,1,24,3072]{6,5,4,3,2,1,0:T(8,128)(2,1)S(1)} %constant_dynamic-slice_fusion.15), channel_id=1, source_target_pairs={{0,16},{4,20},{8,24},{12,28},{16,0},{20,4},{24,8},{28,12},{1,17},{... | collective-permute-start | bytes 442376 | tf_op jit(solution)/shard_map/ppermute | solution.py:26
  614.2 11.5 %collective-permute-start.51 = (bf16[1,1,1,1,1,24,3072]{6,5,4,3,2,1,0:T(8,128)(2,1)S(1)}, bf16[1,1,1,1,1,24,3072]{6,5,4,3,2,1,0:T(8,128)(2,1)S(1)}, u32[]{:S(2)}, u32[]{:S(2)}) collective-permute-start(bf16[1,1,1,1,1,24,3072]{6,5,4,3,2,1,0:T(8,128)(2,1)S(1)} %constant_dynamic-slice_fusion.20), channel_id=1, source_target_pairs={{0,16},{4,20},{8,24},{12,28},{16,0},{20,4},{24,8},{28,12},{1,17},{... | collective-permute-start | bytes 442376 | tf_op jit(solution)/shard_map/ppermute | solution.py:26
  624.1 12.3 %collective-permute-start.44 = (bf16[2,2,1,1,1,24,3200]{6,5,4,3,2,1,0:T(8,128)(2,1)S(1)}, bf16[2,2,1,1,1,24,3200]{6,5,4,3,2,1,0:T(8,128)(2,1)S(1)}, u32[]{:S(2)}, u32[]{:S(2)}) collective-permute-start(bf16[2,2,1,1,1,24,3200]{6,5,4,3,2,1,0:T(8,128)(2,1)S(1)} %constant_dynamic-slice_fusion.27), channel_id=1, source_target_pairs={{0,4},{4,0},{8,12},{12,8},{16,20},{20,16},{24,28},{28,24},{1,5},{5... | collective-permute-start | bytes 1843208 | tf_op jit(solution)/shard_map/ppermute | solution.py:26
  (126 other events, 798.1 us)

commit v2 on v1

v2 whole, which is shorter than its diff:
```python
import functools
import heapq

import jax
import jax.numpy as jnp
from jax import lax
from jax.experimental import pallas as pl
from jax.experimental.pallas import tpu as pltpu
import numpy as np
from jax.sharding import PartitionSpec as P

D = 768
HEADS = 12
HD = 64
FF = 3072
LAYERS = 2
PAD = 128
HALF = D // 2
LOW = jnp.bfloat16
FULL = jnp.float32


def bits_of(name):
    return lax.axis_size(name).bit_length() - 1


def swap(value, name, bit):
    pairs = [(i, i ^ (1 << bit)) for i in range(lax.axis_size(name))]
    return lax.ppermute(value, name, pairs)


def swap_core(value):
    return swap(value, "narrow", 0)


def own_bit(name, bit):
    return (lax.axis_index(name) >> bit) & 1


def core_low():
    return own_bit("narrow", 0) == 0


def axis_of(name, bit):
    if name == "wide":
        return bits_of("wide") - 1 - bit
    return bits_of("wide")


def order(first):
    far = [("wide", bit) for bit in range(bits_of("wide") - 1, 0, -1)]
    middle = [("wide", 0), ("narrow", 1)]
    if first == "narrow":
        middle.reverse()
    return far + middle


def flip(values):
    half = values.shape[-1] // 2
    turned = jnp.concatenate([values[..., half:], values[..., :half]], axis=-1)
    return jnp.where(core_low(), values, turned)


def link_of(name, bit):
    if name == "narrow":
        return "x"
    return "y" if bit == 0 else "z"


RATE = 40e3
BACK_RATE = 12e3
CORE_RATE = 500e3
COPY_RATE = 1.0e6
START = 1.5
STEP = 0.8


class Gather:
    def __init__(self, shard, first, rank):
        self.stages = order(first) + [("core", 0)]
        lead = bits_of("wide") + 1
        self.held = shard.reshape((1,) * lead + shard.shape)
        self.rank = rank
        self.done = False

    def link(self, k):
        name, bit = self.stages[k]
        return "core" if name == "core" else link_of(name, bit)

    def time(self, k):
        name, bit = self.stages[k]
        size = self.held.size * 2
        if name == "core":
            return size / CORE_RATE
        return size / RATE * (2 if name == "wide" and bit > 1 else 1)

    def operand(self, k):
        if self.stages[k][0] == "core":
            self.held = self.held.reshape(-1, self.held.shape[-1])
        return self.held

    def send(self, k, value):
        self.held = value
        name, bit = self.stages[k]
        return swap_core(value) if name == "core" else swap(value, name, bit)

    def finish(self, k, other):
        name, bit = self.stages[k]
        if name == "core":
            self.mine, self.other = self.held, other
            self.done = True
            return 0.0
        axis = axis_of(name, bit)
        shape = self.held.shape[:axis] + (2,) + self.held.shape[axis + 1 :]
        place = lax.broadcasted_iota(jnp.int32, shape, axis)
        self.held = jnp.where(place == own_bit(name, bit), self.held, other)
        return STEP + self.held.size * 4 / COPY_RATE


class Scatter:
    def __init__(self, sent, kept, first, rank, groups=1):
        self.groups = groups
        self.stages = [("core", 0)] + order(first)[::-1]
        self.sent, self.kept = sent, kept
        self.rank = rank
        self.done = False

    def link(self, k):
        name, bit = self.stages[k]
        return "core" if name == "core" else link_of(name, bit)

    def time(self, k):
        name, bit = self.stages[k]
        size = self.sent.size * 2
        if name == "core":
            return size / CORE_RATE
        return size / BACK_RATE * (2 if name == "wide" and bit > 1 else 1)

    def operand(self, k):
        return self.sent

    def send(self, k, value):
        name, bit = self.stages[k]
        return swap_core(value) if name == "core" else swap(value, name, bit)

    def finish(self, k, other):
        cost = 2 * STEP + other.size * 6 / COPY_RATE
        if k == 0:
            self.kept = self.kept()
            cost += STEP + other.size * 2 / COPY_RATE
            chips = lax.axis_size("wide") * lax.axis_size("narrow") // 2
            shape = (self.groups,) + (2,) * (bits_of("wide") + 1)
            shape += (other.shape[0] // (chips * self.groups), other.shape[1])
            self.kept, other = self.kept.reshape(shape), other.reshape(shape)
        if k + 1 == len(self.stages):
            total = self.kept.astype(FULL) + other.astype(FULL)
            self.result = total.astype(LOW).reshape(-1, *total.shape[-2:])
            self.done = True
            return cost
        name, bit = self.stages[k + 1]
        axis, mine = 1 + axis_of(name, bit), own_bit(name, bit)

        def part(which):
            cut = [lax.dynamic_index_in_dim(value, which, axis) for value in (self.kept, other)]
            return (cut[0].astype(FULL) + cut[1].astype(FULL)).astype(LOW)

        self.sent, self.kept = part(1 - mine), part(mine)
        return cost


class Exchange:
    def __init__(self, value, bit, rank):
        self.value, self.bit, self.rank = value, bit, rank
        self.done = False

    def link(self, k):
        return "core" if self.bit == 0 else "x"

    def time(self, k):
        return self.value.size * 2 / (CORE_RATE if self.bit == 0 else RATE)

    def operand(self, k):
        return self.value

    def send(self, k, value):
        self.value = value
        return swap(value, "narrow", self.bit)

    def finish(self, k, other):
        self.other = other
        self.done = True
        return 0.0


class Pump:
    def __init__(self, depth=2):
        self.now = 0.0
        self.depth = depth
        self.flying = []
        self.links = {}
        self.count = 0
        self.last = None
        self.sent = None
        self.value = None

    def add(self, stream):
        self.request(stream, 0)

    def request(self, stream, k):
        link = self.links.setdefault(stream.link(k), [0, 0.0, []])
        if link[0] < self.depth:
            self.issue(stream, k, link)
        else:
            self.count += 1
            heapq.heappush(link[2], (stream.rank, self.count, stream, k))

    def issue(self, stream, k, link):
        operand = stream.operand(k)
        for other in (self.last, self.sent):
            if other is not None:
                operand, _ = lax.optimization_barrier((operand, other))
        self.sent = operand
        if self.value is not None:
            operand, self.value = lax.optimization_barrier((operand, self.value))
        link[0] += 1
        self.now += 0.3 if stream.link(k) == "core" else START
        end = max(self.now, link[1]) + stream.time(k) + 0.7
        link[1] = end - 0.7
        other = stream.send(k, operand)
        if stream.link(k) == "core":
            self.sent = other
        self.count += 1
        heapq.heappush(self.flying, (end, self.count, stream, k, other))

    def step(self):
        end, _, stream, k, other = heapq.heappop(self.flying)
        self.now = max(self.now, end)
        link = self.links[stream.link(k)]
        link[0] -= 1
        self.last = other
        self.now += stream.finish(k, other)
        if not stream.done:
            self.request(stream, k + 1)
        if link[2] and link[0] < self.depth:
            _, _, waiting, j = heapq.heappop(link[2])
            self.issue(waiting, j, link)

    def advance(self, time, value):
        self.value = value
        self.now += time
        while self.flying and self.flying[0][0] <= self.now:
            self.step()
        value, self.value = self.value, None
        return value

    def idle(self, time):
        while self.flying and self.flying[0][0] <= time:
            self.step()
        self.now = max(self.now, time)

    def need(self, streams, value=None):
        self.value = value
        while not all(stream.done for stream in streams):
            self.step()
        value, self.value = self.value, None
        return value


BLOCKS = D // 128


def stack_heads(pair):
    lane = lax.broadcasted_iota(jnp.int32, pair.shape, 1)
    zero = jnp.zeros_like(pair)
    return jnp.concatenate(
        [jnp.where(lane < HD, pair, zero), jnp.where(lane < HD, zero, pair)], axis=0
    )


def pick_heads(stacked):
    rows = stacked.shape[0] // 2
    lane = lax.broadcasted_iota(jnp.int32, (rows, stacked.shape[1]), 1)
    return jnp.where(lane < HD, stacked[:rows], stacked[rows:])


def dot_t(left, right):
    return lax.dot_general(left, right, (((1,), (1,)), ((), ())), preferred_element_type=FULL)


def dot_l(left, right):
    return lax.dot_general(left, right, (((0,), (0,)), ((), ())), preferred_element_type=FULL)


def attend_kernel(meta, query, key_own, value_own, key_other, value_other, mixed, probs):
    length = meta[0]
    stacked = stack_heads(query[...])
    keys = jnp.concatenate([key_own[...], key_other[...]], axis=0)
    scores = dot_t(stacked, keys) * HD**-0.5
    rows = keys.shape[0] // 4
    column = lax.broadcasted_iota(jnp.int32, (1, keys.shape[0]), 1)
    place = column + meta[1]
    for j in range(1, 4):
        place = jnp.where(column >= j * rows, column - j * rows + meta[1 + j], place)
    scores = jnp.where(place < length, scores, -1e30)
    raised = jnp.exp(scores - jnp.max(scores, axis=1, keepdims=True))
    low = (raised / jnp.sum(raised, axis=1, keepdims=True)).astype(LOW)
    probs[0] = low
    values = jnp.concatenate([value_own[...], value_other[...]], axis=0)
    mixed[...] = pick_heads(jnp.dot(low, values, preferred_element_type=FULL)).astype(LOW)


def specs(rows):
    def at(index):
        return pl.BlockSpec((rows, 128), index)

    plain = at(lambda h, *_: (0, h))
    far = at(lambda h, *_: (0, BLOCKS + h))
    probs = pl.BlockSpec((1, 2 * rows, 2 * rows), lambda h, *_: (h, 0, 0))
    return plain, [plain, far, plain, far], probs


def attend(queries, own, other, meta):
    rows, width = queries.shape
    plain, keys, probs = specs(rows)
    return pl.pallas_call(
        attend_kernel,
        grid_spec=pltpu.PrefetchScalarGridSpec(
            num_scalar_prefetch=1,
            grid=(BLOCKS,),
            in_specs=[plain] + keys,
            out_specs=[plain, probs],
        ),
        out_shape=[
            jax.ShapeDtypeStruct(queries.shape, LOW),
            jax.ShapeDtypeStruct((BLOCKS, 2 * rows, 2 * rows), LOW),
        ],
        cost_estimate=pl.CostEstimate(
            flops=BLOCKS * 4 * rows * rows * 512 * 2,
            bytes_accessed=8 * rows * width * 2,
            transcendentals=BLOCKS * 4 * rows * rows,
        ),
    )(meta, queries, own, own, other, other)


def attend_back_kernel(
    query,
    key_own,
    value_own,
    key_other,
    value_other,
    mixed_grad,
    probs,
    query_grad,
    both_grad,
    both_grad_other,
):
    rows = query.shape[0]
    queries = stack_heads(query[...])
    grads = stack_heads(mixed_grad[...])
    low = probs[0]
    keys = jnp.concatenate([key_own[...], key_other[...]], axis=0)
    values = jnp.concatenate([value_own[...], value_other[...]], axis=0)
    prob_grad = dot_t(grads, values)
    wide = low.astype(FULL)
    weighted = jnp.sum(wide * prob_grad, axis=1, keepdims=True)
    score_grad = (wide * (prob_grad - weighted)).astype(LOW)
    query_grad[...] = (
        pick_heads(jnp.dot(score_grad, keys, preferred_element_type=FULL)) * HD**-0.5
    ).astype(LOW)
    key_all = (dot_l(score_grad, queries) * HD**-0.5).astype(LOW)
    value_all = dot_l(low, grads).astype(LOW)
    both_grad[0] = key_all[:rows]
    both_grad[1] = value_all[:rows]
    both_grad_other[0] = key_all[rows:]
    both_grad_other[1] = value_all[rows:]


def attend_back(queries, mixed_grad, probs, own, other):
    rows, width = queries.shape
    plain, keys, spec_probs = specs(rows)
    part = jax.ShapeDtypeStruct((2, rows, width), LOW)
    part_spec = pl.BlockSpec((2, rows, 128), lambda h: (0, 0, h))
    return pl.pallas_call(
        attend_back_kernel,
        grid=(BLOCKS,),
        in_specs=[plain] + keys + [plain, spec_probs],
        out_specs=[plain, part_spec, part_spec],
        out_shape=[jax.ShapeDtypeStruct(queries.shape, LOW), part, part],
        cost_estimate=pl.CostEstimate(
            flops=BLOCKS * 4 * rows * rows * 1024 * 2,
            bytes_accessed=16 * rows * width * 2,
            transcendentals=0,
        ),
    )(queries, own, own, other, other, mixed_grad, probs)


def matmul(left, right):
    return jnp.dot(left, right, preferred_element_type=FULL)


def normalise(values):
    average = jnp.mean(values, axis=-1, keepdims=True)
    centred = values - average
    variance = jnp.mean(centred * centred, axis=-1, keepdims=True)
    scale = lax.rsqrt(variance + 1e-05)
    return centred * scale, scale


def normalise_back(grad, gain, unit, scale):
    scaled = grad * gain
    first = jnp.mean(scaled, axis=-1, keepdims=True)
    second = jnp.mean(scaled * unit, axis=-1, keepdims=True)
    return scale * (scaled - first - unit * second)


def column_sum(values):
    if values.dtype == LOW:
        return matmul(jnp.ones((8, values.shape[0]), LOW), values)[:1]
    return jnp.sum(values, axis=0, keepdims=True)


def left_t(left, right):
    return jnp.einsum("ra,rb->ab", left, right, preferred_element_type=FULL)


def right_t(left, right):
    return jnp.einsum("ra,ba->rb", left, right, preferred_element_type=FULL)


def halves(values):
    turned_values = flip(values)
    half = values.shape[-1] // 2
    return turned_values[..., :half], turned_values[..., half:]


def unfold(parts):
    first = core_low()
    out = []
    for mine, other, pieces, size in parts:
        for j in range(pieces):
            pair = mine[:, j * size : (j + 1) * size], other[:, j * size : (j + 1) * size]
            out += [jnp.where(first, *pair), jnp.where(first, *pair[::-1])]
    return jnp.concatenate(out, axis=1)


def forward_layer(pump, hidden, layer, vectors, meta):
    inputs = hidden.astype(LOW)
    vec = vectors
    own = jnp.concatenate(
        [
            matmul(inputs, layer["key"]).astype(LOW),
            (matmul(inputs, layer["value"]) + vec["value_bias"]).astype(LOW),
        ],
        axis=1,
    )
    far = swap_core(own)
    queries = (matmul(inputs, layer["query"]) + vec["query_bias"]).astype(LOW)
    mixed, probs = attend(queries, own, far, meta)
    pre_one = hidden + (matmul(mixed, layer["out"]) + vec["out_bias"])
    unit_one, scale_one = normalise(pre_one)
    normed = unit_one * vec["first_gain"] + vec["first_shift"]
    normed_low = normed.astype(LOW)
    activated, slope = [], []
    for g in range(GROUPS):
        upward = matmul(normed_low, layer["up"][g]) + vec["up_bias"][:, g * D : (g + 1) * D]
        share = 0.5 * (1.0 + lax.erf(upward * (0.5**0.5)))
        density = jnp.exp(-0.5 * upward * upward) * 0.3989422804014327
        activated.append((upward * share).astype(LOW))
        slope.append((share + upward * density).astype(LOW))
    activated = jnp.concatenate(activated, axis=1)
    pre_two = normed + (matmul(activated, layer["down_all"]) + vec["down_bias"])
    unit_two, scale_two = normalise(pre_two)
    result = unit_two * vec["second_gain"] + vec["second_shift"]
    kept = (inputs, queries, own, far, probs, mixed, unit_one, scale_one, normed_low)
    kept += (activated, slope, unit_two, scale_two)
    return result, kept


def product(left, right):
    sent = left_t(left, right[1]).astype(LOW)
    return sent, lambda: left_t(left, right[0]).astype(LOW)


def backward_layer(pump, upstream, kept, layer, vec, last, rank, tie):
    (inputs, queries, own, far, probs, mixed, unit_one, scale_one, normed_low) = kept[:9]
    activated, slope, unit_two, scale_two = kept[9:]
    grads = {}
    streams = {}
    grads["second_gain"] = column_sum(upstream * unit_two)
    grads["second_shift"] = column_sum(upstream)
    d_two = normalise_back(upstream, vec["second_gain"], unit_two, scale_two)
    down_grad = lax.optimization_barrier(d_two.astype(LOW))
    grads["down_bias"] = column_sum(down_grad)
    first = last is not None
    if first:
        down_halves = halves(down_grad)
        streams["down"] = Scatter(*product(activated, down_halves), "narrow", rank, GROUPS)
        pump.add(streams["down"])
    up_grad = jnp.concatenate(
        [(right_t(down_grad, layer["down"][g]) * slope[g]).astype(LOW) for g in range(GROUPS)],
        axis=1,
    )
    up_grad = lax.optimization_barrier(up_grad)
    up_grad = pump.advance(8.0, up_grad)
    grads["up_bias"] = column_sum(up_grad)
    if first:
        streams["up"] = Scatter(*product(normed_low, halves(up_grad)), "wide", rank + 1)
        pump.add(streams["up"])
    else:
        parts = products(normed_low, activated, up_grad, down_grad)
        up_grad, parts = lax.optimization_barrier((up_grad, parts))
        streams["ff"] = lax.psum_scatter(
            parts, ("wide", "narrow"), scatter_dimension=0, tiled=True
        )
        pump.now += 9.0
    d_normed = d_two
    for g in range(GROUPS):
        d_normed = d_normed + right_t(up_grad[:, g * D : (g + 1) * D], layer["up"][g])
    grads["first_gain"] = column_sum(d_normed * unit_one)
    grads["first_shift"] = column_sum(d_normed)
    d_one = normalise_back(d_normed, vec["first_gain"], unit_one, scale_one)
    branch_grad = lax.optimization_barrier(d_one.astype(LOW))
    branch_grad = pump.advance(14.0, branch_grad)
    grads["out_bias"] = column_sum(branch_grad)
    branch_halves = halves(branch_grad)
    mixed_grad = right_t(branch_grad, layer["out"]).astype(LOW)
    mixed_grad = pump.advance(3.0, mixed_grad)
    query_grad, both, both_far = attend_back(queries, mixed_grad, probs, own, far)
    both_far = pump.advance(10.0, both_far)
    back = swap_core(both_far)
    grads["query_bias"] = column_sum(query_grad)
    query_halves = halves(query_grad)
    sent = [
        left_t(inputs, query_halves[1]).astype(LOW),
        left_t(mixed, branch_halves[1]).astype(LOW),
    ]
    sent[0] = pump.advance(3.0, sent[0])
    both = (both.astype(FULL) + back.astype(FULL)).astype(LOW)
    grads["value_bias"] = column_sum(both[1])
    key_halves, value_halves = halves(both[0]), halves(both[1])
    pairs = [jnp.concatenate([key_halves[i], value_halves[i]], axis=1) for i in range(2)]
    packs = last(grads) if first else None
    if first:
        sent.append(packs[1])

    def kept_part():
        parts = [left_t(inputs, query_halves[0]), left_t(mixed, branch_halves[0])]
        if first:
            parts.append(packs[0].astype(FULL))
        return jnp.concatenate(parts, axis=1).astype(LOW)

    streams["qo"] = Scatter(jnp.concatenate(sent, axis=1), kept_part, "wide", rank + 2)
    streams["kv"] = Scatter(*product(inputs, pairs), "narrow", rank + 2)
    pump.add(streams["qo"])
    pump.add(streams["kv"])
    d_input = d_one + right_t(query_grad, layer["query"])
    d_input = d_input + right_t(both[0], layer["key"]) + right_t(both[1], layer["value"])
    d_input = tie(d_input)
    d_input = pump.advance(8.0, d_input)
    return d_input, streams, grads


NAMES = (
    "query_bias",
    "value_bias",
    "out_bias",
    "down_bias",
    "first_gain",
    "first_shift",
    "second_gain",
    "second_shift",
    "up_bias",
)


GROUPS = FF // D
COUNT = 8 + GROUPS
WIDTH = 4 * D + 2 * FF


def regroup():
    share = D // (lax.axis_size("wide") * lax.axis_size("narrow"))
    devices = D // (GROUPS * share)
    order_out = np.arange(D).reshape(devices, GROUPS, share).transpose(1, 0, 2).reshape(D)
    moves = np.zeros((D, D), np.float32)
    moves[order_out, np.arange(D)] = 1.0
    return jnp.asarray(moves, LOW)


def diagonal(rows, columns):
    row = lax.broadcasted_iota(jnp.int32, (rows, columns), 0)
    return (row == lax.broadcasted_iota(jnp.int32, (rows, columns), 1)).astype(LOW)


def pack_whole(grads):
    vectors = [grads[name] for name in NAMES]

    def kernel(*refs):
        ins, out = refs[:-1], refs[-1]
        rows = [ref[...] for ref in ins[:-1]]
        rows += [ins[-1][:, g * D : (g + 1) * D] for g in range(GROUPS)]
        rows.append(jnp.zeros((16 - len(rows), D), FULL))
        stacked = jnp.concatenate(rows, axis=0).astype(LOW)
        out[...] = dot_l(stacked, diagonal(16, PAD)).astype(LOW)

    return pl.pallas_call(
        kernel,
        out_shape=jax.ShapeDtypeStruct((D, PAD), LOW),
    )(*vectors)


def unpack_whole(core, mine, other):
    def kernel(core_ref, mine_ref, other_ref, *outs):
        def write(order_of):
            for index, ref in enumerate(order_of):
                rows = dot_t(diagonal(16, PAD), ref[...])
                outs[2 * index][...] = rows
                for g in range(GROUPS):
                    outs[2 * index + 1][:, g * D : (g + 1) * D] = rows[8 + g : 9 + g]

        @pl.when(core_ref[0] == 0)
        def _():
            write((mine_ref, other_ref))

        @pl.when(core_ref[0] != 0)
        def _():
            write((other_ref, mine_ref))

    spec = pl.BlockSpec(memory_space=pltpu.VMEM)
    outs = pl.pallas_call(
        kernel,
        in_specs=[pl.BlockSpec(memory_space=pltpu.SMEM), spec, spec],
        out_shape=[jax.ShapeDtypeStruct((16, D), FULL), jax.ShapeDtypeStruct((1, FF), FULL)] * 2,
    )(core, mine, other)
    out = []
    for index in range(LAYERS):
        rows = outs[2 * index]
        vectors = {name: rows[i : i + 1] for i, name in enumerate(NAMES[:-1])}
        vectors["up_bias"] = outs[2 * index + 1]
        out.append(vectors)
    return out


def group_columns(values, moves, back=False):
    cut = D // GROUPS
    if not back:
        parts = [
            jnp.dot(values[:, q * D : (q + 1) * D], moves, preferred_element_type=FULL)
            for q in range(GROUPS)
        ]
        return [
            jnp.concatenate([part[:, g * cut : (g + 1) * cut] for part in parts], axis=1)
            for g in range(GROUPS)
        ]
    out = []
    for q in range(GROUPS):
        part = [values[:, g * D + q * cut : g * D + (q + 1) * cut] for g in range(GROUPS)]
        out.append(dot_t(jnp.concatenate(part, axis=1), moves))
    return out


def pack_shards(core, weights, vectors, moves):
    query, key, value, out, up, down = weights
    share = query.shape[1]
    names = list(NAMES)

    def kernel(core_ref, q_ref, k_ref, v_ref, o_ref, u_ref, d_ref, moves_ref, *refs):
        ins, (mine_ref, sent_ref, whole_ref) = refs[:-3], refs[-3:]
        for j, ref in enumerate((k_ref, v_ref, q_ref, o_ref)):
            whole_ref[j] = ref[1]
        packs = []
        for index in range(LAYERS):
            base = 4 + index * 2 * GROUPS
            for g, part in enumerate(group_columns(u_ref[index], moves_ref[...])):
                whole_ref[base + g] = part.astype(LOW)
            for g in range(GROUPS):
                whole_ref[base + GROUPS + g] = d_ref[index, g * share : (g + 1) * share]
            rows = [ref[index : index + 1].astype(FULL) for ref in ins[:-1]]
            for g in range(GROUPS):
                rows.append(ins[-1][index : index + 1, g * share : (g + 1) * share].astype(FULL))
            rows.append(jnp.zeros((PAD - len(rows), share), FULL))
            packs.append(jnp.concatenate(rows, axis=0).T.astype(LOW))

        def write(target, side):
            for j, ref in enumerate((k_ref, v_ref, q_ref, o_ref)):
                target[:, j * HALF : (j + 1) * HALF] = ref[0, :, side * HALF : (side + 1) * HALF]
            target[:, 4 * HALF :] = packs[side]

        @pl.when(core_ref[0] == 0)
        def _():
            write(mine_ref, 0)
            write(sent_ref, 1)

        @pl.when(core_ref[0] != 0)
        def _():
            write(mine_ref, 1)
            write(sent_ref, 0)

    spec = pl.BlockSpec(memory_space=pltpu.VMEM)
    half = jax.ShapeDtypeStruct((share, 4 * HALF + PAD), LOW)
    return pl.pallas_call(
        kernel,
        in_specs=[pl.BlockSpec(memory_space=pltpu.SMEM)] + [spec] * (7 + len(names)),
        out_shape=[half, half, jax.ShapeDtypeStruct((4 + 4 * GROUPS, share, D), LOW)],
    )(core, *weights, moves, *[vectors[name] for name in names])


def join_rows(core, mine, other, cuts):
    def kernel(core_ref, mine_ref, other_ref, *outs):
        for (start, size), out in zip(cuts, outs):
            out[core_ref[0]] = mine_ref[:, start : start + size]
            out[1 - core_ref[0]] = other_ref[:, start : start + size]

    spec = pl.BlockSpec(memory_space=pltpu.VMEM)
    return pl.pallas_call(
        kernel,
        in_specs=[pl.BlockSpec(memory_space=pltpu.SMEM), spec, spec],
        out_shape=[jax.ShapeDtypeStruct((2, mine.shape[0], size), LOW) for _, size in cuts],
    )(core, mine, other)


def unpack_shards(core, first, second, moves):
    share = second.shape[0]

    def kernel(core_ref, second_ref, moves_ref, *refs):
        group, outs = refs[:4], refs[4:]
        grouped = second_ref[:, :FF]
        for q, part in enumerate(group_columns(grouped, moves_ref[...], back=True)):
            outs[4][1, :, q * D : (q + 1) * D] = part
        for g in range(GROUPS):
            start = (GROUPS + g) * D
            outs[5][1, g * share : (g + 1) * share] = second_ref[:, start : start + D].astype(FULL)

        def write(flipped):
            for side in range(2):
                rows = group[side ^ flipped]
                downs = group[2 + (side ^ flipped)]
                cut = slice(side * HALF, (side + 1) * HALF)
                tail = 4 * HALF + FF // 2
                for j, place in enumerate((0, 3, 1, 2)):
                    outs[place][0, :, cut] = rows[:, j * HALF : (j + 1) * HALF].astype(FULL)
                    start = tail + PAD + j * HALF
                    outs[place][1, :, cut] = rows[:, start : start + HALF].astype(FULL)
                outs[6][side] = rows[:, tail : tail + PAD].astype(FULL).T
                for g in range(GROUPS):
                    place = slice(g * share, (g + 1) * share)
                    outs[5][0, place, cut] = downs[place].astype(FULL)
            ups = [group[side ^ flipped][:, 4 * HALF : 4 * HALF + FF // 2] for side in range(2)]
            ups = group_columns(jnp.concatenate(ups, axis=1), moves_ref[...], back=True)
            for q, part in enumerate(ups):
                outs[4][0, :, q * D : (q + 1) * D] = part

        @pl.when(core_ref[0] == 0)
        def _():
            write(0)

        @pl.when(core_ref[0] != 0)
        def _():
            write(1)

    spec = pl.BlockSpec(memory_space=pltpu.VMEM)
    shapes = [(share, D)] * 4 + [(share, FF), (GROUPS * share, D), (PAD, share)]
    *weights, rows = pl.pallas_call(
        kernel,
        in_specs=[pl.BlockSpec(memory_space=pltpu.SMEM)] + [spec] * (2 + len(first)),
        out_shape=[jax.ShapeDtypeStruct((LAYERS,) + shape, FULL) for shape in shapes],
    )(core, second, moves, *first)
    vectors = {name: rows[:, i] for i, name in enumerate(NAMES[:-1])}
    vectors["up_bias"] = rows[:, 8 : 8 + GROUPS].reshape(LAYERS, -1)
    return weights, vectors


def products(normed, activated, up, down):
    rows = normed.shape[0]
    steps = 2 * GROUPS

    def kernel(normed_ref, act_ref, up_ref, down_ref, out):
        step = pl.program_id(0)

        @pl.when(step < GROUPS)
        def _():
            out[...] = dot_l(normed_ref[...], up_ref[...]).astype(LOW)

        @pl.when(step >= GROUPS)
        def _():
            out[...] = dot_l(act_ref[...], down_ref[...]).astype(LOW)

    def at(low):
        return pl.BlockSpec((rows, D), lambda i: (0, jnp.clip(i - low, 0, GROUPS - 1)))

    whole = pl.BlockSpec((rows, D), lambda i: (0, 0))
    return pl.pallas_call(
        kernel,
        grid=(steps,),
        in_specs=[whole, at(GROUPS), at(0), whole],
        out_specs=pl.BlockSpec((D, D), lambda i: (0, i)),
        out_shape=jax.ShapeDtypeStruct((D, steps * D), LOW),
        cost_estimate=pl.CostEstimate(
            flops=2 * rows * D * D * steps, bytes_accessed=D * D * steps * 2, transcendentals=0
        ),
    )(normed, activated, up, down)


def body(
    tokens,
    query_weight,
    key_weight,
    value_weight,
    out_weight,
    up_weight,
    down_weight,
    query_bias,
    value_bias,
    out_bias,
    up_bias,
    down_bias,
    first_gain,
    first_shift,
    second_gain,
    second_shift,
    lengths,
    cotangent,
):
    pairs, rows_pair, width = tokens.shape
    given = dict(
        query_bias=query_bias,
        value_bias=value_bias,
        out_bias=out_bias,
        up_bias=up_bias,
        down_bias=down_bias,
        first_gain=first_gain,
        first_shift=first_shift,
        second_gain=second_gain,
        second_shift=second_shift,
    )
    core = own_bit("narrow", 0).astype(jnp.int32).reshape(1)
    side_x = own_bit("narrow", 1)
    moves = regroup()
    mine, sent, shard = pack_shards(
        core,
        (query_weight, key_weight, value_weight, out_weight, up_weight, down_weight),
        given,
        moves,
    )
    other = swap_core(sent)
    whole = lax.all_gather(shard, ("wide", "narrow"), axis=1, tiled=True)
    kv_0, qo_0 = join_rows(core, mine, other, [(0, D), (D, D + PAD)])
    pump = Pump()
    pump.now = 13.0
    gathers = [Gather(kv_0, "wide", 0), Gather(qo_0, "narrow", 0)]
    for stream in gathers:
        pump.add(stream)

    def collect(values, rank):
        keep = lax.dynamic_index_in_dim(values, side_x, 0, keepdims=False)
        sent = lax.dynamic_index_in_dim(values, 1 - side_x, 0, keepdims=False)
        stream = Exchange(sent, 1, rank)
        pump.add(stream)

        def joined():
            pump.need([stream])
            return jnp.concatenate([keep, stream.other], axis=0)

        return joined

    def hand_back(values, rank):
        mine = values[:rows_pair]
        stream = Exchange(values[rows_pair:], 1, rank)
        pump.add(stream)
        first = side_x == 0
        return stream, lambda: jnp.stack(
            [jnp.where(first, mine, stream.other), jnp.where(first, stream.other, mine)], axis=0
        )

    narrow = lax.axis_index("narrow")
    scalars = [lax.dynamic_index_in_dim(lengths, side_x, 0, keepdims=False)]
    scalars += [(narrow ^ j) * rows_pair for j in (0, 2, 1, 3)]
    meta = jnp.stack([value.astype(jnp.int32) for value in scalars])

    hidden = collect(tokens, -1)
    upstream = collect(cotangent, 9)
    pump.need(gathers)
    parts = [(stream.mine, stream.other, 2, HALF) for stream in gathers]
    kv, qo = unfold(parts[:1]), unfold(parts[1:])
    first_pieces = dict(key=kv[:, :D], value=kv[:, D:], query=qo[:, :D], out=qo[:, D:])
    second_pieces = dict(key=whole[0], value=whole[1], query=whole[2], out=whole[3])
    layers = []
    for index, pieces in enumerate((first_pieces, second_pieces)):
        base = 4 + index * 2 * GROUPS
        pieces["up"] = [whole[base + g] for g in range(GROUPS)]
        down = whole[base + GROUPS : base + 2 * GROUPS]
        pieces["down"] = [down[g] for g in range(GROUPS)]
        pieces["down_all"] = down.reshape(FF, D)
        layers.append(pieces)
    vectors = unpack_whole(core, gathers[1].mine[:, D:], gathers[1].other[:, D:])
    kept = []
    hidden = hidden().astype(FULL)
    for index in range(LAYERS):
        hidden, saved = forward_layer(
            pump, hidden, layers[index], vectors[index], meta
        )
        kept.append(saved)
    output = hand_back(hidden.astype(LOW), 9)
    grads = [None] * LAYERS
    scatters = [None] * LAYERS

    def pack_all(first_grads):
        low, high = pack_whole(first_grads), pack_whole(grads[1])
        first = core_low()
        return jnp.where(first, low, high), jnp.where(first, high, low)

    upstream = upstream().astype(FULL)

    def hold(value):
        value, scatters[1]["ff"] = lax.optimization_barrier((value, scatters[1]["ff"]))
        return value

    for index in reversed(range(LAYERS)):
        upstream, scatters[index], grads[index] = backward_layer(
            pump,
            upstream,
            kept[index],
            layers[index],
            vectors[index],
            pack_all if index == 0 else None,
            0 if index == 1 else 4,
            hold if index == 0 else lambda value: value,
        )
    tokens_grad = hand_back(upstream.astype(LOW), 9)
    second_ff = scatters[1].pop("ff")
    for streams in scatters[::-1]:
        pump.need(streams.values())
    streams = scatters[0]
    rows = [streams[name].result[0] for name in ("qo", "kv", "up")]
    rows = [rows[0][:, :D], rows[1], rows[2], rows[0][:, D:]]
    rows += [scatters[1][name].result[0] for name in ("qo", "kv")]
    rows = jnp.concatenate(rows, axis=1)
    ends = []
    downs = streams["down"].result
    share = downs.shape[1] // 2
    downs = downs.reshape(GROUPS, 2, share, HALF).transpose(1, 0, 2, 3)
    for values in (rows, downs):
        split = values.reshape(2, -1, values.shape[-1])
        mine = lax.dynamic_index_in_dim(split, core[0], 0, keepdims=False)
        sent = lax.dynamic_index_in_dim(split, 1 - core[0], 0, keepdims=False)
        ends += [mine, swap_core(sent)]
    weight_grads, small = unpack_shards(core, ends, second_ff, moves)
    pump.need([output[0], tokens_grad[0]])
    names = (
        "query_bias",
        "value_bias",
        "out_bias",
        "up_bias",
        "down_bias",
        "first_gain",
        "first_shift",
        "second_gain",
        "second_shift",
    )
    return (output[1](), tokens_grad[1](), *weight_grads, *[small[name] for name in names])


def solution(mesh):
    rows = P("wide", "narrow", None)
    weight = P(None, ("wide", "narrow"), None)
    vector = P(None, ("wide", "narrow"))
    return jax.shard_map(
        body,
        mesh=mesh,
        in_specs=(rows,) + (weight,) * 6 + (vector,) * 9 + (P("wide"), rows),
        out_specs=(rows, rows) + (weight,) * 6 + (vector,) * 9,
        check_vma=False,
    )
```

time: 675 us -> 530 us (0.79)
  waiting for transfers between devices: 300 us -> 200 us
  other arithmetic: 89.6 us -> 43.5 us
  local copies, waits for them, and re-layouts: 80.1 us -> 40.4 us
  matrix products: 68.6 us -> 105 us
  starting transfers between devices: 72.2 us -> 56.1 us
  Pallas kernels: 48.1 us -> 61.6 us
  between operations: 3.12 us -> 16.4 us
    ppermute x72 -> x51, waiting for transfers between devices: 300 us -> 159 us  [swap(): return lax.ppermute(value, name, pairs)]
    all_gather x0 -> x1, waiting for transfers between devices: none -> 40.4 us  [body(): whole = lax.all_gather(shard, ('wide', 'narrow'), axis=1, tiled=True)]
    dot_general x8 -> x24, matrix products: 22.2 us -> 42.7 us  [right_t(): return jnp.einsum('ra,ba->rb', left, right, preferred_element_type=FULL)]
    pallas_call x2 -> x9, Pallas kernels: 25.2 us -> 44.7 us  [the longest x2 17.9 us: attend_back(): pl.pallas_call(attend_back_kernel, grid=(BLOCKS,), in_specs=[plain] + key...]
    concatenate x32 -> x8, other arithmetic: 22.5 us -> 4.44 us  [the longest x2 1.56 us: backward_layer(): jnp.concatenate([(right_t(down_grad, layer['down'][g]) * slope[g]).astype...]
    ppermute x72 -> x51, starting transfers between devices: 72.2 us -> 56 us  [swap(): return lax.ppermute(value, name, pairs)]
    reshape x20 -> x1, local copies, waits for them, and re-layouts: 16.6 us -> 0.65 us  [unpack_shards(): vectors['up_bias'] = rows[:, 8:8 + GROUPS].reshape(LAYERS, -1)]
    dot_general x10 -> x28, matrix products: 28.2 us -> 43.4 us  [matmul(): return jnp.dot(left, right, preferred_element_type=FULL)]
  transfers between devices with their start and end apart: 72 -> 53, of which waited for: 39 -> 28; matrix products, arithmetic and copies ran while one was open for 29% -> 23% of each run, Pallas kernels for 4% -> 6%
where the time goes in v2:
time: 530 us; the launch traced here: 523 us
  waiting for transfers between devices  200 us (38%)
  matrix products  105 us (20%)
  Pallas kernels  61.6 us (12%)
  starting transfers between devices  56.1 us (11%)
  other arithmetic  43.5 us (8%)
  local copies, waits for them, and re-layouts  40.4 us (8%)
  between operations  16.4 us (3%)
    ppermute x51, waiting for transfers between devices, swap(): return lax.ppermute(value, name, pairs)  159 us
    ppermute x51, starting transfers between devices, swap(): return lax.ppermute(value, name, pairs)  56 us
    dot_general x28, matrix products, matmul(): return jnp.dot(left, right, preferred_element_type=FULL)  43.4 us
    dot_general x24, matrix products, right_t(): return jnp.einsum('ra,ba->rb', left, right, preferred_element_type=FULL)  42.7 us
    all_gather x1, waiting for transfers between devices, body(): whole = lax.all_gather(shard, ('wide', 'narrow'), axis=1, tiled=True)  40.4 us
    dot_general x16, matrix products, left_t(): return jnp.einsum('ra,rb->ab', left, right, preferred_element_type=FULL)  18.8 us
    pallas_call x2, Pallas kernels, attend_back(): pl.pallas_call(attend_back_kernel, grid=(BLOCKS,), in_specs=[plain] + key...  17.9 us
    pallas_call x2, Pallas kernels, attend(): pl.pallas_call(attend_kernel, grid_spec=pltpu.PrefetchScalarGridSpec(num_...  16.9 us
  transfers between devices with their start and end apart: 53, of which 28 were waited for; matrix products, arithmetic and copies ran while one was open for 23% of the time, Pallas kernels for 6%

profile of v2, /device:TPU:0, one launch (start us, length us, event | category | flops | bytes accessed | tf_op | source)
XLA Modules:
  0.0 522.6 jit_solution(15212608927065864462)
XLA Ops:
  7.3 4.5 shard_map.314
  16.1 3.6 collective-permute-start.3
  19.8 4.8 collective-permute-done.3
  25.6 5.6 %collective-permute-start.5 = (bf16[2,1,1,1,2,24,768]{6,5,4,0,3,2,1:T(8,128)(2,1)S(1)}, bf16[2,1,1,1,2,24,768]{6,5,4,0,3,2,1:T(8,128)(2,1)S(1)}, u32[]{:S(2)}, u32[]{:S(2)}) collective-permute-start(bf16[2,1,1,1,2,24,768]{6,5,4,0,3,2,1:T(8,128)(2,1)S(1)} %broadcast_select_fusion.15), channel_id=1, source_target_pairs={{0,8},{4,12},{8,0},{12,4},{16,24},{20,28},{24,16},{28,20},{1,9},{5... | collective-permute-start | bytes 442376 | tf_op jit(solution)/shard_map/ppermute | solution.py:29
  32.2 4.8 collective-permute-start.4
  37.0 7.4 %collective-permute-done.5 = bf16[2,1,1,1,2,24,768]{6,5,4,0,3,2,1:T(8,128)(2,1)S(1)} collective-permute-done((bf16[2,1,1,1,2,24,768]{6,5,4,0,3,2,1:T(8,128)(2,1)S(1)}, bf16[2,1,1,1,2,24,768]{6,5,4,0,3,2,1:T(8,128)(2,1)S(1)}, u32[]{:S(2)}, u32[]{:S(2)}) %collective-permute-start.5) | collective-permute-done | bytes 147488 | tf_op jit(solution)/shard_map/ppermute | solution.py:29
  45.5 5.1 collective-permute-done.4
  53.6 12.6 %collective-permute-done.6 = bf16[2,2,1,1,2,24,896]{6,5,4,1,0,3,2:T(8,128)(2,1)S(1)} collective-permute-done((bf16[2,2,1,1,2,24,896]{6,5,4,1,0,3,2:T(8,128)(2,1)S(1)}, bf16[2,2,1,1,2,24,896]{6,5,4,1,0,3,2:T(8,128)(2,1)S(1)}, u32[]{:S(2)}, u32[]{:S(2)}) %collective-permute-start.6) | collective-permute-done | bytes 344096 | tf_op jit(solution)/shard_map/ppermute | solution.py:29
  66.3 24.0 %collective-permute-done.9 = bf16[2,2,2,1,2,24,768]{6,5,4,2,1,0,3:T(8,128)(2,1)S(1)} collective-permute-done((bf16[2,2,2,1,2,24,768]{6,5,4,2,1,0,3:T(8,128)(2,1)S(1)}, bf16[2,2,2,1,2,24,768]{6,5,4,2,1,0,3:T(8,128)(2,1)S(1)}, u32[]{:S(2)}, u32[]{:S(2)}) %collective-permute-start.9) | collective-permute-done | bytes 589856 | tf_op jit(solution)/shard_map/ppermute | solution.py:29
  94.1 16.3 %collective-permute-done.8 = bf16[2,2,1,2,2,24,896]{6,5,4,3,1,0,2:T(8,128)(2,1)S(1)} collective-permute-done((bf16[2,2,1,2,2,24,896]{6,5,4,3,1,0,2:T(8,128)(2,1)S(1)}, bf16[2,2,1,2,2,24,896]{6,5,4,3,1,0,2:T(8,128)(2,1)S(1)}, u32[]{:S(2)}, u32[]{:S(2)}) %collective-permute-start.8) | collective-permute-done | bytes 688160 | tf_op jit(solution)/shard_map/ppermute | solution.py:29
  112.7 2.5 collective-permute-start.1
  115.9 2.9 broadcast_select_fusion.7
  118.8 6.1 %collective-permute-done.1 = bf16[128,768]{1,0:T(8,128)(2,1)S(1)} collective-permute-done((bf16[128,768]{1,0:T(8,128)(2,1)}, bf16[128,768]{1,0:T(8,128)(2,1)S(1)}, u32[]{:S(2)}, u32[]{:S(2)}) %collective-permute-start.1) | collective-permute-done | bytes 196640 | tf_op jit(solution)/shard_map/ppermute | solution.py:29
  127.8 2.1 shard_map.316
  135.2 2.3 broadcast_select_fusion.3
  138.9 8.3 %shard_map.317 = (bf16[256,768]{1,0:T(8,128)(2,1)}, bf16[6,512,512]{2,1,0:T(8,128)(2,1)}) custom-call(s32[5]{0:T(128)} %stack.38.meta, bf16[256,768]{1,0:T(8,128)(2,1)} %fusion.7.query, bf16[256,1536]{1,0:T(8,128)(2,1)} %copy-done.35, bf16[256,1536]{1,0:T(8,128)(2,1)} %copy-done.35, bf16[256,1536]{1,0:T(8,128)(2,1)} %collective-permute-done.12.key_other.value_other, ...), custom_call_target="tpu_custom_call" | custom-call | flops 1610612736 | bytes 3145728 | tf_op jit(solution)/shard_map/pallas_call | solution.py:325
  149.2 40.4 %all-gather.2.cloned.1.call-done = bf16[20,768,768]{2,1,0:T(8,128)(2,1)} async-done(((bf16[20,24,768]{2,1,0:T(8,128)(2,1)}), bf16[20,768,768]{2,1,0:T(8,128)(2,1)}) %all-gather.2.cloned.1.call-update) | async-done | bytes 23592976 | tf_op jit(solution)/shard_map/all_gather | solution.py:846
  189.7 6.5 %fusion.154 = (bf16[4,768,768]{2,1,0:T(8,128)(2,1)S(1)}, bf16[4,768,768]{2,1,0:T(8,128)(2,1)}) fusion(bf16[20,768,768]{2,1,0:T(8,128)(2,1)} %all-gather.2.cloned.1.call-done), kind=kLoop, calls=%fused_computation.451 | loop fusion | bytes 18874368 | tf_op jit(solution)/shard_map/slice | solution.py:891
  196.2 2.7 multiply_convert_fusion.4
  198.9 2.8 multiply_convert_fusion.5
  201.7 2.8 multiply_convert_fusion.6
  204.6 2.8 multiply_convert_fusion.7
  215.1 2.5 fusion.9.query
  217.6 8.6 %shard_map.318 = (bf16[256,768]{1,0:T(8,128)(2,1)}, bf16[6,512,512]{2,1,0:T(8,128)(2,1)}) custom-call(s32[5]{0:T(128)} %stack.38.meta, bf16[256,768]{1,0:T(8,128)(2,1)} %fusion.9.query, bf16[256,1536]{1,0:T(8,128)(2,1)} %copy-done.36, bf16[256,1536]{1,0:T(8,128)(2,1)} %copy-done.36, bf16[256,1536]{1,0:T(8,128)(2,1)} %collective-permute-done.13.key_other.value_other, ...), custom_call_target="tpu_custom_call" | custom-call | flops 1610612736 | bytes 3145728 | tf_op jit(solution)/shard_map/pallas_call | solution.py:325
  226.2 2.0 fusion.172
  228.7 2.0 multiply_convert_fusion
  230.7 2.0 multiply_convert_fusion.1
  232.7 1.9 multiply_convert_fusion.2
  241.7 2.0 fusion.14
  243.7 1.8 fusion.13
  245.6 1.8 fusion.12
  247.4 1.8 fusion.11
  250.7 9.5 %shard_map.319 = bf16[768,6144]{1,0:T(8,128)(2,1)} custom-call(bf16[256,768]{1,0:T(8,128)(2,1)} %copy-done.26, bf16[256,3072]{1,0:T(8,128)(2,1)} %pad_maximum_fusion.1.act_ref, bf16[256,3072]{1,0:T(8,128)(2,1)} %pad_maximum_fusion.2.up_ref, bf16[256,768]{1,0:T(8,128)(2,1)} %copy-done.12), custom_call_target="tpu_custom_call" | custom-call | flops 2415919104 | bytes 9437184 | tf_op jit(solution)/shard_map/pallas_call | solution.py:792
  260.2 2.2 convolution_add_fusion.9
  264.2 1.9 convolution_add_fusion.7
  266.1 2.6 multiply_reduce_fusion
  273.5 2.5 convolution_convert_fusion.17.mixed_grad
  276.0 9.0 %shard_map.320 = (bf16[256,768]{1,0:T(8,128)(2,1)}, bf16[2,256,768]{2,1,0:T(8,128)(2,1)}, bf16[2,256,768]{2,1,0:T(8,128)(2,1)}) custom-call(bf16[256,768]{1,0:T(8,128)(2,1)} %fusion.9.query, bf16[256,1536]{1,0:T(8,128)(2,1)} %copy-done.36, bf16[256,1536]{1,0:T(8,128)(2,1)} %copy-done.36, bf16[256,1536]{1,0:T(8,128)(2,1)} %collective-permute-done.13.key_other.value_other, ...), custom_call_target="tpu_custom_call" | custom-call | flops 3221225472 | bytes 6291456 | tf_op jit(solution)/shard_map/pallas_call | solution.py:383
  297.3 2.2 collective-permute-done.14
  310.2 1.9 fusion.22
  312.1 1.9 fusion.3
  324.3 2.0 fusion.18
  326.3 2.0 fusion.17
  328.3 1.9 fusion.16
  330.3 1.9 fusion.15
  346.4 2.0 multiply_reduce_fusion.2
  351.6 25.3 %collective-permute-done.28 = bf16[4,2,2,1,2,48,384]{6,5,4,3,2,1,0:T(8,128)(2,1)S(1)} collective-permute-done((bf16[4,2,2,1,2,48,384]{6,5,4,3,2,1,0:T(8,128)(2,1)S(1)}, bf16[4,2,2,1,2,48,384]{6,5,4,3,2,1,0:T(8,128)(2,1)S(1)}, u32[]{:S(2)}, u32[]{:S(2)}) %collective-permute-start.28) | collective-permute-done | bytes 1179680 | tf_op jit(solution)/shard_map/ppermute | solution.py:29
  378.3 2.4 add_convert_fusion.1
  381.9 8.9 %shard_map.321 = (bf16[256,768]{1,0:T(8,128)(2,1)}, bf16[2,256,768]{2,1,0:T(8,128)(2,1)}, bf16[2,256,768]{2,1,0:T(8,128)(2,1)}) custom-call(bf16[256,768]{1,0:T(8,128)(2,1)} %fusion.7.query, bf16[256,1536]{1,0:T(8,128)(2,1)} %copy-done.35, bf16[256,1536]{1,0:T(8,128)(2,1)} %copy-done.35, bf16[256,1536]{1,0:T(8,128)(2,1)} %collective-permute-done.12.key_other.value_other, ...), custom_call_target="tpu_custom_call" | custom-call | flops 3221225472 | bytes 6291456 | tf_op jit(solution)/shard_map/pallas_call | solution.py:383
  416.8 15.5 %collective-permute-done.26 = bf16[1,2,2,2,1,48,1536]{6,5,4,3,2,1,0:T(8,128)(2,1)} collective-permute-done((bf16[1,2,2,2,1,48,1536]{6,5,4,3,2,1,0:T(8,128)(2,1)}, bf16[1,2,2,2,1,48,1536]{6,5,4,3,2,1,0:T(8,128)(2,1)}, u32[]{:S(2)}, u32[]{:S(2)}) %collective-permute-start.26) | collective-permute-done | bytes 1179680 | tf_op jit(solution)/shard_map/ppermute | solution.py:29
  433.8 2.7 copy.45
  436.6 2.0 add_convert_fusion.8
  447.3 2.4 collective-permute-start.46
  449.7 3.4 collective-permute-done.46
  455.0 3.5 collective-permute-done.47
  459.0 9.2 %collective-permute-done.36 = bf16[1,2,2,1,2,48,768]{6,5,4,3,2,1,0:T(8,128)(2,1)S(1)} collective-permute-done((bf16[1,2,2,1,2,48,768]{6,5,4,3,2,1,0:T(8,128)(2,1)S(1)}, bf16[1,2,2,1,2,48,768]{6,5,4,3,2,1,0:T(8,128)(2,1)S(1)}, u32[]{:S(2)}, u32[]{:S(2)}) %collective-permute-start.36) | collective-permute-done | bytes 589856 | tf_op jit(solution)/shard_map/ppermute | solution.py:29
  474.8 2.4 collective-permute-done.40
  478.1 3.2 collective-permute-done.39
  481.8 1.9 collective-permute-start.41
  485.6 3.8 collective-permute-done.41
  490.1 2.0 collective-permute-start.43
  492.2 5.0 collective-permute-done.43
  498.9 4.7 collective-permute-done.44
  506.6 5.7 %shard_map.324 = (f32[2,24,768]{2,1,0:T(8,128)}, f32[2,24,768]{2,1,0:T(8,128)}, f32[2,24,768]{2,1,0:T(8,128)}, f32[2,24,768]{2,1,0:T(8,128)}, f32[2,24,3072]{2,1...) custom-call(s32[1]{0:T(128)} %bitcast.2.core_ref, ...), custom_call_target="tpu_custom_call" | custom-call | tf_op jit(solution)/shard_map/pallas_call | solution.py:763
  (497 shorter events, 161.0 us)
Async XLA Ops:
  7.2 182.5 %all-gather.2.cloned.1.call-start = ((), (), s32[]{:S(2)}) async-start(), calls=%async_computation.1 | async-start | bytes 24330240 | tf_op jit(solution)/shard_map/all_gather | solution.py:846
  11.7 469.7 %reduce-scatter.2.cloned.1.call-start = ((), (), s32[]{:S(2)}) async-start(), calls=%async_computation.2 | async-start | bytes 9732096 | tf_op jit(solution)/shard_map/reduce_scatter | solution.py:512
  11.8 2.1 collective-permute-start
  13.0 227.6 %copy-start.25 = (bf16[128,768]{1,0:T(8,128)(2,1)}, bf16[128,768]{1,0:T(8,128)(2,1)S(1)}, u32[]{:S(2)}) copy-start(bf16[128,768]{1,0:T(8,128)(2,1)S(1)} %get-tuple-element.405) | copy-start | bytes 589828
  16.1 8.5 %collective-permute-start.3 = (bf16[1,1,1,1,2,24,768]{6,5,4,3,2,1,0:T(8,128)(2,1)}, bf16[1,1,1,1,2,24,768]{6,5,4,3,2,1,0:T(8,128)(2,1)S(1)}, u32[]{:S(2)}, u32[]{:S(2)}) collective-permute-start(bf16[1,1,1,1,2,24,768]{6,5,4,3,2,1,0:T(8,128)(2,1)} %bitcast.290), channel_id=1, source_target_pairs={{0,16},{4,20},{8,24},{12,28},{16,0},{20,4},{24,8},{28,12},{1,17},{... | collective-permute-start | bytes 221192 | tf_op jit(solution)/shard_map/ppermute | solution.py:29
  19.7 11.5 %collective-permute-start.2 = (bf16[1,1,1,1,2,24,896]{6,5,4,3,2,1,0:T(8,128)(2,1)}, bf16[1,1,1,1,2,24,896]{6,5,4,3,2,1,0:T(8,128)(2,1)S(1)}, u32[]{:S(2)}, u32[]{:S(2)}) collective-permute-start(bf16[1,1,1,1,2,24,896]{6,5,4,3,2,1,0:T(8,128)(2,1)} %bitcast.288), channel_id=1, source_target_pairs={{0,16},{4,20},{8,24},{12,28},{16,0},{20,4},{24,8},{28,12},{1,17},{... | collective-permute-start | bytes 258056 | tf_op jit(solution)/shard_map/ppermute | solution.py:29
  25.6 18.8 %collective-permute-start.5 = (bf16[2,1,1,1,2,24,768]{6,5,4,0,3,2,1:T(8,128)(2,1)S(1)}, bf16[2,1,1,1,2,24,768]{6,5,4,0,3,2,1:T(8,128)(2,1)S(1)}, u32[]{:S(2)}, u32[]{:S(2)}) collective-permute-start(bf16[2,1,1,1,2,24,768]{6,5,4,0,3,2,1:T(8,128)(2,1)S(1)} %broadcast_select_fusion.15), channel_id=1, source_target_pairs={{0,8},{4,12},{8,0},{12,4},{16,24},{20,28},{24,16},{28,20},{1,9},{5... | collective-permute-start | bytes 442376 | tf_op jit(solution)/shard_map/ppermute | solution.py:29
  32.2 18.5 %collective-permute-start.4 = (bf16[2,1,1,1,2,24,896]{6,5,4,0,3,2,1:T(8,128)(2,1)S(1)}, bf16[2,1,1,1,2,24,896]{6,5,4,0,3,2,1:T(8,128)(2,1)S(1)}, u32[]{:S(2)}, u32[]{:S(2)}) collective-permute-start(bf16[2,1,1,1,2,24,896]{6,5,4,0,3,2,1:T(8,128)(2,1)S(1)} %broadcast_select_fusion.14), channel_id=1, source_target_pairs={{0,8},{4,12},{8,0},{12,4},{16,24},{20,28},{24,16},{28,20},{1,9},{5... | collective-permute-start | bytes 516104 | tf_op jit(solution)/shard_map/ppermute | solution.py:29
  44.5 8.1 %collective-permute-start.7 = (bf16[2,2,1,1,2,24,768]{6,5,4,1,0,3,2:T(8,128)(2,1)S(1)}, bf16[2,2,1,1,2,24,768]{6,5,4,1,0,3,2:T(8,128)(2,1)S(1)}, u32[]{:S(2)}, u32[]{:S(2)}) collective-permute-start(bf16[2,2,1,1,2,24,768]{6,5,4,1,0,3,2:T(8,128)(2,1)S(1)} %broadcast_select_fusion.11), channel_id=1, source_target_pairs={{0,4},{4,0},{8,12},{12,8},{16,20},{20,16},{24,28},{28,24},{1,5},{5... | collective-permute-start | bytes 884744 | tf_op jit(solution)/shard_map/ppermute | solution.py:29
  50.8 15.4 %collective-permute-start.6 = (bf16[2,2,1,1,2,24,896]{6,5,4,1,0,3,2:T(8,128)(2,1)S(1)}, bf16[2,2,1,1,2,24,896]{6,5,4,1,0,3,2:T(8,128)(2,1)S(1)}, u32[]{:S(2)}, u32[]{:S(2)}) collective-permute-start(bf16[2,2,1,1,2,24,896]{6,5,4,1,0,3,2:T(8,128)(2,1)S(1)} %broadcast_select_fusion.10), channel_id=1, source_target_pairs={{0,2},{1,3},{2,0},{3,1},{4,6},{5,7},{6,4},{7,5},{8,10},{9,11},{10,... | collective-permute-start | bytes 1032200 | tf_op jit(solution)/shard_map/ppermute | solution.py:29
  52.8 37.6 %collective-permute-start.9 = (bf16[2,2,2,1,2,24,768]{6,5,4,2,1,0,3:T(8,128)(2,1)S(1)}, bf16[2,2,2,1,2,24,768]{6,5,4,2,1,0,3:T(8,128)(2,1)S(1)}, u32[]{:S(2)}, u32[]{:S(2)}) collective-permute-start(bf16[2,2,2,1,2,24,768]{6,5,4,2,1,0,3:T(8,128)(2,1)S(1)} %broadcast_select_fusion.1), channel_id=1, source_target_pairs={{0,2},{1,3},{2,0},{3,1},{4,6},{5,7},{6,4},{7,5},{8,10},{9,11},{10,... | collective-permute-start | bytes 1769480 | tf_op jit(solution)/shard_map/ppermute | solution.py:29
  92.4 20.2 %collective-permute-start.10 = (bf16[768,768]{1,0:T(8,128)(2,1)S(1)}, bf16[768,768]{1,0:T(8,128)(2,1)}, u32[]{:S(2)}, u32[]{:S(2)}) collective-permute-start(bf16[768,768]{1,0:T(8,128)(2,1)S(1)} %bitcast_select_fusion.1), channel_id=1, source_target_pairs={{0,1},{1,0},{2,3},{3,2},{4,5},{5,4},{6,7},{7,6},{8,9},{9,8},{10,11... | collective-permute-start | bytes 3538952 | tf_op jit(solution)/shard_map/ppermute | solution.py:29
  92.5 17.9 %collective-permute-start.8 = (bf16[2,2,1,2,2,24,896]{6,5,4,3,1,0,2:T(8,128)(2,1)S(1)}, bf16[2,2,1,2,2,24,896]{6,5,4,3,1,0,2:T(8,128)(2,1)S(1)}, u32[]{:S(2)}, u32[]{:S(2)}) collective-permute-start(bf16[2,2,1,2,2,24,896]{6,5,4,3,1,0,2:T(8,128)(2,1)S(1)} %broadcast_select_fusion), channel_id=1, source_target_pairs={{0,4},{4,0},{8,12},{12,8},{16,20},{20,16},{24,28},{28,24},{1,5},{5... | collective-permute-start | bytes 2064392 | tf_op jit(solution)/shard_map/ppermute | solution.py:29
  112.6 13.6 %collective-permute-start.11 = (bf16[768,896]{1,0:T(8,128)(2,1)S(1)}, bf16[768,896]{1,0:T(8,128)(2,1)}, u32[]{:S(2)}, u32[]{:S(2)}) collective-permute-start(bf16[768,896]{1,0:T(8,128)(2,1)S(1)} %bitcast_select_fusion), channel_id=1, source_target_pairs={{0,1},{1,0},{2,3},{3,2},{4,5},{5,4},{6,7},{7,6},{8,9},{9,8},{10,11... | collective-permute-start | bytes 4128776 | tf_op jit(solution)/shard_map/ppermute | solution.py:29
  112.7 12.2 %collective-permute-start.1 = (bf16[128,768]{1,0:T(8,128)(2,1)}, bf16[128,768]{1,0:T(8,128)(2,1)S(1)}, u32[]{:S(2)}, u32[]{:S(2)}) collective-permute-start(bf16[128,768]{1,0:T(8,128)(2,1)} %get-tuple-element.147), channel_id=1, source_target_pairs={{0,2},{1,3},{2,0},{3,1},{4,6},{5,7},{6,4},{7,5},{8,10},{9,11},{10,... | collective-permute-start | bytes 589832 | tf_op jit(solution)/shard_map/ppermute | solution.py:29
  132.7 6.2 %collective-permute-start.12 = (bf16[256,1536]{1,0:T(8,128)(2,1)S(1)}, bf16[256,1536]{1,0:T(8,128)(2,1)}, u32[]{:S(2)}, u32[]{:S(2)}) collective-permute-start(bf16[256,1536]{1,0:T(8,128)(2,1)S(1)} %pad_maximum_fusion.11.key_own.value_own), channel_id=1, source_target_pairs={{0,1},{1,0},{2,3},{3,2},{4,5},{5,4},{6,7},{7,6},{8,9},{9,8},{10,11... | collective-permute-start | bytes 2359304 | tf_op jit(solution)/shard_map/ppermute | solution.py:29
  137.5 9.7 %copy-start.50 = (bf16[768,384]{1,0:T(8,128)(2,1)}, bf16[768,384]{1,0:T(8,128)(2,1)S(1)}, u32[]{:S(2)}) copy-start(bf16[768,384]{1,0:T(8,128)(2,1)S(1)} %get-tuple-element.321) | copy-start | bytes 1769476
  148.8 58.6 %copy-start.73 = (f32[256]{0:T(256)}, f32[256]{0:T(256)S(1)}, u32[]{:S(2)}) copy-start(f32[256]{0:T(256)S(1)} %broadcast_multiply_fusion.11) | copy-start | bytes 3076
  149.0 58.4 %copy-start.84 = (f32[256]{0:T(256)}, f32[256]{0:T(256)S(1)}, u32[]{:S(2)}) copy-start(f32[256]{0:T(256)S(1)} %add_rsqrt_fusion.3) | copy-start | bytes 3076
  149.2 55.3 %copy-start.14 = (bf16[256,768]{1,0:T(8,128)(2,1)}, bf16[256,768]{1,0:T(8,128)(2,1)S(1)}, u32[]{:S(2)}) copy-start(bf16[256,768]{1,0:T(8,128)(2,1)S(1)} %fusion.72) | copy-start | bytes 1179652
  209.0 17.2 %copy-start.71 = (f32[256]{0:T(256)}, f32[256]{0:T(256)S(1)}, u32[]{:S(2)}) copy-start(f32[256]{0:T(256)S(1)} %broadcast_multiply_fusion.10) | copy-start | bytes 3076
  209.2 17.0 %copy-start.75 = (f32[256]{0:T(256)}, f32[256]{0:T(256)S(1)}, u32[]{:S(2)}) copy-start(f32[256]{0:T(256)S(1)} %add_rsqrt_fusion.2) | copy-start | bytes 3076
  213.0 4.5 collective-permute-start.13
  213.4 26.3 %collective-permute-start.15 = (bf16[128,768]{1,0:T(8,128)(2,1)}, bf16[128,768]{1,0:T(8,128)(2,1)S(1)}, u32[]{:S(2)}, u32[]{:S(2)}) collective-permute-start(bf16[128,768]{1,0:T(8,128)(2,1)} %get-tuple-element.150), channel_id=1, source_target_pairs={{0,2},{1,3},{2,0},{3,1},{4,6},{5,7},{6,4},{7,5},{8,10},{9,11},{10,... | collective-permute-start | bytes 589832 | tf_op jit(solution)/shard_map/ppermute | solution.py:29
  228.2 9.6 %copy-start.1 = (f32[256,768]{1,0:T(8,128)}, f32[256,768]{1,0:T(8,128)S(1)}, u32[]{:S(2)}) copy-start(f32[256,768]{1,0:T(8,128)S(1)} %get-tuple-element.432) | copy-start | bytes 2359300
  228.2 9.6 %copy-start.77 = (f32[256]{0:T(256)}, f32[256]{0:T(256)S(1)}, u32[]{:S(2)}) copy-start(f32[256]{0:T(256)S(1)} %broadcast_multiply_fusion.9) | copy-start | bytes 3076
  291.4 9.1 %collective-permute-start.16 = (bf16[2,256,768]{2,1,0:T(8,128)(2,1)}, bf16[2,256,768]{2,1,0:T(8,128)(2,1)}, u32[]{:S(2)}, u32[]{:S(2)}) collective-permute-start(bf16[2,256,768]{2,1,0:T(8,128)(2,1)} %get-tuple-element.177), channel_id=1, source_target_pairs={{0,1},{1,0},{2,3},{3,2},{4,5},{5,4},{6,7},{7,6},{8,9},{9,8},{10,11... | collective-permute-start | bytes 2359304 | tf_op jit(solution)/shard_map/ppermute | solution.py:29
  292.2 7.4 %collective-permute-start.14 = (bf16[128,768]{1,0:T(8,128)(2,1)S(1)}, bf16[128,768]{1,0:T(8,128)(2,1)S(1)}, u32[]{:S(2)}, u32[]{:S(2)}) collective-permute-start(bf16[128,768]{1,0:T(8,128)(2,1)S(1)} %slice.594), channel_id=1, source_target_pairs={{0,2},{1,3},{2,0},{3,1},{4,6},{5,7},{6,4},{7,5},{8,10},{9,11},{10,... | collective-permute-start | bytes 589832 | tf_op jit(solution)/shard_map/ppermute | solution.py:29
  299.6 5.8 %collective-permute-start.17 = (bf16[768,768]{0,1:T(8,128)(2,1)S(1)}, bf16[768,768]{0,1:T(8,128)(2,1)}, u32[]{:S(2)}, u32[]{:S(2)}) collective-permute-start(bf16[768,768]{0,1:T(8,128)(2,1)S(1)} %pad_maximum_fusion.10), channel_id=1, source_target_pairs={{0,1},{1,0},{2,3},{3,2},{4,5},{5,4},{6,7},{7,6},{8,9},{9,8},{10,11... | collective-permute-start | bytes 3538952 | tf_op jit(solution)/shard_map/ppermute | solution.py:29
  305.3 12.0 %collective-permute-start.18 = (bf16[768,768]{1,0:T(8,128)(2,1)}, bf16[768,768]{1,0:T(8,128)(2,1)}, u32[]{:S(2)}, u32[]{:S(2)}) collective-permute-start(bf16[768,768]{1,0:T(8,128)(2,1)} %convolution_convert_fusion.6), channel_id=1, source_target_pairs={{0,1},{1,0},{2,3},{3,2},{4,5},{5,4},{6,7},{7,6},{8,9},{9,8},{10,11... | collective-permute-start | bytes 3538952 | tf_op jit(solution)/shard_map/ppermute | solution.py:29
  317.4 18.0 %collective-permute-start.20 = (bf16[1,2,2,2,1,48,768]{6,5,4,3,2,1,0:T(8,128)(2,1)S(1)}, bf16[1,2,2,2,1,48,768]{6,5,4,3,2,1,0:T(8,128)(2,1)S(1)}, u32[]{:S(2)}, u32[]{:S(2)}) collective-permute-start(bf16[1,2,2,2,1,48,768]{6,5,4,3,2,1,0:T(8,128)(2,1)S(1)} %get-tuple-element.194), channel_id=1, source_target_pairs={{0,2},{1,3},{2,0},{3,1},{4,6},{5,7},{6,4},{7,5},{8,10},{9,11},{10,... | collective-permute-start | bytes 1769480 | tf_op jit(solution)/shard_map/ppermute | solution.py:29
  319.5 16.9 %collective-permute-start.21 = (bf16[1,2,2,1,2,48,768]{6,5,4,3,2,1,0:T(8,128)(2,1)S(1)}, bf16[1,2,2,1,2,48,768]{6,5,4,3,2,1,0:T(8,128)(2,1)S(1)}, u32[]{:S(2)}, u32[]{:S(2)}) collective-permute-start(bf16[1,2,2,1,2,48,768]{6,5,4,3,2,1,0:T(8,128)(2,1)S(1)} %get-tuple-element.195), channel_id=1, source_target_pairs={{0,4},{4,0},{8,12},{12,8},{16,20},{20,16},{24,28},{28,24},{1,5},{5... | collective-permute-start | bytes 1769480 | tf_op jit(solution)/shard_map/ppermute | solution.py:29
  324.2 13.1 %collective-permute-start.19 = (bf16[3072,384]{1,0:T(8,128)(2,1)S(1)}, bf16[3072,384]{1,0:T(8,128)(2,1)S(1)}, u32[]{:S(2)}, u32[]{:S(2)}) collective-permute-start(bf16[3072,384]{1,0:T(8,128)(2,1)S(1)} %convolution_convert_fusion), channel_id=1, source_target_pairs={{0,1},{1,0},{2,3},{3,2},{4,5},{5,4},{6,7},{7,6},{8,9},{9,8},{10,11... | collective-permute-start | bytes 7077896 | tf_op jit(solution)/shard_map/ppermute | solution.py:29
  340.1 38.3 %collective-permute-start.22 = (bf16[768,1536]{1,0:T(8,128)(2,1)S(1)}, bf16[768,1536]{1,0:T(8,128)(2,1)S(1)}, u32[]{:S(2)}, u32[]{:S(2)}) collective-permute-start(bf16[768,1536]{1,0:T(8,128)(2,1)S(1)} %convolution_convert_fusion.2), channel_id=1, source_target_pairs={{0,1},{1,0},{2,3},{3,2},{4,5},{5,4},{6,7},{7,6},{8,9},{9,8},{10,11... | collective-permute-start | bytes 7077896 | tf_op jit(solution)/shard_map/ppermute | solution.py:29
  340.6 36.4 %collective-permute-start.28 = (bf16[4,2,2,1,2,48,384]{6,5,4,3,2,1,0:T(8,128)(2,1)S(1)}, bf16[4,2,2,1,2,48,384]{6,5,4,3,2,1,0:T(8,128)(2,1)S(1)}, u32[]{:S(2)}, u32[]{:S(2)}) collective-permute-start(bf16[4,2,2,1,2,48,384]{6,5,4,3,2,1,0:T(8,128)(2,1)S(1)} %get-tuple-element.222), channel_id=1, source_target_pairs={{0,4},{4,0},{8,12},{12,8},{16,20},{20,16},{24,28},{28,24},{1,5},{5... | collective-permute-start | bytes 3538952 | tf_op jit(solution)/shard_map/ppermute | solution.py:29
  390.8 12.1 %collective-permute-start.23 = (bf16[2,256,768]{2,1,0:T(8,128)(2,1)}, bf16[2,256,768]{2,1,0:T(8,128)(2,1)S(1)}, u32[]{:S(2)}, u32[]{:S(2)}) collective-permute-start(bf16[2,256,768]{2,1,0:T(8,128)(2,1)} %get-tuple-element.210), channel_id=1, source_target_pairs={{0,1},{1,0},{2,3},{3,2},{4,5},{5,4},{6,7},{7,6},{8,9},{9,8},{10,11... | collective-permute-start | bytes 2359304 | tf_op jit(solution)/shard_map/ppermute | solution.py:29
  390.9 10.1 %collective-permute-start.25 = (bf16[1,2,2,1,1,48,768]{6,5,4,3,2,1,0:T(8,128)(2,1)}, bf16[1,2,2,1,1,48,768]{6,5,4,3,2,1,0:T(8,128)(2,1)S(1)}, u32[]{:S(2)}, u32[]{:S(2)}) collective-permute-start(bf16[1,2,2,1,1,48,768]{6,5,4,3,2,1,0:T(8,128)(2,1)} %get-tuple-element.215), channel_id=1, source_target_pairs={{0,2},{1,3},{2,0},{3,1},{4,6},{5,7},{6,4},{7,5},{8,10},{9,11},{10,... | collective-permute-start | bytes 884744 | tf_op jit(solution)/shard_map/ppermute | solution.py:29
  392.6 39.7 %collective-permute-start.26 = (bf16[1,2,2,2,1,48,1536]{6,5,4,3,2,1,0:T(8,128)(2,1)}, bf16[1,2,2,2,1,48,1536]{6,5,4,3,2,1,0:T(8,128)(2,1)}, u32[]{:S(2)}, u32[]{:S(2)}) collective-permute-start(bf16[1,2,2,2,1,48,1536]{6,5,4,3,2,1,0:T(8,128)(2,1)} %get-tuple-element.218), channel_id=1, source_target_pairs={{0,2},{1,3},{2,0},{3,1},{4,6},{5,7},{6,4},{7,5},{8,10},{9,11},{10,... | collective-permute-start | bytes 3538952 | tf_op jit(solution)/shard_map/ppermute | solution.py:29
  393.0 9.1 %collective-permute-start.27 = (bf16[1,2,2,1,1,48,768]{6,5,4,3,2,1,0:T(8,128)(2,1)}, bf16[1,2,2,1,1,48,768]{6,5,4,3,2,1,0:T(8,128)(2,1)S(1)}, u32[]{:S(2)}, u32[]{:S(2)}) collective-permute-start(bf16[1,2,2,1,1,48,768]{6,5,4,3,2,1,0:T(8,128)(2,1)} %get-tuple-element.219), channel_id=1, source_target_pairs={{0,4},{4,0},{8,12},{12,8},{16,20},{20,16},{24,28},{28,24},{1,5},{5... | collective-permute-start | bytes 884744 | tf_op jit(solution)/shard_map/ppermute | solution.py:29
  407.8 3.2 collective-permute-start.24
  411.0 25.6 %collective-permute-start.29 = (bf16[768,768]{1,0:T(8,128)(2,1)}, bf16[768,768]{1,0:T(8,128)(2,1)}, u32[]{:S(2)}, u32[]{:S(2)}) collective-permute-start(bf16[768,768]{1,0:T(8,128)(2,1)} %convolution_convert_fusion.4), channel_id=1, source_target_pairs={{0,1},{1,0},{2,3},{3,2},{4,5},{5,4},{6,7},{7,6},{8,9},{9,8},{10,11... | collective-permute-start | bytes 3538952 | tf_op jit(solution)/shard_map/ppermute | solution.py:29
  415.5 16.8 %copy-start.11 = (bf16[1,2,2,2,1,48,1536]{6,5,4,3,2,1,0:T(8,128)(2,1)S(1)}, bf16[1,2,2,2,1,48,1536]{6,5,4,3,2,1,0:T(8,128)(2,1)}, u32[]{:S(2)}) copy-start(bf16[1,2,2,2,1,48,1536]{6,5,4,3,2,1,0:T(8,128)(2,1)} %get-tuple-element.317) | copy-start | bytes 3538948
  438.7 6.8 %collective-permute-start.34 = (bf16[1,2,1,1,1,48,768]{6,5,4,3,2,1,0:T(8,128)(2,1)S(1)}, bf16[1,2,1,1,1,48,768]{6,5,4,3,2,1,0:T(8,128)(2,1)S(1)}, u32[]{:S(2)}, u32[]{:S(2)}) collective-permute-start(bf16[1,2,1,1,1,48,768]{6,5,4,3,2,1,0:T(8,128)(2,1)S(1)} %copy-done.68), channel_id=1, source_target_pairs={{0,8},{4,12},{8,0},{12,4},{16,24},{20,28},{24,16},{28,20},{1,9},{5... | collective-permute-start | bytes 442376 | tf_op jit(solution)/shard_map/ppermute | solution.py:29
  439.4 7.9 %collective-permute-start.33 = (bf16[1,2,1,1,1,48,768]{6,5,4,3,2,1,0:T(8,128)(2,1)S(1)}, bf16[1,2,1,1,1,48,768]{6,5,4,3,2,1,0:T(8,128)(2,1)S(1)}, u32[]{:S(2)}, u32[]{:S(2)}) collective-permute-start(bf16[1,2,1,1,1,48,768]{6,5,4,3,2,1,0:T(8,128)(2,1)S(1)} %copy-done.67), channel_id=1, source_target_pairs={{0,8},{4,12},{8,0},{12,4},{16,24},{20,28},{24,16},{28,20},{1,9},{5... | collective-permute-start | bytes 442376 | tf_op jit(solution)/shard_map/ppermute | solution.py:29
  440.8 17.8 %copy-start.21 = (bf16[4,2,2,1,1,48,384]{6,5,4,3,2,1,0:T(8,128)(2,1)S(1)}, bf16[4,2,2,1,1,48,384]{6,5,4,3,2,1,0:T(8,128)(2,1)}, u32[]{:S(2)}) copy-start(bf16[4,2,2,1,1,48,384]{6,5,4,3,2,1,0:T(8,128)(2,1)} %get-tuple-element.327) | copy-start | bytes 1769476
  441.1 28.8 %collective-permute-start.31 = (bf16[1,2,2,1,1,48,1536]{6,5,4,3,2,1,0:T(8,128)(2,1)S(1)}, bf16[1,2,2,1,1,48,1536]{6,5,4,3,2,1,0:T(8,128)(2,1)S(1)}, u32[]{:S(2)}, u32[]{:S(2)}) collective-permute-start(bf16[1,2,2,1,1,48,1536]{6,5,4,3,2,1,0:T(8,128)(2,1)S(1)} %get-tuple-element.230), channel_id=1, source_target_pairs={{0,4},{4,0},{8,12},{12,8},{16,20},{20,16},{24,28},{28,24},{1,5},{5... | collective-permute-start | bytes 1769480 | tf_op jit(solution)/shard_map/ppermute | solution.py:29
  441.8 16.7 %collective-permute-start.32 = (bf16[4,2,2,1,1,48,384]{6,5,4,3,2,1,0:T(8,128)(2,1)S(1)}, bf16[4,2,2,1,1,48,384]{6,5,4,3,2,1,0:T(8,128)(2,1)S(1)}, u32[]{:S(2)}, u32[]{:S(2)}) collective-permute-start(bf16[4,2,2,1,1,48,384]{6,5,4,3,2,1,0:T(8,128)(2,1)S(1)} %copy-done.56), channel_id=1, source_target_pairs={{0,2},{1,3},{2,0},{3,1},{4,6},{5,7},{6,4},{7,5},{8,10},{9,11},{10,... | collective-permute-start | bytes 1769480 | tf_op jit(solution)/shard_map/ppermute | solution.py:29
  443.4 24.8 %collective-permute-start.36 = (bf16[1,2,2,1,2,48,768]{6,5,4,3,2,1,0:T(8,128)(2,1)S(1)}, bf16[1,2,2,1,2,48,768]{6,5,4,3,2,1,0:T(8,128)(2,1)S(1)}, u32[]{:S(2)}, u32[]{:S(2)}) collective-permute-start(bf16[1,2,2,1,2,48,768]{6,5,4,3,2,1,0:T(8,128)(2,1)S(1)} %get-tuple-element.227), channel_id=1, source_target_pairs={{0,4},{4,0},{8,12},{12,8},{16,20},{20,16},{24,28},{28,24},{1,5},{5... | collective-permute-start | bytes 1769480 | tf_op jit(solution)/shard_map/ppermute | solution.py:29
  445.5 27.1 %collective-permute-start.30 = (bf16[1,2,2,2,1,48,896]{6,5,4,3,2,1,0:T(8,128)(2,1)S(1)}, bf16[1,2,2,2,1,48,896]{6,5,4,3,2,1,0:T(8,128)(2,1)S(1)}, u32[]{:S(2)}, u32[]{:S(2)}) collective-permute-start(bf16[1,2,2,2,1,48,896]{6,5,4,3,2,1,0:T(8,128)(2,1)S(1)} %get-tuple-element.232), channel_id=1, source_target_pairs={{0,2},{1,3},{2,0},{3,1},{4,6},{5,7},{6,4},{7,5},{8,10},{9,11},{10,... | collective-permute-start | bytes 2064392 | tf_op jit(solution)/shard_map/ppermute | solution.py:29
  447.3 5.8 %collective-permute-start.46 = (bf16[1,1,1,1,1,48,768]{6,5,4,3,2,1,0:T(8,128)(2,1)S(1)}, bf16[1,1,1,1,1,48,768]{6,5,4,3,2,1,0:T(8,128)(2,1)S(1)}, u32[]{:S(2)}, u32[]{:S(2)}) collective-permute-start(bf16[1,1,1,1,1,48,768]{6,5,4,3,2,1,0:T(8,128)(2,1)S(1)} %add_convert_fusion.55), channel_id=1, source_target_pairs={{0,16},{4,20},{8,24},{12,28},{16,0},{20,4},{24,8},{28,12},{1,17},{... | collective-permute-start | bytes 221192 | tf_op jit(solution)/shard_map/ppermute | solution.py:29
  453.1 5.4 %collective-permute-start.47 = (bf16[1,1,1,1,1,48,768]{6,5,4,3,2,1,0:T(8,128)(2,1)S(1)}, bf16[1,1,1,1,1,48,768]{6,5,4,3,2,1,0:T(8,128)(2,1)S(1)}, u32[]{:S(2)}, u32[]{:S(2)}) collective-permute-start(bf16[1,1,1,1,1,48,768]{6,5,4,3,2,1,0:T(8,128)(2,1)S(1)} %add_convert_fusion.56), channel_id=1, source_target_pairs={{0,16},{4,20},{8,24},{12,28},{16,0},{20,4},{24,8},{28,12},{1,17},{... | collective-permute-start | bytes 221192 | tf_op jit(solution)/shard_map/ppermute | solution.py:29
  458.7 11.4 %collective-permute-start.35 = (bf16[4,2,1,1,1,48,384]{6,5,4,3,2,1,0:T(8,128)(2,1)S(1)}, bf16[4,2,1,1,1,48,384]{6,5,4,3,2,1,0:T(8,128)(2,1)S(1)}, u32[]{:S(2)}, u32[]{:S(2)}) collective-permute-start(bf16[4,2,1,1,1,48,384]{6,5,4,3,2,1,0:T(8,128)(2,1)S(1)} %get-tuple-element.241), channel_id=1, source_target_pairs={{0,8},{4,12},{8,0},{12,4},{16,24},{20,28},{24,16},{28,20},{1,9},{5... | collective-permute-start | bytes 884744 | tf_op jit(solution)/shard_map/ppermute | solution.py:29
  468.4 8.9 %collective-permute-start.40 = (bf16[1,2,2,1,1,48,768]{6,5,4,3,2,1,0:T(8,128)(2,1)S(1)}, bf16[1,2,2,1,1,48,768]{6,5,4,3,2,1,0:T(8,128)(2,1)S(1)}, u32[]{:S(2)}, u32[]{:S(2)}) collective-permute-start(bf16[1,2,2,1,1,48,768]{6,5,4,3,2,1,0:T(8,128)(2,1)S(1)} %get-tuple-element.244), channel_id=1, source_target_pairs={{0,2},{1,3},{2,0},{3,1},{4,6},{5,7},{6,4},{7,5},{8,10},{9,11},{10,... | collective-permute-start | bytes 884744 | tf_op jit(solution)/shard_map/ppermute | solution.py:29
  470.2 7.9 %collective-permute-start.49 = (bf16[4,1,1,1,1,48,384]{6,5,4,3,2,1,0:T(8,128)(2,1)S(1)}, bf16[4,1,1,1,1,48,384]{6,5,4,3,2,1,0:T(8,128)(2,1)S(1)}, u32[]{:S(2)}, u32[]{:S(2)}) collective-permute-start(bf16[4,1,1,1,1,48,384]{6,5,4,3,2,1,0:T(8,128)(2,1)S(1)} %add_convert_fusion.40), channel_id=1, source_target_pairs={{0,16},{4,20},{8,24},{12,28},{16,0},{20,4},{24,8},{28,12},{1,17},{... | collective-permute-start | bytes 442376 | tf_op jit(solution)/shard_map/ppermute | solution.py:29
  472.7 8.6 %collective-permute-start.39 = (bf16[1,2,1,1,1,48,1536]{6,5,4,3,2,1,0:T(8,128)(2,1)S(1)}, bf16[1,2,1,1,1,48,1536]{6,5,4,3,2,1,0:T(8,128)(2,1)S(1)}, u32[]{:S(2)}, u32[]{:S(2)}) collective-permute-start(bf16[1,2,1,1,1,48,1536]{6,5,4,3,2,1,0:T(8,128)(2,1)S(1)} %get-tuple-element.246), channel_id=1, source_target_pairs={{0,8},{4,12},{8,0},{12,4},{16,24},{20,28},{24,16},{28,20},{1,9},{5... | collective-permute-start | bytes 884744 | tf_op jit(solution)/shard_map/ppermute | solution.py:29
  473.1 11.3 %collective-permute-start.38 = (bf16[1,2,2,1,1,48,896]{6,5,4,3,2,1,0:T(8,128)(2,1)S(1)}, bf16[1,2,2,1,1,48,896]{6,5,4,3,2,1,0:T(8,128)(2,1)S(1)}, u32[]{:S(2)}, u32[]{:S(2)}) collective-permute-start(bf16[1,2,2,1,1,48,896]{6,5,4,3,2,1,0:T(8,128)(2,1)S(1)} %get-tuple-element.247), channel_id=1, source_target_pairs={{0,4},{4,0},{8,12},{12,8},{16,20},{20,16},{24,28},{28,24},{1,5},{5... | collective-permute-start | bytes 1032200 | tf_op jit(solution)/shard_map/ppermute | solution.py:29
  481.5 7.9 %collective-permute-start.42 = (bf16[1,2,1,1,1,48,768]{6,5,4,3,2,1,0:T(8,128)(2,1)S(1)}, bf16[1,2,1,1,1,48,768]{6,5,4,3,2,1,0:T(8,128)(2,1)S(1)}, u32[]{:S(2)}, u32[]{:S(2)}) collective-permute-start(bf16[1,2,1,1,1,48,768]{6,5,4,3,2,1,0:T(8,128)(2,1)S(1)} %get-tuple-element.252), channel_id=1, source_target_pairs={{0,8},{4,12},{8,0},{12,4},{16,24},{20,28},{24,16},{28,20},{1,9},{5... | collective-permute-start | bytes 442376 | tf_op jit(solution)/shard_map/ppermute | solution.py:29
  481.8 7.6 %collective-permute-start.41 = (bf16[1,1,1,1,1,48,1536]{6,5,4,3,2,1,0:T(8,128)(2,1)S(1)}, bf16[1,1,1,1,1,48,1536]{6,5,4,3,2,1,0:T(8,128)(2,1)S(1)}, u32[]{:S(2)}, u32[]{:S(2)}) collective-permute-start(bf16[1,1,1,1,1,48,1536]{6,5,4,3,2,1,0:T(8,128)(2,1)S(1)} %add_convert_fusion.39), channel_id=1, source_target_pairs={{0,16},{4,20},{8,24},{12,28},{16,0},{20,4},{24,8},{28,12},{1,17},{... | collective-permute-start | bytes 442376 | tf_op jit(solution)/shard_map/ppermute | solution.py:29
  484.4 20.9 %collective-permute-start.50 = (bf16[96,384]{1,0:T(8,128)(2,1)S(1)}, bf16[96,384]{1,0:T(8,128)(2,1)S(1)}, u32[]{:S(2)}, u32[]{:S(2)}) collective-permute-start(bf16[96,384]{1,0:T(8,128)(2,1)S(1)} %get-tuple-element.409), channel_id=1, source_target_pairs={{0,1},{1,0},{2,3},{3,2},{4,5},{5,4},{6,7},{7,6},{8,9},{9,8},{10,11... | collective-permute-start | bytes 221192 | tf_op jit(solution)/shard_map/ppermute | solution.py:29
  484.5 20.0 %collective-permute-start.37 = (bf16[128,768]{1,0:T(8,128)(2,1)S(1)}, bf16[128,768]{1,0:T(8,128)(2,1)S(1)}, u32[]{:S(2)}, u32[]{:S(2)}) collective-permute-start(bf16[128,768]{1,0:T(8,128)(2,1)S(1)} %slice.628), channel_id=1, source_target_pairs={{0,2},{1,3},{2,0},{3,1},{4,6},{5,7},{6,4},{7,5},{8,10},{9,11},{10,... | collective-permute-start | bytes 589832 | tf_op jit(solution)/shard_map/ppermute | solution.py:29
  489.4 9.4 %collective-permute-start.45 = (bf16[1,1,1,1,1,48,768]{6,5,4,3,2,1,0:T(8,128)(2,1)S(1)}, bf16[1,1,1,1,1,48,768]{6,5,4,3,2,1,0:T(8,128)(2,1)S(1)}, u32[]{:S(2)}, u32[]{:S(2)}) collective-permute-start(bf16[1,1,1,1,1,48,768]{6,5,4,3,2,1,0:T(8,128)(2,1)S(1)} %add_convert_fusion.54), channel_id=1, source_target_pairs={{0,16},{4,20},{8,24},{12,28},{16,0},{20,4},{24,8},{28,12},{1,17},{... | collective-permute-start | bytes 221192 | tf_op jit(solution)/shard_map/ppermute | solution.py:29
  490.1 7.1 %collective-permute-start.43 = (bf16[1,2,1,1,1,48,896]{6,5,4,3,2,1,0:T(8,128)(2,1)S(1)}, bf16[1,2,1,1,1,48,896]{6,5,4,3,2,1,0:T(8,128)(2,1)S(1)}, u32[]{:S(2)}, u32[]{:S(2)}) collective-permute-start(bf16[1,2,1,1,1,48,896]{6,5,4,3,2,1,0:T(8,128)(2,1)S(1)} %get-tuple-element.257), channel_id=1, source_target_pairs={{0,8},{4,12},{8,0},{12,4},{16,24},{20,28},{24,16},{28,20},{1,9},{5... | collective-permute-start | bytes 516104 | tf_op jit(solution)/shard_map/ppermute | solution.py:29
  497.2 6.4 %collective-permute-start.44 = (bf16[1,1,1,1,1,48,896]{6,5,4,3,2,1,0:T(8,128)(2,1)S(1)}, bf16[1,1,1,1,1,48,896]{6,5,4,3,2,1,0:T(8,128)(2,1)S(1)}, u32[]{:S(2)}, u32[]{:S(2)}) collective-permute-start(bf16[1,1,1,1,1,48,896]{6,5,4,3,2,1,0:T(8,128)(2,1)S(1)} %add_convert_fusion.46), channel_id=1, source_target_pairs={{0,16},{4,20},{8,24},{12,28},{16,0},{20,4},{24,8},{28,12},{1,17},{... | collective-permute-start | bytes 258056 | tf_op jit(solution)/shard_map/ppermute | solution.py:29
  504.5 1.5 collective-permute-start.48
  (99 other events, 321.6 us)
Sparse Core Ops, SparseCore 0:
  11.9 177.7 all-gather.1
  292.8 146.7 reduce-scatter.1

commit v3 on v2

--- a/solution.py
+++ b/solution.py
@@ -193,7 +193,7 @@
 
 
 class Pump:
-    def __init__(self, depth=2):
+    def __init__(self, depth=3):
         self.now = 0.0
         self.depth = depth
         self.flying = []

time: 530 us -> 541 us (1.021)
  other arithmetic: 43.5 us -> 52.4 us
    convert_element_type x24, other arithmetic: 16.3 us -> 25.2 us  [part(): return (cut[0].astype(FULL) + cut[1].astype(FULL)).astype(LOW)]
    unnamed x225 -> x247, local copies, waits for them, and re-layouts: 8.72 us -> 10.9 us
  transfers between devices with their start and end apart: 53 -> 53, of which waited for: 28 -> 26; matrix products, arithmetic and copies ran while one was open for 23% -> 24% of each run, Pallas kernels for 6% -> 6%
where the time goes in v3:
time: 541 us; the launch traced here: 534 us
  waiting for transfers between devices  199 us (37%)
  matrix products  107 us (20%)
  Pallas kernels  61.9 us (11%)
  starting transfers between devices  55.3 us (10%)
  other arithmetic  52.4 us (10%)
  local copies, waits for them, and re-layouts  42 us (8%)
  between operations  16.5 us (3%)
    ppermute x51, waiting for transfers between devices, swap(): return lax.ppermute(value, name, pairs)  158 us
    ppermute x51, starting transfers between devices, swap(): return lax.ppermute(value, name, pairs)  55.2 us
    dot_general x28, matrix products, matmul(): return jnp.dot(left, right, preferred_element_type=FULL)  44.5 us
    dot_general x24, matrix products, right_t(): return jnp.einsum('ra,ba->rb', left, right, preferred_element_type=FULL)  43.6 us
    all_gather x1, waiting for transfers between devices, body(): whole = lax.all_gather(shard, ('wide', 'narrow'), axis=1, tiled=True)  40.4 us
    convert_element_type x24, other arithmetic, part(): return (cut[0].astype(FULL) + cut[1].astype(FULL)).astype(LOW)  25.2 us
    dot_general x16, matrix products, left_t(): return jnp.einsum('ra,rb->ab', left, right, preferred_element_type=FULL)  18.7 us
    pallas_call x2, Pallas kernels, attend_back(): pl.pallas_call(attend_back_kernel, grid=(BLOCKS,), in_specs=[plain] + key...  18 us
  transfers between devices with their start and end apart: 53, of which 26 were waited for; matrix products, arithmetic and copies ran while one was open for 24% of the time, Pallas kernels for 6%

profile of v3, /device:TPU:0, one launch (start us, length us, event | category | flops | bytes accessed | tf_op | source)
XLA Modules:
  0.0 533.6 jit_solution(7908381061072785635)
XLA Ops:
  7.3 4.5 shard_map.314
  16.1 3.6 collective-permute-start.3
  19.8 4.8 collective-permute-done.3
  25.6 5.6 %collective-permute-start.5 = (bf16[2,1,1,1,2,24,768]{6,5,4,0,3,2,1:T(8,128)(2,1)S(1)}, bf16[2,1,1,1,2,24,768]{6,5,4,0,3,2,1:T(8,128)(2,1)S(1)}, u32[]{:S(2)}, u32[]{:S(2)}) collective-permute-start(bf16[2,1,1,1,2,24,768]{6,5,4,0,3,2,1:T(8,128)(2,1)S(1)} %broadcast_select_fusion.15), channel_id=1, source_target_pairs={{0,8},{4,12},{8,0},{12,4},{16,24},{20,28},{24,16},{28,20},{1,9},{5... | collective-permute-start | bytes 442376 | tf_op jit(solution)/shard_map/ppermute | solution.py:29
  32.2 4.9 collective-permute-start.4
  37.0 7.3 %collective-permute-done.5 = bf16[2,1,1,1,2,24,768]{6,5,4,0,3,2,1:T(8,128)(2,1)S(1)} collective-permute-done((bf16[2,1,1,1,2,24,768]{6,5,4,0,3,2,1:T(8,128)(2,1)S(1)}, bf16[2,1,1,1,2,24,768]{6,5,4,0,3,2,1:T(8,128)(2,1)S(1)}, u32[]{:S(2)}, u32[]{:S(2)}) %collective-permute-start.5) | collective-permute-done | bytes 147488 | tf_op jit(solution)/shard_map/ppermute | solution.py:29
  45.5 5.1 collective-permute-done.4
  53.6 12.6 %collective-permute-done.6 = bf16[2,2,1,1,2,24,896]{6,5,4,1,0,3,2:T(8,128)(2,1)S(1)} collective-permute-done((bf16[2,2,1,1,2,24,896]{6,5,4,1,0,3,2:T(8,128)(2,1)S(1)}, bf16[2,2,1,1,2,24,896]{6,5,4,1,0,3,2:T(8,128)(2,1)S(1)}, u32[]{:S(2)}, u32[]{:S(2)}) %collective-permute-start.6) | collective-permute-done | bytes 344096 | tf_op jit(solution)/shard_map/ppermute | solution.py:29
  66.3 24.0 %collective-permute-done.9 = bf16[2,2,2,1,2,24,768]{6,5,4,2,1,0,3:T(8,128)(2,1)S(1)} collective-permute-done((bf16[2,2,2,1,2,24,768]{6,5,4,2,1,0,3:T(8,128)(2,1)S(1)}, bf16[2,2,2,1,2,24,768]{6,5,4,2,1,0,3:T(8,128)(2,1)S(1)}, u32[]{:S(2)}, u32[]{:S(2)}) %collective-permute-start.9) | collective-permute-done | bytes 589856 | tf_op jit(solution)/shard_map/ppermute | solution.py:29
  94.0 16.3 %collective-permute-done.8 = bf16[2,2,1,2,2,24,896]{6,5,4,3,1,0,2:T(8,128)(2,1)S(1)} collective-permute-done((bf16[2,2,1,2,2,24,896]{6,5,4,3,1,0,2:T(8,128)(2,1)S(1)}, bf16[2,2,1,2,2,24,896]{6,5,4,3,1,0,2:T(8,128)(2,1)S(1)}, u32[]{:S(2)}, u32[]{:S(2)}) %collective-permute-start.8) | collective-permute-done | bytes 688160 | tf_op jit(solution)/shard_map/ppermute | solution.py:29
  112.7 2.5 collective-permute-start.1
  115.9 2.9 broadcast_select_fusion.7
  118.8 6.1 %collective-permute-done.1 = bf16[128,768]{1,0:T(8,128)(2,1)S(1)} collective-permute-done((bf16[128,768]{1,0:T(8,128)(2,1)}, bf16[128,768]{1,0:T(8,128)(2,1)S(1)}, u32[]{:S(2)}, u32[]{:S(2)}) %collective-permute-start.1) | collective-permute-done | bytes 196640 | tf_op jit(solution)/shard_map/ppermute | solution.py:29
  127.8 2.1 shard_map.316
  135.2 2.3 broadcast_select_fusion.3
  138.9 8.3 %shard_map.317 = (bf16[256,768]{1,0:T(8,128)(2,1)}, bf16[6,512,512]{2,1,0:T(8,128)(2,1)}) custom-call(s32[5]{0:T(128)} %stack.38.meta, bf16[256,768]{1,0:T(8,128)(2,1)} %fusion.7.query, bf16[256,1536]{1,0:T(8,128)(2,1)} %copy-done.38, bf16[256,1536]{1,0:T(8,128)(2,1)} %copy-done.38, bf16[256,1536]{1,0:T(8,128)(2,1)} %collective-permute-done.12.key_other.value_other, ...), custom_call_target="tpu_custom_call" | custom-call | flops 1610612736 | bytes 3145728 | tf_op jit(solution)/shard_map/pallas_call | solution.py:325
  149.2 40.4 %all-gather.2.cloned.1.call-done = bf16[20,768,768]{2,1,0:T(8,128)(2,1)} async-done(((bf16[20,24,768]{2,1,0:T(8,128)(2,1)}), bf16[20,768,768]{2,1,0:T(8,128)(2,1)}) %all-gather.2.cloned.1.call-update) | async-done | bytes 23592976 | tf_op jit(solution)/shard_map/all_gather | solution.py:846
  189.7 6.6 %fusion.154 = (bf16[4,768,768]{2,1,0:T(8,128)(2,1)S(1)}, bf16[4,768,768]{2,1,0:T(8,128)(2,1)}) fusion(bf16[20,768,768]{2,1,0:T(8,128)(2,1)} %all-gather.2.cloned.1.call-done), kind=kLoop, calls=%fused_computation.451 | loop fusion | bytes 18874368 | tf_op jit(solution)/shard_map/slice | solution.py:891
  196.2 2.7 multiply_convert_fusion.4
  198.9 2.8 multiply_convert_fusion.5
  201.8 2.9 multiply_convert_fusion.6
  204.6 2.8 multiply_convert_fusion.7
  215.1 2.5 fusion.9.query
  217.6 8.6 %shard_map.318 = (bf16[256,768]{1,0:T(8,128)(2,1)}, bf16[6,512,512]{2,1,0:T(8,128)(2,1)}) custom-call(s32[5]{0:T(128)} %stack.38.meta, bf16[256,768]{1,0:T(8,128)(2,1)} %fusion.9.query, bf16[256,1536]{1,0:T(8,128)(2,1)} %copy-done.39, bf16[256,1536]{1,0:T(8,128)(2,1)} %copy-done.39, bf16[256,1536]{1,0:T(8,128)(2,1)} %collective-permute-done.13.key_other.value_other, ...), custom_call_target="tpu_custom_call" | custom-call | flops 1610612736 | bytes 3145728 | tf_op jit(solution)/shard_map/pallas_call | solution.py:325
  226.3 2.0 fusion.172
  228.7 2.0 multiply_convert_fusion
  230.7 2.0 multiply_convert_fusion.1
  241.8 2.0 fusion.14
  250.8 9.6 %shard_map.319 = bf16[768,6144]{1,0:T(8,128)(2,1)} custom-call(bf16[256,768]{1,0:T(8,128)(2,1)} %copy-done.28, bf16[256,3072]{1,0:T(8,128)(2,1)} %pad_maximum_fusion.1.act_ref, bf16[256,3072]{1,0:T(8,128)(2,1)} %pad_maximum_fusion.2.up_ref, bf16[256,768]{1,0:T(8,128)(2,1)} %copy-done.11), custom_call_target="tpu_custom_call" | custom-call | flops 2415919104 | bytes 9437184 | tf_op jit(solution)/shard_map/pallas_call | solution.py:792
  260.3 2.2 convolution_add_fusion.9
  266.2 2.6 multiply_reduce_fusion.2
  270.8 2.6 convolution_convert_fusion.17.mixed_grad
  273.4 9.0 %shard_map.320 = (bf16[256,768]{1,0:T(8,128)(2,1)}, bf16[2,256,768]{2,1,0:T(8,128)(2,1)}, bf16[2,256,768]{2,1,0:T(8,128)(2,1)}) custom-call(bf16[256,768]{1,0:T(8,128)(2,1)} %fusion.9.query, bf16[256,1536]{1,0:T(8,128)(2,1)} %copy-done.39, bf16[256,1536]{1,0:T(8,128)(2,1)} %copy-done.39, bf16[256,1536]{1,0:T(8,128)(2,1)} %collective-permute-done.13.key_other.value_other, ...), custom_call_target="tpu_custom_call" | custom-call | flops 3221225472 | bytes 6291456 | tf_op jit(solution)/shard_map/pallas_call | solution.py:383
  310.1 1.9 fusion.22
  324.3 2.0 fusion.18
  326.3 1.9 fusion.17
  328.3 2.0 fusion.16
  346.4 2.0 multiply_reduce_fusion.1
  351.6 25.3 %collective-permute-done.28 = bf16[4,2,2,1,2,48,384]{6,5,4,3,2,1,0:T(8,128)(2,1)S(1)} collective-permute-done((bf16[4,2,2,1,2,48,384]{6,5,4,3,2,1,0:T(8,128)(2,1)S(1)}, bf16[4,2,2,1,2,48,384]{6,5,4,3,2,1,0:T(8,128)(2,1)S(1)}, u32[]{:S(2)}, u32[]{:S(2)}) %collective-permute-start.28) | collective-permute-done | bytes 1179680 | tf_op jit(solution)/shard_map/ppermute | solution.py:29
  378.3 2.4 add_convert_fusion
  381.9 9.0 %shard_map.321 = (bf16[256,768]{1,0:T(8,128)(2,1)}, bf16[2,256,768]{2,1,0:T(8,128)(2,1)}, bf16[2,256,768]{2,1,0:T(8,128)(2,1)}) custom-call(bf16[256,768]{1,0:T(8,128)(2,1)} %fusion.7.query, bf16[256,1536]{1,0:T(8,128)(2,1)} %copy-done.38, bf16[256,1536]{1,0:T(8,128)(2,1)} %copy-done.38, bf16[256,1536]{1,0:T(8,128)(2,1)} %collective-permute-done.12.key_other.value_other, ...), custom_call_target="tpu_custom_call" | custom-call | flops 3221225472 | bytes 6291456 | tf_op jit(solution)/shard_map/pallas_call | solution.py:383
  409.9 2.1 add_convert_fusion.42
  418.1 12.6 %collective-permute-done.29 = bf16[1,2,2,2,1,48,1536]{6,5,4,3,2,1,0:T(8,128)(2,1)} collective-permute-done((bf16[1,2,2,2,1,48,1536]{6,5,4,3,2,1,0:T(8,128)(2,1)}, bf16[1,2,2,2,1,48,1536]{6,5,4,3,2,1,0:T(8,128)(2,1)}, u32[]{:S(2)}, u32[]{:S(2)}) %collective-permute-start.29) | collective-permute-done | bytes 1179680 | tf_op jit(solution)/shard_map/ppermute | solution.py:29
  430.7 2.6 add_convert_fusion.9
  433.3 2.7 copy.48
  436.0 2.9 add_convert_fusion.6
  439.0 2.6 add_convert_fusion.8
  442.2 2.6 collective-permute-start.35
  444.8 2.0 collective-permute-start.32
  448.2 4.0 collective-permute-done.32
  455.7 2.3 collective-permute-done.36
  459.3 2.1 collective-permute-start.46
  463.5 2.9 collective-permute-start.47
  466.6 2.3 collective-permute-done.37
  469.1 4.9 collective-permute-done.31
  478.0 2.0 collective-permute-start.39
  480.0 5.3 %collective-permute-done.40 = bf16[1,2,1,1,1,48,1536]{6,5,4,3,2,1,0:T(8,128)(2,1)S(1)} collective-permute-done((bf16[1,2,1,1,1,48,1536]{6,5,4,3,2,1,0:T(8,128)(2,1)S(1)}, bf16[1,2,1,1,1,48,1536]{6,5,4,3,2,1,0:T(8,128)(2,1)S(1)}, u32[]{:S(2)}, u32[]{:S(2)}) %collective-permute-start.40) | collective-permute-done | bytes 294944 | tf_op jit(solution)/shard_map/ppermute | solution.py:29
  485.8 3.0 collective-permute-done.39
  489.1 3.1 collective-permute-start.49
  492.2 4.7 collective-permute-done.43
  498.6 3.8 collective-permute-done.49
  503.3 5.1 collective-permute-done.44
  508.5 5.5 %collective-permute-done.45 = bf16[1,1,1,1,1,48,768]{6,5,4,3,2,1,0:T(8,128)(2,1)S(1)} collective-permute-done((bf16[1,1,1,1,1,48,768]{6,5,4,3,2,1,0:T(8,128)(2,1)S(1)}, bf16[1,1,1,1,1,48,768]{6,5,4,3,2,1,0:T(8,128)(2,1)S(1)}, u32[]{:S(2)}, u32[]{:S(2)}) %collective-permute-start.45) | collective-permute-done | bytes 73760 | tf_op jit(solution)/shard_map/ppermute | solution.py:29
  517.7 5.7 %shard_map.324 = (f32[2,24,768]{2,1,0:T(8,128)}, f32[2,24,768]{2,1,0:T(8,128)}, f32[2,24,768]{2,1,0:T(8,128)}, f32[2,24,768]{2,1,0:T(8,128)}, f32[2,24,3072]{2,1...) custom-call(s32[1]{0:T(128)} %bitcast.2.core_ref, ...), custom_call_target="tpu_custom_call" | custom-call | tf_op jit(solution)/shard_map/pallas_call | solution.py:763
  (519 shorter events, 167.8 us)
Async XLA Ops:
  7.2 182.5 %all-gather.2.cloned.1.call-start = ((), (), s32[]{:S(2)}) async-start(), calls=%async_computation.1 | async-start | bytes 24330240 | tf_op jit(solution)/shard_map/all_gather | solution.py:846
  11.8 441.8 %reduce-scatter.2.cloned.1.call-start = ((), (), s32[]{:S(2)}) async-start(), calls=%async_computation.2 | async-start | bytes 9732096 | tf_op jit(solution)/shard_map/reduce_scatter | solution.py:512
  11.8 2.1 collective-permute-start
  13.0 227.6 %copy-start.27 = (bf16[128,768]{1,0:T(8,128)(2,1)}, bf16[128,768]{1,0:T(8,128)(2,1)S(1)}, u32[]{:S(2)}) copy-start(bf16[128,768]{1,0:T(8,128)(2,1)S(1)} %get-tuple-element.413) | copy-start | bytes 589828
  16.1 8.5 %collective-permute-start.3 = (bf16[1,1,1,1,2,24,768]{6,5,4,3,2,1,0:T(8,128)(2,1)}, bf16[1,1,1,1,2,24,768]{6,5,4,3,2,1,0:T(8,128)(2,1)S(1)}, u32[]{:S(2)}, u32[]{:S(2)}) collective-permute-start(bf16[1,1,1,1,2,24,768]{6,5,4,3,2,1,0:T(8,128)(2,1)} %bitcast.290), channel_id=1, source_target_pairs={{0,16},{4,20},{8,24},{12,28},{16,0},{20,4},{24,8},{28,12},{1,17},{... | collective-permute-start | bytes 221192 | tf_op jit(solution)/shard_map/ppermute | solution.py:29
  19.7 11.5 %collective-permute-start.2 = (bf16[1,1,1,1,2,24,896]{6,5,4,3,2,1,0:T(8,128)(2,1)}, bf16[1,1,1,1,2,24,896]{6,5,4,3,2,1,0:T(8,128)(2,1)S(1)}, u32[]{:S(2)}, u32[]{:S(2)}) collective-permute-start(bf16[1,1,1,1,2,24,896]{6,5,4,3,2,1,0:T(8,128)(2,1)} %bitcast.288), channel_id=1, source_target_pairs={{0,16},{4,20},{8,24},{12,28},{16,0},{20,4},{24,8},{28,12},{1,17},{... | collective-permute-start | bytes 258056 | tf_op jit(solution)/shard_map/ppermute | solution.py:29
  25.6 18.8 %collective-permute-start.5 = (bf16[2,1,1,1,2,24,768]{6,5,4,0,3,2,1:T(8,128)(2,1)S(1)}, bf16[2,1,1,1,2,24,768]{6,5,4,0,3,2,1:T(8,128)(2,1)S(1)}, u32[]{:S(2)}, u32[]{:S(2)}) collective-permute-start(bf16[2,1,1,1,2,24,768]{6,5,4,0,3,2,1:T(8,128)(2,1)S(1)} %broadcast_select_fusion.15), channel_id=1, source_target_pairs={{0,8},{4,12},{8,0},{12,4},{16,24},{20,28},{24,16},{28,20},{1,9},{5... | collective-permute-start | bytes 442376 | tf_op jit(solution)/shard_map/ppermute | solution.py:29
  32.2 18.5 %collective-permute-start.4 = (bf16[2,1,1,1,2,24,896]{6,5,4,0,3,2,1:T(8,128)(2,1)S(1)}, bf16[2,1,1,1,2,24,896]{6,5,4,0,3,2,1:T(8,128)(2,1)S(1)}, u32[]{:S(2)}, u32[]{:S(2)}) collective-permute-start(bf16[2,1,1,1,2,24,896]{6,5,4,0,3,2,1:T(8,128)(2,1)S(1)} %broadcast_select_fusion.14), channel_id=1, source_target_pairs={{0,8},{4,12},{8,0},{12,4},{16,24},{20,28},{24,16},{28,20},{1,9},{5... | collective-permute-start | bytes 516104 | tf_op jit(solution)/shard_map/ppermute | solution.py:29
  44.5 8.1 %collective-permute-start.7 = (bf16[2,2,1,1,2,24,768]{6,5,4,1,0,3,2:T(8,128)(2,1)S(1)}, bf16[2,2,1,1,2,24,768]{6,5,4,1,0,3,2:T(8,128)(2,1)S(1)}, u32[]{:S(2)}, u32[]{:S(2)}) collective-permute-start(bf16[2,2,1,1,2,24,768]{6,5,4,1,0,3,2:T(8,128)(2,1)S(1)} %broadcast_select_fusion.11), channel_id=1, source_target_pairs={{0,4},{4,0},{8,12},{12,8},{16,20},{20,16},{24,28},{28,24},{1,5},{5... | collective-permute-start | bytes 884744 | tf_op jit(solution)/shard_map/ppermute | solution.py:29
  50.8 15.4 %collective-permute-start.6 = (bf16[2,2,1,1,2,24,896]{6,5,4,1,0,3,2:T(8,128)(2,1)S(1)}, bf16[2,2,1,1,2,24,896]{6,5,4,1,0,3,2:T(8,128)(2,1)S(1)}, u32[]{:S(2)}, u32[]{:S(2)}) collective-permute-start(bf16[2,2,1,1,2,24,896]{6,5,4,1,0,3,2:T(8,128)(2,1)S(1)} %broadcast_select_fusion.10), channel_id=1, source_target_pairs={{0,2},{1,3},{2,0},{3,1},{4,6},{5,7},{6,4},{7,5},{8,10},{9,11},{10,... | collective-permute-start | bytes 1032200 | tf_op jit(solution)/shard_map/ppermute | solution.py:29
  52.7 37.6 %collective-permute-start.9 = (bf16[2,2,2,1,2,24,768]{6,5,4,2,1,0,3:T(8,128)(2,1)S(1)}, bf16[2,2,2,1,2,24,768]{6,5,4,2,1,0,3:T(8,128)(2,1)S(1)}, u32[]{:S(2)}, u32[]{:S(2)}) collective-permute-start(bf16[2,2,2,1,2,24,768]{6,5,4,2,1,0,3:T(8,128)(2,1)S(1)} %broadcast_select_fusion.1), channel_id=1, source_target_pairs={{0,2},{1,3},{2,0},{3,1},{4,6},{5,7},{6,4},{7,5},{8,10},{9,11},{10,... | collective-permute-start | bytes 1769480 | tf_op jit(solution)/shard_map/ppermute | solution.py:29
  92.4 20.2 %collective-permute-start.10 = (bf16[768,768]{1,0:T(8,128)(2,1)S(1)}, bf16[768,768]{1,0:T(8,128)(2,1)}, u32[]{:S(2)}, u32[]{:S(2)}) collective-permute-start(bf16[768,768]{1,0:T(8,128)(2,1)S(1)} %bitcast_select_fusion.1), channel_id=1, source_target_pairs={{0,1},{1,0},{2,3},{3,2},{4,5},{5,4},{6,7},{7,6},{8,9},{9,8},{10,11... | collective-permute-start | bytes 3538952 | tf_op jit(solution)/shard_map/ppermute | solution.py:29
  92.5 17.9 %collective-permute-start.8 = (bf16[2,2,1,2,2,24,896]{6,5,4,3,1,0,2:T(8,128)(2,1)S(1)}, bf16[2,2,1,2,2,24,896]{6,5,4,3,1,0,2:T(8,128)(2,1)S(1)}, u32[]{:S(2)}, u32[]{:S(2)}) collective-permute-start(bf16[2,2,1,2,2,24,896]{6,5,4,3,1,0,2:T(8,128)(2,1)S(1)} %broadcast_select_fusion), channel_id=1, source_target_pairs={{0,4},{4,0},{8,12},{12,8},{16,20},{20,16},{24,28},{28,24},{1,5},{5... | collective-permute-start | bytes 2064392 | tf_op jit(solution)/shard_map/ppermute | solution.py:29
  112.6 13.5 %collective-permute-start.11 = (bf16[768,896]{1,0:T(8,128)(2,1)S(1)}, bf16[768,896]{1,0:T(8,128)(2,1)}, u32[]{:S(2)}, u32[]{:S(2)}) collective-permute-start(bf16[768,896]{1,0:T(8,128)(2,1)S(1)} %bitcast_select_fusion), channel_id=1, source_target_pairs={{0,1},{1,0},{2,3},{3,2},{4,5},{5,4},{6,7},{7,6},{8,9},{9,8},{10,11... | collective-permute-start | bytes 4128776 | tf_op jit(solution)/shard_map/ppermute | solution.py:29
  112.7 12.2 %collective-permute-start.1 = (bf16[128,768]{1,0:T(8,128)(2,1)}, bf16[128,768]{1,0:T(8,128)(2,1)S(1)}, u32[]{:S(2)}, u32[]{:S(2)}) collective-permute-start(bf16[128,768]{1,0:T(8,128)(2,1)} %get-tuple-element.151), channel_id=1, source_target_pairs={{0,2},{1,3},{2,0},{3,1},{4,6},{5,7},{6,4},{7,5},{8,10},{9,11},{10,... | collective-permute-start | bytes 589832 | tf_op jit(solution)/shard_map/ppermute | solution.py:29
  132.7 6.2 %collective-permute-start.12 = (bf16[256,1536]{1,0:T(8,128)(2,1)S(1)}, bf16[256,1536]{1,0:T(8,128)(2,1)}, u32[]{:S(2)}, u32[]{:S(2)}) collective-permute-start(bf16[256,1536]{1,0:T(8,128)(2,1)S(1)} %pad_maximum_fusion.11.key_own.value_own), channel_id=1, source_target_pairs={{0,1},{1,0},{2,3},{3,2},{4,5},{5,4},{6,7},{7,6},{8,9},{9,8},{10,11... | collective-permute-start | bytes 2359304 | tf_op jit(solution)/shard_map/ppermute | solution.py:29
  148.8 58.7 %copy-start.82 = (f32[256]{0:T(256)}, f32[256]{0:T(256)S(1)}, u32[]{:S(2)}) copy-start(f32[256]{0:T(256)S(1)} %broadcast_multiply_fusion.11) | copy-start | bytes 3076
  149.0 58.5 %copy-start.93 = (f32[256]{0:T(256)}, f32[256]{0:T(256)S(1)}, u32[]{:S(2)}) copy-start(f32[256]{0:T(256)S(1)} %add_rsqrt_fusion.3) | copy-start | bytes 3076
  149.2 55.4 %copy-start.13 = (bf16[256,768]{1,0:T(8,128)(2,1)}, bf16[256,768]{1,0:T(8,128)(2,1)S(1)}, u32[]{:S(2)}) copy-start(bf16[256,768]{1,0:T(8,128)(2,1)S(1)} %fusion.72) | copy-start | bytes 1179652
  209.0 17.2 %copy-start.80 = (f32[256]{0:T(256)}, f32[256]{0:T(256)S(1)}, u32[]{:S(2)}) copy-start(f32[256]{0:T(256)S(1)} %broadcast_multiply_fusion.10) | copy-start | bytes 3076
  209.3 17.0 %copy-start.84 = (f32[256]{0:T(256)}, f32[256]{0:T(256)S(1)}, u32[]{:S(2)}) copy-start(f32[256]{0:T(256)S(1)} %add_rsqrt_fusion.2) | copy-start | bytes 3076
  213.1 4.5 collective-permute-start.13
  213.4 26.3 %collective-permute-start.15 = (bf16[128,768]{1,0:T(8,128)(2,1)}, bf16[128,768]{1,0:T(8,128)(2,1)S(1)}, u32[]{:S(2)}, u32[]{:S(2)}) collective-permute-start(bf16[128,768]{1,0:T(8,128)(2,1)} %get-tuple-element.154), channel_id=1, source_target_pairs={{0,2},{1,3},{2,0},{3,1},{4,6},{5,7},{6,4},{7,5},{8,10},{9,11},{10,... | collective-permute-start | bytes 589832 | tf_op jit(solution)/shard_map/ppermute | solution.py:29
  291.4 9.0 %collective-permute-start.16 = (bf16[2,256,768]{2,1,0:T(8,128)(2,1)}, bf16[2,256,768]{2,1,0:T(8,128)(2,1)}, u32[]{:S(2)}, u32[]{:S(2)}) collective-permute-start(bf16[2,256,768]{2,1,0:T(8,128)(2,1)} %get-tuple-element.181), channel_id=1, source_target_pairs={{0,1},{1,0},{2,3},{3,2},{4,5},{5,4},{6,7},{7,6},{8,9},{9,8},{10,11... | collective-permute-start | bytes 2359304 | tf_op jit(solution)/shard_map/ppermute | solution.py:29
  292.2 7.4 %collective-permute-start.14 = (bf16[128,768]{1,0:T(8,128)(2,1)S(1)}, bf16[128,768]{1,0:T(8,128)(2,1)S(1)}, u32[]{:S(2)}, u32[]{:S(2)}) collective-permute-start(bf16[128,768]{1,0:T(8,128)(2,1)S(1)} %slice.594), channel_id=1, source_target_pairs={{0,2},{1,3},{2,0},{3,1},{4,6},{5,7},{6,4},{7,5},{8,10},{9,11},{10,... | collective-permute-start | bytes 589832 | tf_op jit(solution)/shard_map/ppermute | solution.py:29
  299.6 5.8 %collective-permute-start.17 = (bf16[768,768]{0,1:T(8,128)(2,1)S(1)}, bf16[768,768]{0,1:T(8,128)(2,1)}, u32[]{:S(2)}, u32[]{:S(2)}) collective-permute-start(bf16[768,768]{0,1:T(8,128)(2,1)S(1)} %pad_maximum_fusion.10), channel_id=1, source_target_pairs={{0,1},{1,0},{2,3},{3,2},{4,5},{5,4},{6,7},{7,6},{8,9},{9,8},{10,11... | collective-permute-start | bytes 3538952 | tf_op jit(solution)/shard_map/ppermute | solution.py:29
  305.3 11.9 %collective-permute-start.18 = (bf16[768,768]{1,0:T(8,128)(2,1)}, bf16[768,768]{1,0:T(8,128)(2,1)}, u32[]{:S(2)}, u32[]{:S(2)}) collective-permute-start(bf16[768,768]{1,0:T(8,128)(2,1)} %convolution_convert_fusion.6), channel_id=1, source_target_pairs={{0,1},{1,0},{2,3},{3,2},{4,5},{5,4},{6,7},{7,6},{8,9},{9,8},{10,11... | collective-permute-start | bytes 3538952 | tf_op jit(solution)/shard_map/ppermute | solution.py:29
  319.0 16.4 %collective-permute-start.19 = (bf16[1,2,2,1,2,48,768]{6,5,4,3,2,1,0:T(8,128)(2,1)S(1)}, bf16[1,2,2,1,2,48,768]{6,5,4,3,2,1,0:T(8,128)(2,1)S(1)}, u32[]{:S(2)}, u32[]{:S(2)}) collective-permute-start(bf16[1,2,2,1,2,48,768]{6,5,4,3,2,1,0:T(8,128)(2,1)S(1)} %get-tuple-element.192), channel_id=1, source_target_pairs={{0,4},{4,0},{8,12},{12,8},{16,20},{20,16},{24,28},{28,24},{1,5},{5... | collective-permute-start | bytes 1769480 | tf_op jit(solution)/shard_map/ppermute | solution.py:29
  320.5 15.8 %collective-permute-start.20 = (bf16[1,2,2,2,1,48,768]{6,5,4,3,2,1,0:T(8,128)(2,1)S(1)}, bf16[1,2,2,2,1,48,768]{6,5,4,3,2,1,0:T(8,128)(2,1)S(1)}, u32[]{:S(2)}, u32[]{:S(2)}) collective-permute-start(bf16[1,2,2,2,1,48,768]{6,5,4,3,2,1,0:T(8,128)(2,1)S(1)} %get-tuple-element.194), channel_id=1, source_target_pairs={{0,2},{1,3},{2,0},{3,1},{4,6},{5,7},{6,4},{7,5},{8,10},{9,11},{10,... | collective-permute-start | bytes 1769480 | tf_op jit(solution)/shard_map/ppermute | solution.py:29
  324.1 13.2 %collective-permute-start.21 = (bf16[3072,384]{1,0:T(8,128)(2,1)S(1)}, bf16[3072,384]{1,0:T(8,128)(2,1)S(1)}, u32[]{:S(2)}, u32[]{:S(2)}) collective-permute-start(bf16[3072,384]{1,0:T(8,128)(2,1)S(1)} %convolution_convert_fusion), channel_id=1, source_target_pairs={{0,1},{1,0},{2,3},{3,2},{4,5},{5,4},{6,7},{7,6},{8,9},{9,8},{10,11... | collective-permute-start | bytes 7077896 | tf_op jit(solution)/shard_map/ppermute | solution.py:29
  340.1 38.2 %collective-permute-start.22 = (bf16[768,1536]{1,0:T(8,128)(2,1)S(1)}, bf16[768,1536]{1,0:T(8,128)(2,1)S(1)}, u32[]{:S(2)}, u32[]{:S(2)}) collective-permute-start(bf16[768,1536]{1,0:T(8,128)(2,1)S(1)} %convolution_convert_fusion.2), channel_id=1, source_target_pairs={{0,1},{1,0},{2,3},{3,2},{4,5},{5,4},{6,7},{7,6},{8,9},{9,8},{10,11... | collective-permute-start | bytes 7077896 | tf_op jit(solution)/shard_map/ppermute | solution.py:29
  340.5 36.4 %collective-permute-start.28 = (bf16[4,2,2,1,2,48,384]{6,5,4,3,2,1,0:T(8,128)(2,1)S(1)}, bf16[4,2,2,1,2,48,384]{6,5,4,3,2,1,0:T(8,128)(2,1)S(1)}, u32[]{:S(2)}, u32[]{:S(2)}) collective-permute-start(bf16[4,2,2,1,2,48,384]{6,5,4,3,2,1,0:T(8,128)(2,1)S(1)} %get-tuple-element.232), channel_id=1, source_target_pairs={{0,4},{4,0},{8,12},{12,8},{16,20},{20,16},{24,28},{28,24},{1,5},{5... | collective-permute-start | bytes 3538952 | tf_op jit(solution)/shard_map/ppermute | solution.py:29
  390.9 10.6 %collective-permute-start.23 = (bf16[2,256,768]{2,1,0:T(8,128)(2,1)}, bf16[2,256,768]{2,1,0:T(8,128)(2,1)S(1)}, u32[]{:S(2)}, u32[]{:S(2)}) collective-permute-start(bf16[2,256,768]{2,1,0:T(8,128)(2,1)} %get-tuple-element.213), channel_id=1, source_target_pairs={{0,1},{1,0},{2,3},{3,2},{4,5},{5,4},{6,7},{7,6},{8,9},{9,8},{10,11... | collective-permute-start | bytes 2359304 | tf_op jit(solution)/shard_map/ppermute | solution.py:29
  390.9 19.0 %collective-permute-start.26 = (bf16[1,2,2,1,1,48,768]{6,5,4,3,2,1,0:T(8,128)(2,1)}, bf16[1,2,2,1,1,48,768]{6,5,4,3,2,1,0:T(8,128)(2,1)}, u32[]{:S(2)}, u32[]{:S(2)}) collective-permute-start(bf16[1,2,2,1,1,48,768]{6,5,4,3,2,1,0:T(8,128)(2,1)} %get-tuple-element.227), channel_id=1, source_target_pairs={{0,2},{1,3},{2,0},{3,1},{4,6},{5,7},{6,4},{7,5},{8,10},{9,11},{10,... | collective-permute-start | bytes 884744 | tf_op jit(solution)/shard_map/ppermute | solution.py:29
  392.5 19.4 %collective-permute-start.27 = (bf16[1,2,2,1,1,48,768]{6,5,4,3,2,1,0:T(8,128)(2,1)}, bf16[1,2,2,1,1,48,768]{6,5,4,3,2,1,0:T(8,128)(2,1)}, u32[]{:S(2)}, u32[]{:S(2)}) collective-permute-start(bf16[1,2,2,1,1,48,768]{6,5,4,3,2,1,0:T(8,128)(2,1)} %get-tuple-element.230), channel_id=1, source_target_pairs={{0,4},{4,0},{8,12},{12,8},{16,20},{20,16},{24,28},{28,24},{1,5},{5... | collective-permute-start | bytes 884744 | tf_op jit(solution)/shard_map/ppermute | solution.py:29
  393.1 37.6 %collective-permute-start.29 = (bf16[1,2,2,2,1,48,1536]{6,5,4,3,2,1,0:T(8,128)(2,1)}, bf16[1,2,2,2,1,48,1536]{6,5,4,3,2,1,0:T(8,128)(2,1)}, u32[]{:S(2)}, u32[]{:S(2)}) collective-permute-start(bf16[1,2,2,2,1,48,1536]{6,5,4,3,2,1,0:T(8,128)(2,1)} %get-tuple-element.233), channel_id=1, source_target_pairs={{0,2},{1,3},{2,0},{3,1},{4,6},{5,7},{6,4},{7,5},{8,10},{9,11},{10,... | collective-permute-start | bytes 3538952 | tf_op jit(solution)/shard_map/ppermute | solution.py:29
  406.5 3.2 collective-permute-start.24
  409.7 29.2 %collective-permute-start.25 = (bf16[768,768]{1,0:T(8,128)(2,1)}, bf16[768,768]{1,0:T(8,128)(2,1)}, u32[]{:S(2)}, u32[]{:S(2)}) collective-permute-start(bf16[768,768]{1,0:T(8,128)(2,1)} %convolution_convert_fusion.4), channel_id=1, source_target_pairs={{0,1},{1,0},{2,3},{3,2},{4,5},{5,4},{6,7},{7,6},{8,9},{9,8},{10,11... | collective-permute-start | bytes 3538952 | tf_op jit(solution)/shard_map/ppermute | solution.py:29
  416.7 14.0 %copy-start.10 = (bf16[1,2,2,2,1,48,1536]{6,5,4,3,2,1,0:T(8,128)(2,1)S(1)}, bf16[1,2,2,2,1,48,1536]{6,5,4,3,2,1,0:T(8,128)(2,1)}, u32[]{:S(2)}) copy-start(bf16[1,2,2,2,1,48,1536]{6,5,4,3,2,1,0:T(8,128)(2,1)} %get-tuple-element.323) | copy-start | bytes 3538948
  441.6 16.4 %collective-permute-start.36 = (bf16[1,2,2,1,1,48,1536]{6,5,4,3,2,1,0:T(8,128)(2,1)}, bf16[1,2,2,1,1,48,1536]{6,5,4,3,2,1,0:T(8,128)(2,1)}, u32[]{:S(2)}, u32[]{:S(2)}) collective-permute-start(bf16[1,2,2,1,1,48,1536]{6,5,4,3,2,1,0:T(8,128)(2,1)} %get-tuple-element.236), channel_id=1, source_target_pairs={{0,4},{4,0},{8,12},{12,8},{16,20},{20,16},{24,28},{28,24},{1,5},{5... | collective-permute-start | bytes 1769480 | tf_op jit(solution)/shard_map/ppermute | solution.py:29
  442.2 19.1 %collective-permute-start.35 = (bf16[4,2,2,1,1,48,384]{6,5,4,3,2,1,0:T(8,128)(2,1)}, bf16[4,2,2,1,1,48,384]{6,5,4,3,2,1,0:T(8,128)(2,1)}, u32[]{:S(2)}, u32[]{:S(2)}) collective-permute-start(bf16[4,2,2,1,1,48,384]{6,5,4,3,2,1,0:T(8,128)(2,1)} %get-tuple-element.237), channel_id=1, source_target_pairs={{0,2},{1,3},{2,0},{3,1},{4,6},{5,7},{6,4},{7,5},{8,10},{9,11},{10,... | collective-permute-start | bytes 1769480 | tf_op jit(solution)/shard_map/ppermute | solution.py:29
  444.8 8.1 %collective-permute-start.33 = (bf16[1,2,1,1,1,48,768]{6,5,4,3,2,1,0:T(8,128)(2,1)S(1)}, bf16[1,2,1,1,1,48,768]{6,5,4,3,2,1,0:T(8,128)(2,1)S(1)}, u32[]{:S(2)}, u32[]{:S(2)}) collective-permute-start(bf16[1,2,1,1,1,48,768]{6,5,4,3,2,1,0:T(8,128)(2,1)S(1)} %copy-done.77), channel_id=1, source_target_pairs={{0,8},{4,12},{8,0},{12,4},{16,24},{20,28},{24,16},{28,20},{1,9},{5... | collective-permute-start | bytes 442376 | tf_op jit(solution)/shard_map/ppermute | solution.py:29
  444.8 7.4 %collective-permute-start.32 = (bf16[1,2,1,1,1,48,768]{6,5,4,3,2,1,0:T(8,128)(2,1)S(1)}, bf16[1,2,1,1,1,48,768]{6,5,4,3,2,1,0:T(8,128)(2,1)S(1)}, u32[]{:S(2)}, u32[]{:S(2)}) collective-permute-start(bf16[1,2,1,1,1,48,768]{6,5,4,3,2,1,0:T(8,128)(2,1)S(1)} %copy-done.76), channel_id=1, source_target_pairs={{0,8},{4,12},{8,0},{12,4},{16,24},{20,28},{24,16},{28,20},{1,9},{5... | collective-permute-start | bytes 442376 | tf_op jit(solution)/shard_map/ppermute | solution.py:29
  446.9 11.1 %copy-start.23 = (bf16[1,2,2,1,1,48,1536]{6,5,4,3,2,1,0:T(8,128)(2,1)S(1)}, bf16[1,2,2,1,1,48,1536]{6,5,4,3,2,1,0:T(8,128)(2,1)}, u32[]{:S(2)}) copy-start(bf16[1,2,2,1,1,48,1536]{6,5,4,3,2,1,0:T(8,128)(2,1)} %get-tuple-element.335) | copy-start | bytes 1769476
  448.2 11.1 %copy-start.29 = (bf16[256,768]{1,0:T(8,128)(2,1)S(1)}, bf16[256,768]{1,0:T(8,128)(2,1)}, u32[]{:S(2)}) copy-start(bf16[256,768]{1,0:T(8,128)(2,1)} %fusion.1) | copy-start | bytes 1179652
  448.2 13.2 %copy-start.21 = (bf16[4,2,2,1,1,48,384]{6,5,4,3,2,1,0:T(8,128)(2,1)S(1)}, bf16[4,2,2,1,1,48,384]{6,5,4,3,2,1,0:T(8,128)(2,1)}, u32[]{:S(2)}) copy-start(bf16[4,2,2,1,1,48,384]{6,5,4,3,2,1,0:T(8,128)(2,1)} %get-tuple-element.337) | copy-start | bytes 1769476
  453.6 20.4 %collective-permute-start.31 = (bf16[1,2,2,2,1,48,896]{6,5,4,3,2,1,0:T(8,128)(2,1)}, bf16[1,2,2,2,1,48,896]{6,5,4,3,2,1,0:T(8,128)(2,1)S(1)}, u32[]{:S(2)}, u32[]{:S(2)}) collective-permute-start(bf16[1,2,2,2,1,48,896]{6,5,4,3,2,1,0:T(8,128)(2,1)} %get-tuple-element.242), channel_id=1, source_target_pairs={{0,2},{1,3},{2,0},{3,1},{4,6},{5,7},{6,4},{7,5},{8,10},{9,11},{10,... | collective-permute-start | bytes 2064392 | tf_op jit(solution)/shard_map/ppermute | solution.py:29
  454.1 14.8 %collective-permute-start.37 = (bf16[1,2,2,1,2,48,768]{6,5,4,3,2,1,0:T(8,128)(2,1)}, bf16[1,2,2,1,2,48,768]{6,5,4,3,2,1,0:T(8,128)(2,1)S(1)}, u32[]{:S(2)}, u32[]{:S(2)}) collective-permute-start(bf16[1,2,2,1,2,48,768]{6,5,4,3,2,1,0:T(8,128)(2,1)} %get-tuple-element.252), channel_id=1, source_target_pairs={{0,4},{4,0},{8,12},{12,8},{16,20},{20,16},{24,28},{28,24},{1,5},{5... | collective-permute-start | bytes 1769480 | tf_op jit(solution)/shard_map/ppermute | solution.py:29
  459.3 7.3 %collective-permute-start.46 = (bf16[1,1,1,1,1,48,768]{6,5,4,3,2,1,0:T(8,128)(2,1)S(1)}, bf16[1,1,1,1,1,48,768]{6,5,4,3,2,1,0:T(8,128)(2,1)S(1)}, u32[]{:S(2)}, u32[]{:S(2)}) collective-permute-start(bf16[1,1,1,1,1,48,768]{6,5,4,3,2,1,0:T(8,128)(2,1)S(1)} %add_convert_fusion.55), channel_id=1, source_target_pairs={{0,16},{4,20},{8,24},{12,28},{16,0},{20,4},{24,8},{28,12},{1,17},{... | collective-permute-start | bytes 221192 | tf_op jit(solution)/shard_map/ppermute | solution.py:29
  461.3 12.7 %copy-start.16 = (bf16[1,2,2,2,1,48,896]{6,5,4,3,2,1,0:T(8,128)(2,1)S(1)}, bf16[1,2,2,2,1,48,896]{6,5,4,3,2,1,0:T(8,128)(2,1)}, u32[]{:S(2)}) copy-start(bf16[1,2,2,2,1,48,896]{6,5,4,3,2,1,0:T(8,128)(2,1)} %get-tuple-element.327) | copy-start | bytes 2064388
  462.6 13.6 %collective-permute-start.30 = (bf16[128,768]{1,0:T(8,128)(2,1)S(1)}, bf16[128,768]{1,0:T(8,128)(2,1)S(1)}, u32[]{:S(2)}, u32[]{:S(2)}) collective-permute-start(bf16[128,768]{1,0:T(8,128)(2,1)S(1)} %slice.640), channel_id=1, source_target_pairs={{0,2},{1,3},{2,0},{3,1},{4,6},{5,7},{6,4},{7,5},{8,10},{9,11},{10,... | collective-permute-start | bytes 589832 | tf_op jit(solution)/shard_map/ppermute | solution.py:29
  463.5 10.7 %collective-permute-start.47 = (bf16[1,1,1,1,1,48,768]{6,5,4,3,2,1,0:T(8,128)(2,1)S(1)}, bf16[1,1,1,1,1,48,768]{6,5,4,3,2,1,0:T(8,128)(2,1)S(1)}, u32[]{:S(2)}, u32[]{:S(2)}) collective-permute-start(bf16[1,1,1,1,1,48,768]{6,5,4,3,2,1,0:T(8,128)(2,1)S(1)} %add_convert_fusion.56), channel_id=1, source_target_pairs={{0,16},{4,20},{8,24},{12,28},{16,0},{20,4},{24,8},{28,12},{1,17},{... | collective-permute-start | bytes 221192 | tf_op jit(solution)/shard_map/ppermute | solution.py:29
  474.2 11.2 %collective-permute-start.40 = (bf16[1,2,1,1,1,48,1536]{6,5,4,3,2,1,0:T(8,128)(2,1)S(1)}, bf16[1,2,1,1,1,48,1536]{6,5,4,3,2,1,0:T(8,128)(2,1)S(1)}, u32[]{:S(2)}, u32[]{:S(2)}) collective-permute-start(bf16[1,2,1,1,1,48,1536]{6,5,4,3,2,1,0:T(8,128)(2,1)S(1)} %get-tuple-element.255), channel_id=1, source_target_pairs={{0,8},{4,12},{8,0},{12,4},{16,24},{20,28},{24,16},{28,20},{1,9},{5... | collective-permute-start | bytes 884744 | tf_op jit(solution)/shard_map/ppermute | solution.py:29
  474.3 11.1 %collective-permute-start.34 = (bf16[1,2,2,1,1,48,896]{6,5,4,3,2,1,0:T(8,128)(2,1)S(1)}, bf16[1,2,2,1,1,48,896]{6,5,4,3,2,1,0:T(8,128)(2,1)S(1)}, u32[]{:S(2)}, u32[]{:S(2)}) collective-permute-start(bf16[1,2,2,1,1,48,896]{6,5,4,3,2,1,0:T(8,128)(2,1)S(1)} %get-tuple-element.248), channel_id=1, source_target_pairs={{0,4},{4,0},{8,12},{12,8},{16,20},{20,16},{24,28},{28,24},{1,5},{5... | collective-permute-start | bytes 1032200 | tf_op jit(solution)/shard_map/ppermute | solution.py:29
  476.2 12.7 %collective-permute-start.42 = (bf16[1,2,2,1,1,48,768]{6,5,4,3,2,1,0:T(8,128)(2,1)S(1)}, bf16[1,2,2,1,1,48,768]{6,5,4,3,2,1,0:T(8,128)(2,1)S(1)}, u32[]{:S(2)}, u32[]{:S(2)}) collective-permute-start(bf16[1,2,2,1,1,48,768]{6,5,4,3,2,1,0:T(8,128)(2,1)S(1)} %get-tuple-element.254), channel_id=1, source_target_pairs={{0,2},{1,3},{2,0},{3,1},{4,6},{5,7},{6,4},{7,5},{8,10},{9,11},{10,... | collective-permute-start | bytes 884744 | tf_op jit(solution)/shard_map/ppermute | solution.py:29
  478.0 10.8 %collective-permute-start.39 = (bf16[4,2,1,1,1,48,384]{6,5,4,3,2,1,0:T(8,128)(2,1)S(1)}, bf16[4,2,1,1,1,48,384]{6,5,4,3,2,1,0:T(8,128)(2,1)S(1)}, u32[]{:S(2)}, u32[]{:S(2)}) collective-permute-start(bf16[4,2,1,1,1,48,384]{6,5,4,3,2,1,0:T(8,128)(2,1)S(1)} %get-tuple-element.256), channel_id=1, source_target_pairs={{0,8},{4,12},{8,0},{12,4},{16,24},{20,28},{24,16},{28,20},{1,9},{5... | collective-permute-start | bytes 884744 | tf_op jit(solution)/shard_map/ppermute | solution.py:29
  485.5 11.4 %collective-permute-start.43 = (bf16[1,1,1,1,1,48,1536]{6,5,4,3,2,1,0:T(8,128)(2,1)S(1)}, bf16[1,1,1,1,1,48,1536]{6,5,4,3,2,1,0:T(8,128)(2,1)S(1)}, u32[]{:S(2)}, u32[]{:S(2)}) collective-permute-start(bf16[1,1,1,1,1,48,1536]{6,5,4,3,2,1,0:T(8,128)(2,1)S(1)} %add_convert_fusion.39), channel_id=1, source_target_pairs={{0,16},{4,20},{8,24},{12,28},{16,0},{20,4},{24,8},{28,12},{1,17},{... | collective-permute-start | bytes 442376 | tf_op jit(solution)/shard_map/ppermute | solution.py:29
  489.0 8.0 %collective-permute-start.38 = (bf16[1,2,1,1,1,48,896]{6,5,4,3,2,1,0:T(8,128)(2,1)S(1)}, bf16[1,2,1,1,1,48,896]{6,5,4,3,2,1,0:T(8,128)(2,1)S(1)}, u32[]{:S(2)}, u32[]{:S(2)}) collective-permute-start(bf16[1,2,1,1,1,48,896]{6,5,4,3,2,1,0:T(8,128)(2,1)S(1)} %get-tuple-element.257), channel_id=1, source_target_pairs={{0,8},{4,12},{8,0},{12,4},{16,24},{20,28},{24,16},{28,20},{1,9},{5... | collective-permute-start | bytes 516104 | tf_op jit(solution)/shard_map/ppermute | solution.py:29
  489.1 13.2 %collective-permute-start.49 = (bf16[4,1,1,1,1,48,384]{6,5,4,3,2,1,0:T(8,128)(2,1)S(1)}, bf16[4,1,1,1,1,48,384]{6,5,4,3,2,1,0:T(8,128)(2,1)S(1)}, u32[]{:S(2)}, u32[]{:S(2)}) collective-permute-start(bf16[4,1,1,1,1,48,384]{6,5,4,3,2,1,0:T(8,128)(2,1)S(1)} %add_convert_fusion.40), channel_id=1, source_target_pairs={{0,16},{4,20},{8,24},{12,28},{16,0},{20,4},{24,8},{28,12},{1,17},{... | collective-permute-start | bytes 442376 | tf_op jit(solution)/shard_map/ppermute | solution.py:29
  497.0 6.3 %collective-permute-start.41 = (bf16[1,1,1,1,1,48,896]{6,5,4,3,2,1,0:T(8,128)(2,1)S(1)}, bf16[1,1,1,1,1,48,896]{6,5,4,3,2,1,0:T(8,128)(2,1)S(1)}, u32[]{:S(2)}, u32[]{:S(2)}) collective-permute-start(bf16[1,1,1,1,1,48,896]{6,5,4,3,2,1,0:T(8,128)(2,1)S(1)} %add_convert_fusion.46), channel_id=1, source_target_pairs={{0,16},{4,20},{8,24},{12,28},{16,0},{20,4},{24,8},{28,12},{1,17},{... | collective-permute-start | bytes 258056 | tf_op jit(solution)/shard_map/ppermute | solution.py:29
  502.4 6.0 %collective-permute-start.44 = (bf16[1,2,1,1,1,48,768]{6,5,4,3,2,1,0:T(8,128)(2,1)S(1)}, bf16[1,2,1,1,1,48,768]{6,5,4,3,2,1,0:T(8,128)(2,1)S(1)}, u32[]{:S(2)}, u32[]{:S(2)}) collective-permute-start(bf16[1,2,1,1,1,48,768]{6,5,4,3,2,1,0:T(8,128)(2,1)S(1)} %get-tuple-element.265), channel_id=1, source_target_pairs={{0,8},{4,12},{8,0},{12,4},{16,24},{20,28},{24,16},{28,20},{1,9},{5... | collective-permute-start | bytes 442376 | tf_op jit(solution)/shard_map/ppermute | solution.py:29
  508.4 5.5 %collective-permute-start.45 = (bf16[1,1,1,1,1,48,768]{6,5,4,3,2,1,0:T(8,128)(2,1)S(1)}, bf16[1,1,1,1,1,48,768]{6,5,4,3,2,1,0:T(8,128)(2,1)S(1)}, u32[]{:S(2)}, u32[]{:S(2)}) collective-permute-start(bf16[1,1,1,1,1,48,768]{6,5,4,3,2,1,0:T(8,128)(2,1)S(1)} %add_convert_fusion.53), channel_id=1, source_target_pairs={{0,16},{4,20},{8,24},{12,28},{16,0},{20,4},{24,8},{28,12},{1,17},{... | collective-permute-start | bytes 221192 | tf_op jit(solution)/shard_map/ppermute | solution.py:29
  514.9 2.1 collective-permute-start.48
  515.5 1.4 collective-permute-start.50
  (110 other events, 386.3 us)
Sparse Core Ops, SparseCore 0:
  11.9 177.7 all-gather.1
  295.1 147.1 reduce-scatter.1
